TPU v7x, 32 devices: a whole 2x2x4 slice. The times are simulated.
32 devices in a mesh: groups: 2 (over y), pipe: 16 (over z, x, core).
Axes of the slice: x: 2, y: 2, z: 4, core: 2. Of those that a mesh axis runs over, the one named last changes fastest.
Arguments:
- hidden: bfloat16 [256, 18432], P(('groups', 'pipe')), parts along dimension 0, may hold values from -128 to 128
- head_rows: bfloat16 [4096, 18432], P(('groups', 'pipe')), parts along dimension 0, may hold values from -1 to 1
- teacher: bfloat16 [256, 2048], P('groups', 'pipe'), parts along dimension 0, may hold values from -240 to 240
- targets: int32 [256], P('groups'), parts along dimension 0, may hold values from 0 to 2047
- token_weight: float32 [256], P('groups'), parts along dimension 0, may hold values from 0.5 to 2
Outputs:
- loss: float32 [256], P(('groups', 'pipe')), parts along dimension 0
- grad_hidden: bfloat16 [256, 18432], P(('groups', 'pipe')), parts along dimension 0
- grad_head: bfloat16 [4096, 18432], P(('groups', 'pipe')), parts along dimension 0
There are 2 independent parts, one for each index of `groups`. A program takes and returns all parts, laid end to end along the dimension named above; each array names one. Nothing has to cross between parts.
All inputs are finite; a program needn't handle non-finite values.
Results may differ from a plain program's by a relative error of at most 0.0051.
Values may be sent and summed in bfloat16 or wider, within the bound.
No kernel may reach another device: no remote copies, remote signals or barrier semaphores. Data moves between devices by JAX's collectives and lax.ppermute only.
A program may use at most 128 MiB of HBM per device.

v0:
```python
import jax
import jax.numpy as jnp
from jax import lax
from jax.sharding import PartitionSpec as P


def per_device(hidden, head_rows, teacher, targets, token_weight):
    local_tokens = hidden.shape[0]
    local_ids = head_rows.shape[0]
    whole = lax.all_gather(hidden, "pipe", axis=0, tiled=True)
    student = 3.0 * lax.dot_general(
        whole, head_rows, (((1,), (1,)), ((), ())), preferred_element_type=jnp.float32
    )
    teach = teacher.astype(jnp.float32)
    columns = lax.axis_index("pipe") * local_ids + jnp.arange(local_ids, dtype=jnp.int32)
    onehot = (targets[:, None] == columns[None, :]).astype(jnp.float32)
    picked_part = jnp.sum(onehot * student, axis=1)
    smax, tmax = lax.pmax((jnp.max(student, axis=1), jnp.max(teach, axis=1)), "pipe")
    sexp = jnp.exp(student - smax[:, None])
    texp = jnp.exp(teach - tmax[:, None])
    szero, tzero, cross, picked = lax.psum(
        (
            jnp.sum(sexp, axis=1),
            jnp.sum(texp, axis=1),
            jnp.sum(texp * (teach - student), axis=1),
            picked_part,
        ),
        "pipe",
    )
    slog = smax + jnp.log(szero)
    tlog = tmax + jnp.log(tzero)
    loss_rows = cross / tzero - tlog + 2.0 * slog - picked
    loss = lax.dynamic_slice_in_dim(
        loss_rows, lax.axis_index("pipe") * local_tokens, local_tokens, 0
    )
    dlogit = (
        3.0 * token_weight[:, None] * (2.0 * sexp / szero[:, None] - texp / tzero[:, None] - onehot)
    ).astype(jnp.bfloat16)
    grad_head = lax.dot_general(
        dlogit, whole, (((0,), (0,)), ((), ())), preferred_element_type=jnp.float32
    ).astype(jnp.bfloat16)
    term = jnp.dot(dlogit, head_rows, preferred_element_type=jnp.float32)
    summed = lax.psum_scatter(term, "pipe", scatter_dimension=0, tiled=True)
    return (loss, summed.astype(jnp.bfloat16), grad_head)


def solution(mesh):
    placed = (
        P(("groups", "pipe"), None),
        P(("groups", "pipe"), None),
        P("groups", "pipe"),
        P("groups"),
        P("groups"),
    )
    return jax.shard_map(
        per_device,
        mesh=mesh,
        in_specs=placed,
        out_specs=(P(("groups", "pipe")), P(("groups", "pipe"), None), P(("groups", "pipe"), None)),
        check_vma=False,
    )
```

profile of v0, /device:TPU:0, one launch (start us, length us, event | category | flops | bytes accessed | tf_op | source)
XLA Modules:
  0.0 257.6 jit_solution(995512277455195946)
XLA Ops:
  7.2 0.0 all-gather.2.cloned.1.call-start
  7.2 0.7 all-gather.2.cloned.1.call-update
  7.9 0.0 reduce-scatter.2.cloned.1.call-start
  7.9 0.9 copy.8
  8.8 0.9 reduce_max.23
  9.7 0.7 broadcast_multiply_fusion
  10.4 0.0 copy-start
  10.4 55.9 %all-gather.2.cloned.1.call-done = bf16[128,18432]{1,0:T(8,128)(2,1)} async-done(((bf16[8,18432]{1,0:T(8,128)(2,1)}), bf16[128,18432]{1,0:T(8,128)(2,1)}) %all-gather.2.cloned.1.call-update) | async-done | bytes 4718608 | tf_op jit(solution)/shard_map/all_gather | solution.py:10
  66.2 5.2 %fusion.14 = (f32[128]{0:T(128)S(1)}, f32[128,128]{0,1:T(8,128)S(1)}) fusion(bf16[128,18432]{1,0:T(8,128)(2,1)} %all-gather.2.cloned.1.call-done, bf16[128,18432]{1,0:T(8,128)(2,1)} %param.6), kind=kOutput, calls=%fused_computation.22 | convolution fusion | flops 604012416 | bytes 9503232 | tf_op jit(solution)/shard_map/dot_general | solution.py:11
  71.4 31.7 %all-reduce.1 = (f32[128]{0:T(128)S(1)}, f32[128]{0:T(128)S(1)}) all-reduce(bf16[128]{0:T(256)(128)(2,1)S(1)} %reduce_max.23, f32[128]{0:T(128)S(1)} %get-tuple-element.13), channel_id=1, replica_groups=mesh['groups'=2,'pipe'=16] {'pipe'}, use_global_device_ids=true, to_apply=%region_1.0 | all-reduce | flops 256 | bytes 1792 | tf_op jit(solution)/shard_map/pmax | solution.py:18
  103.1 0.0 copy-done
  103.1 0.1 fusion.4
  103.2 29.5 %all-reduce = (f32[128]{0:T(128)S(1)}, f32[128]{0:T(128)S(1)}, f32[128]{0:T(128)S(1)}, f32[128]{0:T(128)S(1)}) all-reduce(f32[128]{0:T(128)S(1)} %get-tuple-element.4, f32[128]{0:T(128)S(1)} %get-tuple-element.5, f32[128]{0:T(128)S(1)} %get-tuple-element.6, f32[128]{0:T(128)S(1)} %get-tuple-element.3), channel_id=1, replica_groups=mesh['groups'=2,'pipe'=16] {'pipe'}, use_global_device_ids=true, to_apply=%region_11.0 | all-reduce | flops 512 | bytes 4096 | tf_op jit(solution)/shard_map/psum | solution.py:21
  132.7 7.5 %fusion.12 = f32[128,18432]{1,0:T(8,128)} fusion(bf16[128,18432]{1,0:T(8,128)(2,1)} %param.6, bf16[128,128]{0,1:T(8,128)(2,1)S(1)} %copy.8, f32[128,128]{0,1:T(8,128)S(1)} %get-tuple-element.14, f32[128]{0:T(128)S(1)} %get-tuple-element.9, f32[128]{0:T(128)S(1)} %get-tuple-element.8, f32[128]{0:T(128)S(1)} %broadcast_multiply_fusion, s32[128]{0:T(128)S(1)} %copy-done, ...), kind=kOutput, calls=%fused_computation.21 | convolution fusion | flops 604176384 | bytes 14257664 | tf_op jit(solution)/shard_map/dot_general | solution.py:42
  140.2 0.0 reduce-scatter.2.cloned.1.call-update
  140.2 0.6 dynamic_slice.3
  140.8 6.2 %convolution_convert_fusion = bf16[128,18432]{1,0:T(8,128)(2,1)} fusion(bf16[128,18432]{1,0:T(8,128)(2,1)} %all-gather.2.cloned.1.call-done, bf16[128,128]{0,1:T(8,128)(2,1)S(1)} %copy.8, f32[128,128]{0,1:T(8,128)S(1)} %get-tuple-element.14, f32[128]{0:T(128)S(1)} %get-tuple-element.9, f32[128]{0:T(128)S(1)} %get-tuple-element.8, ...), kind=kOutput, calls=%fused_computation | convolution fusion | flops 606535680 | bytes 9539072 | tf_op jit(solution)/shard_map/dot_general | solution.py:39
  147.0 102.0 %reduce-scatter.2.cloned.1.call-done = f32[8,18432]{1,0:T(8,128)} async-done(((f32[128,18432]{1,0:T(8,128)}), f32[8,18432]{1,0:T(8,128)}) %reduce-scatter.2.cloned.1.call-update) | async-done | bytes 589840 | tf_op jit(solution)/shard_map/reduce_scatter | solution.py:43
  249.0 1.8 convert_element_type.18
  (2 shorter events, 0.0 us)
Async XLA Ops:
  7.2 59.1 %all-gather.2.cloned.1.call-start = ((), (), s32[]{:S(2)}) async-start(), calls=%async_computation.1 | async-start | bytes 5013504 | tf_op jit(solution)/shard_map/all_gather | solution.py:10
  7.9 241.1 %reduce-scatter.2.cloned.1.call-start = ((), (), s32[]{:S(2)}) async-start(), calls=%async_computation.2 | async-start | bytes 10027008 | tf_op jit(solution)/shard_map/reduce_scatter | solution.py:43
  10.4 92.8 %copy-start = (s32[128]{0:T(128)S(1)}, s32[128]{0:T(128)}, u32[]{:S(2)}) copy-start(s32[128]{0:T(128)} %param.8) | copy-start | bytes 1540
Sparse Core Ops, SparseCore 0:
  10.3 55.9 all-gather.1
  140.3 108.5 reduce-scatter.1
where the time goes:
time: 258 us
  waiting for transfers between devices  159 us (62%)
  blocking collectives  61.2 us (24%)
  matrix products  18.8 us (7%)
  between operations  14.1 us (5%)
  other arithmetic  3.46 us (1%)
    reduce_scatter x1, waiting for transfers between devices, per_device(): summed = lax.psum_scatter(term, 'pipe', scatter_dimension=0, tiled=True)  102 us
    all_gather x1, waiting for transfers between devices, per_device(): whole = lax.all_gather(hidden, 'pipe', axis=0, tiled=True)  55.9 us
    pmax x1, blocking collectives, per_device(): lax.pmax((jnp.max(student, axis=1), jnp.max(teach, axis=1)), 'pipe')  31.7 us
    psum x1, blocking collectives, per_device(): lax.psum((jnp.sum(sexp, axis=1), jnp.sum(texp, axis=1), jnp.sum(texp * (t...  29.5 us
    dot_general x1, matrix products, per_device(): term = jnp.dot(dlogit, head_rows, preferred_element_type=jnp.float32)  7.45 us
    dot_general x1, matrix products, per_device(): lax.dot_general(dlogit, whole, (((0,), (0,)), ((), ())), preferred_elemen...  6.18 us
    dot_general x1, matrix products, per_device(): lax.dot_general(whole, head_rows, (((1,), (1,)), ((), ())), preferred_ele...  5.17 us
  transfers between devices with their start and end apart: 2, of which 2 were waited for; matrix products, arithmetic and copies ran while one was open for 4% of the time, Pallas kernels for 0%

commit v1 on v0

v1 whole, which is shorter than its diff:
```python
import jax
import jax.numpy as jnp
from jax import lax
from jax.sharding import PartitionSpec as P

F32 = jnp.float32
BF16 = jnp.bfloat16


def chip_ring(chips):
    return list(range(0, chips, 2)) + list(reversed(range(1, chips, 2)))


def ring_shift(ring, by):
    n = len(ring)
    return [(2 * ring[i] + c, 2 * ring[(i + by) % n] + c) for i in range(n) for c in (0, 1)]


def swap_pairs(devices, mask):
    return [(i, i ^ mask) for i in range(devices)]


def merge(a, b):
    sm = jnp.maximum(a[0], b[0])
    tm = jnp.maximum(a[1], b[1])
    sa, sb = jnp.exp(a[0] - sm), jnp.exp(b[0] - sm)
    ta, tb = jnp.exp(a[1] - tm), jnp.exp(b[1] - tm)
    return jnp.stack(
        [sm, tm, a[2] * sa + b[2] * sb, a[3] * ta + b[3] * tb, a[4] * ta + b[4] * tb, a[5] + b[5]]
    )


def local_stats(student, teach, onehot):
    sm = jnp.max(student, axis=1)
    tm = jnp.max(teach, axis=1)
    sexp = jnp.exp(student - sm[:, None])
    texp = jnp.exp(teach - tm[:, None])
    return jnp.stack(
        [
            sm,
            tm,
            jnp.sum(sexp, axis=1),
            jnp.sum(texp, axis=1),
            jnp.sum(texp * (teach - student), axis=1),
            jnp.sum(onehot * student, axis=1),
        ]
    )


def roll_to(x, shift, axis):
    size = x.shape[axis]
    return lax.dynamic_slice_in_dim(jnp.concatenate([x, x], axis), shift, size, axis)


def program(devices, hidden, head_rows, teacher, targets, token_weight):
    chips = devices // 2
    ring = chip_ring(chips)
    far = chips // 2
    tokens, width = hidden.shape
    ids = head_rows.shape[0]
    half = width // 2
    block = 2 * tokens
    total = chips * block

    me = lax.axis_index("pipe")
    core = me % 2
    chip = me // 2
    place = jnp.where(chip % 2 == 0, chip // 2, chips - 1 - chip // 2)
    to_core = swap_pairs(devices, 1)
    right, left = ring_shift(ring, 1), ring_shift(ring, -1)

    def send(x, perm):
        return lax.ppermute(x, "pipe", perm)

    def my_half(x):
        return lax.dynamic_slice_in_dim(x, core * half, half, 1)

    def other_half(x):
        return lax.dynamic_slice_in_dim(x, (1 - core) * half, half, 1)

    mine = my_half(hidden)
    theirs = send(other_half(hidden), to_core)
    block0 = jnp.where(
        core == 0, jnp.concatenate([mine, theirs]), jnp.concatenate([theirs, mine])
    )
    own_head = my_half(head_rows)
    sib_head = send(other_half(head_rows), to_core)

    blocks = {0: block0}
    from_left = from_right = block0
    for step in range(1, far):
        from_left = send(from_left, right)
        from_right = send(from_right, left)
        blocks[-step] = from_left
        blocks[step] = from_right
    quarter = half // 2
    blocks[far] = jnp.concatenate(
        [send(from_left[:, :quarter], right), send(from_right[:, quarter:], left)], axis=1
    )
    order = list(range(0, far + 1)) + list(range(1 - far, 0))
    whole = jnp.concatenate([blocks[k] for k in order])

    def by_distance(x):
        parts = [x[block * c : block * (c + 1)] for c in ring]
        return roll_to(jnp.concatenate(parts), place * block, 0)

    sib_teacher = send(teacher, to_core)
    teach = by_distance(jnp.concatenate([teacher, sib_teacher], axis=1)).astype(F32)
    target = by_distance(targets)
    weight = by_distance(token_weight)
    lanes = jnp.arange(ids, dtype=jnp.int32)
    columns = jnp.concatenate([me * ids + lanes, (me ^ 1) * ids + lanes])
    onehot = (target[:, None] == columns[None, :]).astype(F32)

    def logits(x, w):
        return lax.dot_general(x, w, (((1,), (1,)), ((), ())), preferred_element_type=F32)

    own_part, sib_part = logits(whole, own_head), logits(whole, sib_head)
    swapped = send(jnp.concatenate([sib_part, own_part], axis=1), to_core)
    student = 3.0 * (jnp.concatenate([own_part, sib_part], axis=1) + swapped)

    stats = local_stats(student, teach, onehot)
    stats = roll_to(stats, (chips - place) * block % total, 1)
    mask = 2
    while mask < devices:
        stats = merge(stats, send(stats, swap_pairs(devices, mask)))
        mask *= 2
    stats = roll_to(stats, place * block, 1)
    smax, tmax, szero, tzero, cross, picked = [stats[i] for i in range(6)]
    loss_rows = cross / tzero - (tmax + jnp.log(tzero)) + 2.0 * (smax + jnp.log(szero)) - picked
    loss = lax.dynamic_slice_in_dim(loss_rows[:block], core * tokens, tokens, 0)

    sexp = jnp.exp(student - smax[:, None])
    texp = jnp.exp(teach - tmax[:, None])
    dlogit = (
        3.0 * weight[:, None] * (2.0 * sexp / szero[:, None] - texp / tzero[:, None] - onehot)
    ).astype(BF16)

    both_heads = jnp.concatenate([own_head, sib_head])
    term = jnp.dot(dlogit, both_heads, preferred_element_type=F32)
    at = {k: term[block * i : block * (i + 1)] for i, k in enumerate(order)}
    at[-far] = at[far]
    to_right = send(at[far][:, :quarter].astype(BF16), right)
    to_left = send(at[far][:, quarter:].astype(BF16), left)
    for step in range(far - 1, 0, -1):
        if step == far - 1:
            went = jnp.concatenate(
                [at[step][:, :quarter] + to_right.astype(F32), at[step][:, quarter:]], axis=1
            )
            came = jnp.concatenate(
                [at[-step][:, :quarter], at[-step][:, quarter:] + to_left.astype(F32)], axis=1
            )
        else:
            went = at[step] + to_right.astype(F32)
            came = at[-step] + to_left.astype(F32)
        to_right = send(went.astype(BF16), right)
        to_left = send(came.astype(BF16), left)
    summed = (at[0] + to_right.astype(F32) + to_left.astype(F32)).astype(BF16)
    keep = lax.dynamic_slice_in_dim(summed, core * tokens, tokens, 0)
    give = lax.dynamic_slice_in_dim(summed, (1 - core) * tokens, tokens, 0)
    got = send(give, to_core)

    def both_halves(x, y):
        return jnp.where(
            core == 0, jnp.concatenate([x, y], axis=1), jnp.concatenate([y, x], axis=1)
        )

    grad_hidden = both_halves(keep, got)

    def outer(d):
        return lax.dot_general(
            d, whole, (((0,), (0,)), ((), ())), preferred_element_type=F32
        ).astype(BF16)

    grad_sib = send(outer(dlogit[:, ids:]), to_core)
    grad_head = both_halves(outer(dlogit[:, :ids]), grad_sib)
    return loss, grad_hidden, grad_head


def solution(mesh):
    devices = mesh.shape["pipe"]

    def per_device(*args):
        return program(devices, *args)

    placed = (
        P(("groups", "pipe"), None),
        P(("groups", "pipe"), None),
        P("groups", "pipe"),
        P("groups"),
        P("groups"),
    )
    return jax.shard_map(
        per_device,
        mesh=mesh,
        in_specs=placed,
        out_specs=(P(("groups", "pipe")), P(("groups", "pipe"), None), P(("groups", "pipe"), None)),
        check_vma=False,
    )
```

time: 258 us -> 108 us (0.42)
  waiting for transfers between devices: 159 us -> 52.4 us
  blocking collectives: 61.2 us -> 0 us
  starting transfers between devices: 0.08 us -> 26 us
  between operations: 14.1 us -> 0.97 us
  matrix products: 18.8 us -> 7.64 us
  local copies, waits for them, and re-layouts: 1.46 us -> 9.53 us
  other arithmetic: 3.46 us -> 10.9 us
    reduce_scatter x1 -> x0, waiting for transfers between devices: 102 us -> none  [per_device(): summed = lax.psum_scatter(term, 'pipe', scatter_dimension=0, tiled=True)]
    all_gather x1 -> x0, waiting for transfers between devices: 55.9 us -> none  [per_device(): whole = lax.all_gather(hidden, 'pipe', axis=0, tiled=True)]
    ppermute x0 -> x25, waiting for transfers between devices: none -> 52.4 us  [send(): return lax.ppermute(x, 'pipe', perm)]
    pmax x1 -> x0, blocking collectives: 31.7 us -> none  [per_device(): lax.pmax((jnp.max(student, axis=1), jnp.max(teach, axis=1)), 'pipe')]
    psum x1 -> x0, blocking collectives: 29.5 us -> none  [per_device(): lax.psum((jnp.sum(sexp, axis=1), jnp.sum(texp, axis=1), jnp.sum(texp * (t...]
    ppermute x0 -> x25, starting transfers between devices: none -> 26 us  [send(): return lax.ppermute(x, 'pipe', perm)]
    dot_general x3 -> x5, matrix products: 18.8 us -> 7.64 us  [the longest x2 3.23 us: logits(): lax.dot_general(x, w, (((1,), (1,)), ((), ())), preferred_element_type=F32)]
    dynamic_slice x1 -> x5, local copies, waits for them, and re-layouts: 0.59 us -> 6.58 us  [the longest x2 5.88 us: other_half(): return lax.dynamic_slice_in_dim(x, (1 - core) * half, half, 1)]
  transfers between devices with their start and end apart: 2 -> 25, of which waited for: 2 -> 18; matrix products, arithmetic and copies ran while one was open for 4% -> 15% of each run, Pallas kernels for 0% -> 0%
where the time goes in v1:
time: 108 us; the launch traced here: 107 us
  waiting for transfers between devices  52.4 us (49%)
  starting transfers between devices  26 us (24%)
  other arithmetic  10.9 us (10%)
  local copies, waits for them, and re-layouts  9.53 us (9%)
  matrix products  7.64 us (7%)
    ppermute x25, waiting for transfers between devices, send(): return lax.ppermute(x, 'pipe', perm)  52.4 us
    ppermute x25, starting transfers between devices, send(): return lax.ppermute(x, 'pipe', perm)  26 us
    dynamic_slice x2, local copies, waits for them, and re-layouts, other_half(): return lax.dynamic_slice_in_dim(x, (1 - core) * half, half, 1)  5.88 us
    select_n x2, other arithmetic, both_halves(): jnp.where(core == 0, jnp.concatenate([x, y], axis=1), jnp.concatenate([y,...  3.51 us
    dot_general x2, matrix products, logits(): lax.dot_general(x, w, (((1,), (1,)), ((), ())), preferred_element_type=F32)  3.23 us
    dot_general x1, matrix products, program(): term = jnp.dot(dlogit, both_heads, preferred_element_type=F32)  2.88 us
  transfers between devices with their start and end apart: 25, of which 18 were waited for; matrix products, arithmetic and copies ran while one was open for 15% of the time, Pallas kernels for 0%

profile of v1, /device:TPU:0, one launch (start us, length us, event | category | flops | bytes accessed | tf_op | source)
XLA Modules:
  0.0 107.4 jit_solution(3528773853492587862)
XLA Ops:
  2.2 4.9 %constant_dynamic-slice_fusion.2 = (bf16[128,9216]{1,0:T(8,128)(2,1)}, bf16[128,9216]{1,0:T(8,128)(2,1)}) fusion(bf16[128,18432]{1,0:T(8,128)(2,1)} %param.6, s32[]{:T(128)S(6)} %select_n.77, s32[]{:T(128)S(6)} %select_n.76), kind=kLoop, calls=%fused_computation.84 | loop fusion | bytes 9437192 | tf_op jit(solution)/shard_map/dynamic_slice | solution.py:79
  7.9 2.6 %collective-permute-start.1 = (bf16[16,9216]{1,0:T(8,128)(2,1)S(1)}, bf16[16,9216]{1,0:T(8,128)(2,1)}, u32[]{:S(2)}, u32[]{:S(2)}) collective-permute-start(bf16[16,9216]{1,0:T(8,128)(2,1)S(1)} %get-tuple-element.18), channel_id=1, source_target_pairs={{0,2},{1,3},{4,0},{5,1},{8,4},{9,5},{12,8},{13,9},{14,12},{15,13},... | collective-permute-start | bytes 884744 | tf_op jit(solution)/shard_map/ppermute | solution.py:73
  13.7 4.7 %collective-permute-done.1 = bf16[16,9216]{1,0:T(8,128)(2,1)} collective-permute-done((bf16[16,9216]{1,0:T(8,128)(2,1)S(1)}, bf16[16,9216]{1,0:T(8,128)(2,1)}, u32[]{:S(2)}, u32[]{:S(2)}) %collective-permute-start.1) | collective-permute-done | bytes 294944 | tf_op jit(solution)/shard_map/ppermute | solution.py:73
  18.3 1.7 %collective-permute-start.2 = (bf16[16,9216]{1,0:T(8,128)(2,1)}, bf16[16,9216]{1,0:T(8,128)(2,1)S(1)}, u32[]{:S(2)}, u32[]{:S(2)}) collective-permute-start(bf16[16,9216]{1,0:T(8,128)(2,1)} %collective-permute-done.1), channel_id=1, source_target_pairs={{0,2},{1,3},{4,0},{5,1},{8,4},{9,5},{12,8},{13,9},{14,12},{15,13},... | collective-permute-start | bytes 884744 | tf_op jit(solution)/shard_map/ppermute | solution.py:73
  21.5 5.9 %collective-permute-done.2 = bf16[16,9216]{1,0:T(8,128)(2,1)S(1)} collective-permute-done((bf16[16,9216]{1,0:T(8,128)(2,1)}, bf16[16,9216]{1,0:T(8,128)(2,1)S(1)}, u32[]{:S(2)}, u32[]{:S(2)}) %collective-permute-start.2) | collective-permute-done | bytes 294944 | tf_op jit(solution)/shard_map/ppermute | solution.py:73
  27.4 1.5 %collective-permute-start.3 = (bf16[16,9216]{1,0:T(8,128)(2,1)S(1)}, bf16[16,9216]{1,0:T(8,128)(2,1)S(1)}, u32[]{:S(2)}, u32[]{:S(2)}) collective-permute-start(bf16[16,9216]{1,0:T(8,128)(2,1)S(1)} %collective-permute-done.2), channel_id=1, source_target_pairs={{0,2},{1,3},{4,0},{5,1},{8,4},{9,5},{12,8},{13,9},{14,12},{15,13},... | collective-permute-start | bytes 884744 | tf_op jit(solution)/shard_map/ppermute | solution.py:73
  29.4 5.9 %collective-permute-done.3 = bf16[16,9216]{1,0:T(8,128)(2,1)S(1)} collective-permute-done((bf16[16,9216]{1,0:T(8,128)(2,1)S(1)}, bf16[16,9216]{1,0:T(8,128)(2,1)S(1)}, u32[]{:S(2)}, u32[]{:S(2)}) %collective-permute-start.3) | collective-permute-done | bytes 294944 | tf_op jit(solution)/shard_map/ppermute | solution.py:73
  35.3 1.3 %collective-permute-start.8 = (bf16[16,4608]{1,0:T(8,128)(2,1)S(1)}, bf16[16,4608]{1,0:T(8,128)(2,1)S(1)}, u32[]{:S(2)}, u32[]{:S(2)}) collective-permute-start(bf16[16,4608]{1,0:T(8,128)(2,1)S(1)} %slice.299), channel_id=1, source_target_pairs={{0,2},{1,3},{4,0},{5,1},{8,4},{9,5},{12,8},{13,9},{14,12},{15,13},... | collective-permute-start | bytes 442376 | tf_op jit(solution)/shard_map/ppermute | solution.py:73
  37.5 3.0 %collective-permute-done.8 = bf16[16,4608]{1,0:T(8,128)(2,1)S(1)} collective-permute-done((bf16[16,4608]{1,0:T(8,128)(2,1)S(1)}, bf16[16,4608]{1,0:T(8,128)(2,1)S(1)}, u32[]{:S(2)}, u32[]{:S(2)}) %collective-permute-start.8) | collective-permute-done | bytes 147488 | tf_op jit(solution)/shard_map/ppermute | solution.py:73
  40.5 1.3 %collective-permute-done.7 = bf16[16,4608]{1,0:T(8,128)(2,1)S(1)} collective-permute-done((bf16[16,4608]{1,0:T(8,128)(2,1)S(1)}, bf16[16,4608]{1,0:T(8,128)(2,1)S(1)}, u32[]{:S(2)}, u32[]{:S(2)}) %collective-permute-start.7) | collective-permute-done | bytes 147488 | tf_op jit(solution)/shard_map/ppermute | solution.py:73
  42.8 2.4 %fusion.44 = f32[128,128]{0,1:T(8,128)S(1)} fusion(bf16[128,9216]{1,0:T(8,128)(2,1)S(1)} %constant_dynamic-update-slice_fusion, bf16[128,9216]{1,0:T(8,128)(2,1)} %collective-permute-done.9), kind=kOutput, calls=%fused_computation.132 | convolution fusion | flops 301989888 | bytes 4784128 | tf_op jit(solution)/shard_map/dot_general | solution.py:116
  45.3 1.3 %collective-permute-done.10 = f32[128,256]{0,1:T(8,128)S(1)} collective-permute-done((f32[128,256]{0,1:T(8,128)S(1)}, f32[128,256]{0,1:T(8,128)S(1)}, u32[]{:S(2)}, u32[]{:S(2)}) %collective-permute-start.10) | collective-permute-done | bytes 131104 | tf_op jit(solution)/shard_map/ppermute | solution.py:73
  47.0 1.6 %collective-permute-start.12 = (f32[6,128]{1,0:T(8,128)S(1)}, f32[6,128]{1,0:T(8,128)S(1)}, u32[]{:S(2)}, u32[]{:S(2)}) collective-permute-start(f32[6,128]{1,0:T(8,128)S(1)} %fusion.33), channel_id=1, source_target_pairs={{0,2},{1,3},{2,0},{3,1},{4,6},{5,7},{6,4},{7,5},{8,10},{9,11},{10,... | collective-permute-start | bytes 9224 | tf_op jit(solution)/shard_map/ppermute | solution.py:73
  48.5 2.0 %collective-permute-done.12 = f32[6,128]{1,0:T(8,128)S(1)} collective-permute-done((f32[6,128]{1,0:T(8,128)S(1)}, f32[6,128]{1,0:T(8,128)S(1)}, u32[]{:S(2)}, u32[]{:S(2)}) %collective-permute-start.12) | collective-permute-done | bytes 3104 | tf_op jit(solution)/shard_map/ppermute | solution.py:73
  50.6 1.2 %collective-permute-start.13 = (f32[6,128]{1,0:T(8,128)S(1)}, f32[6,128]{1,0:T(8,128)S(1)}, u32[]{:S(2)}, u32[]{:S(2)}) collective-permute-start(f32[6,128]{1,0:T(8,128)S(1)} %stack.24), channel_id=1, source_target_pairs={{0,4},{1,5},{2,6},{3,7},{4,0},{5,1},{6,2},{7,3},{8,12},{9,13},{10,... | collective-permute-start | bytes 9224 | tf_op jit(solution)/shard_map/ppermute | solution.py:73
  52.1 2.3 %collective-permute-done.13 = f32[6,128]{1,0:T(8,128)S(1)} collective-permute-done((f32[6,128]{1,0:T(8,128)S(1)}, f32[6,128]{1,0:T(8,128)S(1)}, u32[]{:S(2)}, u32[]{:S(2)}) %collective-permute-start.13) | collective-permute-done | bytes 3104 | tf_op jit(solution)/shard_map/ppermute | solution.py:73
  54.4 2.2 %collective-permute-start.14 = (f32[6,128]{1,0:T(8,128)S(1)}, f32[6,128]{1,0:T(8,128)S(1)}, u32[]{:S(2)}, u32[]{:S(2)}) collective-permute-start(f32[6,128]{1,0:T(8,128)S(1)} %stack.25), channel_id=1, source_target_pairs={{0,8},{1,9},{2,10},{3,11},{4,12},{5,13},{6,14},{7,15},{8,0},{9,1},... | collective-permute-start | bytes 9224 | tf_op jit(solution)/shard_map/ppermute | solution.py:73
  56.7 2.3 %collective-permute-done.14 = f32[6,128]{1,0:T(8,128)S(1)} collective-permute-done((f32[6,128]{1,0:T(8,128)S(1)}, f32[6,128]{1,0:T(8,128)S(1)}, u32[]{:S(2)}, u32[]{:S(2)}) %collective-permute-start.14) | collective-permute-done | bytes 3104 | tf_op jit(solution)/shard_map/ppermute | solution.py:73
  59.2 2.9 %fusion.42 = (bf16[128,9216]{1,0:T(8,128)(2,1)S(1)}, f32[128,9216]{1,0:T(8,128)S(1)}) fusion(bf16[128,256]{0,1:T(8,128)(2,1)S(1)} %fusion.15, bf16[128,9216]{1,0:T(8,128)(2,1)} %collective-permute-done.9, bf16[128,9216]{1,0:T(8,128)(2,1)} %get-tuple-element.24), kind=kOutput, calls=%fused_computation.130 | convolution fusion | flops 614596608 | bytes 11862016 | tf_op jit(solution)/shard_map/dot_general | solution.py:140
  64.2 3.7 %collective-permute-done.15 = bf16[16,4608]{1,0:T(8,128)(2,1)S(1)} collective-permute-done((bf16[16,4608]{1,0:T(8,128)(2,1)S(1)}, bf16[16,4608]{1,0:T(8,128)(2,1)S(1)}, u32[]{:S(2)}, u32[]{:S(2)}) %collective-permute-start.15) | collective-permute-done | bytes 147488 | tf_op jit(solution)/shard_map/ppermute | solution.py:73
  68.6 1.9 %collective-permute-start.16 = (bf16[16,9216]{1,0:T(8,128)(2,1)S(1)}, bf16[16,9216]{1,0:T(8,128)(2,1)S(1)}, u32[]{:S(2)}, u32[]{:S(2)}) collective-permute-start(bf16[16,9216]{1,0:T(8,128)(2,1)S(1)} %pad_maximum_fusion), channel_id=1, source_target_pairs={{0,4},{1,5},{4,8},{5,9},{8,12},{9,13},{12,14},{13,15},{14,10},{15,... | collective-permute-start | bytes 884744 | tf_op jit(solution)/shard_map/ppermute | solution.py:73
  71.4 5.6 %collective-permute-done.16 = bf16[16,9216]{1,0:T(8,128)(2,1)S(1)} collective-permute-done((bf16[16,9216]{1,0:T(8,128)(2,1)S(1)}, bf16[16,9216]{1,0:T(8,128)(2,1)S(1)}, u32[]{:S(2)}, u32[]{:S(2)}) %collective-permute-start.16) | collective-permute-done | bytes 294944 | tf_op jit(solution)/shard_map/ppermute | solution.py:73
  77.8 2.5 %collective-permute-start.17 = (bf16[16,9216]{1,0:T(8,128)(2,1)}, bf16[16,9216]{1,0:T(8,128)(2,1)S(1)}, u32[]{:S(2)}, u32[]{:S(2)}) collective-permute-start(bf16[16,9216]{1,0:T(8,128)(2,1)} %fusion.6), channel_id=1, source_target_pairs={{0,4},{1,5},{4,8},{5,9},{8,12},{9,13},{12,14},{13,15},{14,10},{15,... | collective-permute-start | bytes 884744 | tf_op jit(solution)/shard_map/ppermute | solution.py:73
  80.3 4.6 %collective-permute-done.17 = bf16[16,9216]{1,0:T(8,128)(2,1)S(1)} collective-permute-done((bf16[16,9216]{1,0:T(8,128)(2,1)}, bf16[16,9216]{1,0:T(8,128)(2,1)S(1)}, u32[]{:S(2)}, u32[]{:S(2)}) %collective-permute-start.17) | collective-permute-done | bytes 294944 | tf_op jit(solution)/shard_map/ppermute | solution.py:73
  84.8 1.3 %fusion.7 = (bf16[16,9216]{1,0:T(8,128)(2,1)S(1)}, bf16[16,9216]{1,0:T(8,128)(2,1)S(1)}) fusion(f32[128,9216]{1,0:T(8,128)} %copy-done.1, bf16[16,9216]{1,0:T(8,128)(2,1)S(1)} %collective-permute-done.17, bf16[16,9216]{1,0:T(8,128)(2,1)S(1)} %collective-permute-done.20), kind=kLoop, calls=%fused_computation.14 | loop fusion | flops 884736 | bytes 2359296 | tf_op jit(solution)/shard_map/convert_element_type | solution.py:156
  86.2 2.1 %collective-permute-start.21 = (bf16[16,9216]{1,0:T(8,128)(2,1)S(1)}, bf16[16,9216]{1,0:T(8,128)(2,1)S(1)}, u32[]{:S(2)}, u32[]{:S(2)}) collective-permute-start(bf16[16,9216]{1,0:T(8,128)(2,1)S(1)} %get-tuple-element.20), channel_id=1, source_target_pairs={{0,2},{1,3},{4,0},{5,1},{8,4},{9,5},{12,8},{13,9},{14,12},{15,13},... | collective-permute-start | bytes 884744 | tf_op jit(solution)/shard_map/ppermute | solution.py:73
  89.5 3.8 %collective-permute-done.21 = bf16[16,9216]{1,0:T(8,128)(2,1)S(1)} collective-permute-done((bf16[16,9216]{1,0:T(8,128)(2,1)S(1)}, bf16[16,9216]{1,0:T(8,128)(2,1)S(1)}, u32[]{:S(2)}, u32[]{:S(2)}) %collective-permute-start.21) | collective-permute-done | bytes 294944 | tf_op jit(solution)/shard_map/ppermute | solution.py:73
  94.4 1.7 %collective-permute-start.22 = (bf16[16,9216]{1,0:T(8,128)(2,1)S(1)}, bf16[16,9216]{1,0:T(8,128)(2,1)S(1)}, u32[]{:S(2)}, u32[]{:S(2)}) collective-permute-start(bf16[16,9216]{1,0:T(8,128)(2,1)S(1)} %fusion.5), channel_id=1, source_target_pairs={{0,2},{1,3},{4,0},{5,1},{8,4},{9,5},{12,8},{13,9},{14,12},{15,13},... | collective-permute-start | bytes 884744 | tf_op jit(solution)/shard_map/ppermute | solution.py:73
  96.9 1.6 %collective-permute-done.18 = bf16[16,9216]{1,0:T(8,128)(2,1)S(1)} collective-permute-done((bf16[16,9216]{1,0:T(8,128)(2,1)S(1)}, bf16[16,9216]{1,0:T(8,128)(2,1)S(1)}, u32[]{:S(2)}, u32[]{:S(2)}) %collective-permute-start.18) | collective-permute-done | bytes 294944 | tf_op jit(solution)/shard_map/ppermute | solution.py:73
  98.5 2.7 %collective-permute-done.22 = bf16[16,9216]{1,0:T(8,128)(2,1)S(1)} collective-permute-done((bf16[16,9216]{1,0:T(8,128)(2,1)S(1)}, bf16[16,9216]{1,0:T(8,128)(2,1)S(1)}, u32[]{:S(2)}, u32[]{:S(2)}) %collective-permute-start.22) | collective-permute-done | bytes 294944 | tf_op jit(solution)/shard_map/ppermute | solution.py:73
  101.2 1.2 %fusion.9 = bf16[16,9216]{1,0:T(8,128)(2,1)S(1)} fusion(f32[128,9216]{1,0:T(8,128)} %copy-done.1, bf16[16,9216]{1,0:T(8,128)(2,1)S(1)} %collective-permute-done.22, bf16[16,9216]{1,0:T(8,128)(2,1)S(1)} %collective-permute-done.18), kind=kLoop, calls=%fused_computation.17 | loop fusion | flops 737280 | bytes 1474560 | tf_op jit(solution)/shard_map/convert_element_type | solution.py:158
  104.7 2.7 %maximum_select_fusion = bf16[128,18432]{1,0:T(8,128)(2,1)} fusion(bf16[128,9216]{1,0:T(8,128)(2,1)S(1)} %collective-permute-done.24, bf16[128,9216]{1,0:T(8,128)(2,1)S(1)} %convolution_convert_fusion.1, pred[]{:T(512)S(6)} %eq.25), kind=kLoop, calls=%fused_computation.6 | loop fusion | flops 21233664 | bytes 9437185 | tf_op jit(solution)/shard_map/jit(_where)/select_n | solution.py:164
  (92 shorter events, 20.2 us)
Async XLA Ops:
  1.7 5.5 %copy-start.3 = (bf16[128,128]{1,0:T(8,128)(2,1)S(1)}, bf16[128,128]{1,0:T(8,128)(2,1)}, u32[]{:S(2)}) copy-start(bf16[128,128]{1,0:T(8,128)(2,1)} %param.7) | copy-start | bytes 98308
  1.7 6.1 %copy-start.4 = (s32[128]{0:T(128)S(1)}, s32[128]{0:T(128)}, u32[]{:S(2)}) copy-start(s32[128]{0:T(128)} %param.8) | copy-start | bytes 1540
  1.7 6.2 %collective-permute-start = (bf16[8,9216]{1,0:T(8,128)(2,1)S(1)}, bf16[8,9216]{1,0:T(8,128)(2,1)S(1)}, u32[]{:S(2)}, u32[]{:S(2)}) collective-permute-start(bf16[8,9216]{1,0:T(8,128)(2,1)S(1)} %get-tuple-element.31), channel_id=1, source_target_pairs={{0,1},{1,0},{2,3},{3,2},{4,5},{5,4},{6,7},{7,6},{8,9},{9,8},{10,11... | collective-permute-start | bytes 442376 | tf_op jit(solution)/shard_map/ppermute | solution.py:73
  7.1 35.7 %collective-permute-start.9 = (bf16[128,9216]{1,0:T(8,128)(2,1)}, bf16[128,9216]{1,0:T(8,128)(2,1)}, u32[]{:S(2)}, u32[]{:S(2)}) collective-permute-start(bf16[128,9216]{1,0:T(8,128)(2,1)} %get-tuple-element.23), channel_id=1, source_target_pairs={{0,1},{1,0},{2,3},{3,2},{4,5},{5,4},{6,7},{7,6},{8,9},{9,8},{10,11... | collective-permute-start | bytes 7077896 | tf_op jit(solution)/shard_map/ppermute | solution.py:73
  7.3 4.1 %collective-permute-start.11 = (bf16[128,128]{0,1:T(8,128)(2,1)S(1)}, bf16[128,128]{0,1:T(8,128)(2,1)S(1)}, u32[]{:S(2)}, u32[]{:S(2)}) collective-permute-start(bf16[128,128]{0,1:T(8,128)(2,1)S(1)} %copy.9), channel_id=1, source_target_pairs={{0,1},{1,0},{2,3},{3,2},{4,5},{5,4},{6,7},{7,6},{8,9},{9,8},{10,11... | collective-permute-start | bytes 98312 | tf_op jit(solution)/shard_map/ppermute | solution.py:73
  7.9 10.4 %collective-permute-start.1 = (bf16[16,9216]{1,0:T(8,128)(2,1)S(1)}, bf16[16,9216]{1,0:T(8,128)(2,1)}, u32[]{:S(2)}, u32[]{:S(2)}) collective-permute-start(bf16[16,9216]{1,0:T(8,128)(2,1)S(1)} %get-tuple-element.18), channel_id=1, source_target_pairs={{0,2},{1,3},{4,0},{5,1},{8,4},{9,5},{12,8},{13,9},{14,12},{15,13},... | collective-permute-start | bytes 884744 | tf_op jit(solution)/shard_map/ppermute | solution.py:73
  10.5 9.5 %collective-permute-start.4 = (bf16[16,9216]{1,0:T(8,128)(2,1)S(1)}, bf16[16,9216]{1,0:T(8,128)(2,1)S(1)}, u32[]{:S(2)}, u32[]{:S(2)}) collective-permute-start(bf16[16,9216]{1,0:T(8,128)(2,1)S(1)} %get-tuple-element.18), channel_id=1, source_target_pairs={{0,4},{1,5},{4,8},{5,9},{8,12},{9,13},{12,14},{13,15},{14,10},{15,... | collective-permute-start | bytes 884744 | tf_op jit(solution)/shard_map/ppermute | solution.py:73
  11.4 0.6 copy-start.2
  18.3 9.0 %collective-permute-start.2 = (bf16[16,9216]{1,0:T(8,128)(2,1)}, bf16[16,9216]{1,0:T(8,128)(2,1)S(1)}, u32[]{:S(2)}, u32[]{:S(2)}) collective-permute-start(bf16[16,9216]{1,0:T(8,128)(2,1)} %collective-permute-done.1), channel_id=1, source_target_pairs={{0,2},{1,3},{4,0},{5,1},{8,4},{9,5},{12,8},{13,9},{14,12},{15,13},... | collective-permute-start | bytes 884744 | tf_op jit(solution)/shard_map/ppermute | solution.py:73
  20.0 8.8 %collective-permute-start.5 = (bf16[16,9216]{1,0:T(8,128)(2,1)S(1)}, bf16[16,9216]{1,0:T(8,128)(2,1)S(1)}, u32[]{:S(2)}, u32[]{:S(2)}) collective-permute-start(bf16[16,9216]{1,0:T(8,128)(2,1)S(1)} %collective-permute-done.4), channel_id=1, source_target_pairs={{0,4},{1,5},{4,8},{5,9},{8,12},{9,13},{12,14},{13,15},{14,10},{15,... | collective-permute-start | bytes 884744 | tf_op jit(solution)/shard_map/ppermute | solution.py:73
  20.4 21.6 %copy-start = (bf16[128,9216]{1,0:T(8,128)(2,1)S(1)}, bf16[128,9216]{1,0:T(8,128)(2,1)}, u32[]{:S(2)}) copy-start(bf16[128,9216]{1,0:T(8,128)(2,1)} %get-tuple-element.24) | copy-start | bytes 7077892
  27.4 8.0 %collective-permute-start.3 = (bf16[16,9216]{1,0:T(8,128)(2,1)S(1)}, bf16[16,9216]{1,0:T(8,128)(2,1)S(1)}, u32[]{:S(2)}, u32[]{:S(2)}) collective-permute-start(bf16[16,9216]{1,0:T(8,128)(2,1)S(1)} %collective-permute-done.2), channel_id=1, source_target_pairs={{0,2},{1,3},{4,0},{5,1},{8,4},{9,5},{12,8},{13,9},{14,12},{15,13},... | collective-permute-start | bytes 884744 | tf_op jit(solution)/shard_map/ppermute | solution.py:73
  28.8 7.8 %collective-permute-start.6 = (bf16[16,9216]{1,0:T(8,128)(2,1)S(1)}, bf16[16,9216]{1,0:T(8,128)(2,1)S(1)}, u32[]{:S(2)}, u32[]{:S(2)}) collective-permute-start(bf16[16,9216]{1,0:T(8,128)(2,1)S(1)} %collective-permute-done.5), channel_id=1, source_target_pairs={{0,4},{1,5},{4,8},{5,9},{8,12},{9,13},{12,14},{13,15},{14,10},{15,... | collective-permute-start | bytes 884744 | tf_op jit(solution)/shard_map/ppermute | solution.py:73
  35.3 5.2 %collective-permute-start.8 = (bf16[16,4608]{1,0:T(8,128)(2,1)S(1)}, bf16[16,4608]{1,0:T(8,128)(2,1)S(1)}, u32[]{:S(2)}, u32[]{:S(2)}) collective-permute-start(bf16[16,4608]{1,0:T(8,128)(2,1)S(1)} %slice.299), channel_id=1, source_target_pairs={{0,2},{1,3},{4,0},{5,1},{8,4},{9,5},{12,8},{13,9},{14,12},{15,13},... | collective-permute-start | bytes 442376 | tf_op jit(solution)/shard_map/ppermute | solution.py:73
  36.6 5.2 %collective-permute-start.7 = (bf16[16,4608]{1,0:T(8,128)(2,1)S(1)}, bf16[16,4608]{1,0:T(8,128)(2,1)S(1)}, u32[]{:S(2)}, u32[]{:S(2)}) collective-permute-start(bf16[16,4608]{1,0:T(8,128)(2,1)S(1)} %slice.298), channel_id=1, source_target_pairs={{0,4},{1,5},{4,8},{5,9},{8,12},{9,13},{12,14},{13,15},{14,10},{15,... | collective-permute-start | bytes 442376 | tf_op jit(solution)/shard_map/ppermute | solution.py:73
  42.8 9.1 %copy-start.5 = (f32[128]{0:T(128)S(1)}, f32[128]{0:T(128)}, u32[]{:S(2)}) copy-start(f32[128]{0:T(128)} %param.9) | copy-start | bytes 1540
  45.2 1.4 %collective-permute-start.10 = (f32[128,256]{0,1:T(8,128)S(1)}, f32[128,256]{0,1:T(8,128)S(1)}, u32[]{:S(2)}, u32[]{:S(2)}) collective-permute-start(f32[128,256]{0,1:T(8,128)S(1)} %pad_maximum_fusion.2), channel_id=1, source_target_pairs={{0,1},{1,0},{2,3},{3,2},{4,5},{5,4},{6,7},{7,6},{8,9},{9,8},{10,11... | collective-permute-start | bytes 393224 | tf_op jit(solution)/shard_map/ppermute | solution.py:73
  47.0 3.6 %collective-permute-start.12 = (f32[6,128]{1,0:T(8,128)S(1)}, f32[6,128]{1,0:T(8,128)S(1)}, u32[]{:S(2)}, u32[]{:S(2)}) collective-permute-start(f32[6,128]{1,0:T(8,128)S(1)} %fusion.33), channel_id=1, source_target_pairs={{0,2},{1,3},{2,0},{3,1},{4,6},{5,7},{6,4},{7,5},{8,10},{9,11},{10,... | collective-permute-start | bytes 9224 | tf_op jit(solution)/shard_map/ppermute | solution.py:73
  50.6 3.7 %collective-permute-start.13 = (f32[6,128]{1,0:T(8,128)S(1)}, f32[6,128]{1,0:T(8,128)S(1)}, u32[]{:S(2)}, u32[]{:S(2)}) collective-permute-start(f32[6,128]{1,0:T(8,128)S(1)} %stack.24), channel_id=1, source_target_pairs={{0,4},{1,5},{2,6},{3,7},{4,0},{5,1},{6,2},{7,3},{8,12},{9,13},{10,... | collective-permute-start | bytes 9224 | tf_op jit(solution)/shard_map/ppermute | solution.py:73
  54.4 4.6 %collective-permute-start.14 = (f32[6,128]{1,0:T(8,128)S(1)}, f32[6,128]{1,0:T(8,128)S(1)}, u32[]{:S(2)}, u32[]{:S(2)}) collective-permute-start(f32[6,128]{1,0:T(8,128)S(1)} %stack.25), channel_id=1, source_target_pairs={{0,8},{1,9},{2,10},{3,11},{4,12},{5,13},{6,14},{7,15},{8,0},{9,1},... | collective-permute-start | bytes 9224 | tf_op jit(solution)/shard_map/ppermute | solution.py:73
  62.1 15.7 %copy-start.1 = (f32[128,9216]{1,0:T(8,128)}, f32[128,9216]{1,0:T(8,128)S(1)}, u32[]{:S(2)}) copy-start(f32[128,9216]{1,0:T(8,128)S(1)} %get-tuple-element.74) | copy-start | bytes 14155780
  62.2 5.8 %collective-permute-start.15 = (bf16[16,4608]{1,0:T(8,128)(2,1)S(1)}, bf16[16,4608]{1,0:T(8,128)(2,1)S(1)}, u32[]{:S(2)}, u32[]{:S(2)}) collective-permute-start(bf16[16,4608]{1,0:T(8,128)(2,1)S(1)} %get-tuple-element.25), channel_id=1, source_target_pairs={{0,4},{1,5},{4,8},{5,9},{8,12},{9,13},{12,14},{13,15},{14,10},{15,... | collective-permute-start | bytes 442376 | tf_op jit(solution)/shard_map/ppermute | solution.py:73
  63.3 5.1 %collective-permute-start.19 = (bf16[16,4608]{1,0:T(8,128)(2,1)S(1)}, bf16[16,4608]{1,0:T(8,128)(2,1)S(1)}, u32[]{:S(2)}, u32[]{:S(2)}) collective-permute-start(bf16[16,4608]{1,0:T(8,128)(2,1)S(1)} %get-tuple-element.26), channel_id=1, source_target_pairs={{0,2},{1,3},{4,0},{5,1},{8,4},{9,5},{12,8},{13,9},{14,12},{15,13},... | collective-permute-start | bytes 442376 | tf_op jit(solution)/shard_map/ppermute | solution.py:73
  68.6 8.4 %collective-permute-start.16 = (bf16[16,9216]{1,0:T(8,128)(2,1)S(1)}, bf16[16,9216]{1,0:T(8,128)(2,1)S(1)}, u32[]{:S(2)}, u32[]{:S(2)}) collective-permute-start(bf16[16,9216]{1,0:T(8,128)(2,1)S(1)} %pad_maximum_fusion), channel_id=1, source_target_pairs={{0,4},{1,5},{4,8},{5,9},{8,12},{9,13},{12,14},{13,15},{14,10},{15,... | collective-permute-start | bytes 884744 | tf_op jit(solution)/shard_map/ppermute | solution.py:73
  71.3 9.0 %collective-permute-start.20 = (bf16[16,9216]{1,0:T(8,128)(2,1)}, bf16[16,9216]{1,0:T(8,128)(2,1)S(1)}, u32[]{:S(2)}, u32[]{:S(2)}) collective-permute-start(bf16[16,9216]{1,0:T(8,128)(2,1)} %pad_maximum_fusion.1), channel_id=1, source_target_pairs={{0,2},{1,3},{4,0},{5,1},{8,4},{9,5},{12,8},{13,9},{14,12},{15,13},... | collective-permute-start | bytes 884744 | tf_op jit(solution)/shard_map/ppermute | solution.py:73
  77.8 7.1 %collective-permute-start.17 = (bf16[16,9216]{1,0:T(8,128)(2,1)}, bf16[16,9216]{1,0:T(8,128)(2,1)S(1)}, u32[]{:S(2)}, u32[]{:S(2)}) collective-permute-start(bf16[16,9216]{1,0:T(8,128)(2,1)} %fusion.6), channel_id=1, source_target_pairs={{0,4},{1,5},{4,8},{5,9},{8,12},{9,13},{12,14},{13,15},{14,10},{15,... | collective-permute-start | bytes 884744 | tf_op jit(solution)/shard_map/ppermute | solution.py:73
  86.2 7.1 %collective-permute-start.21 = (bf16[16,9216]{1,0:T(8,128)(2,1)S(1)}, bf16[16,9216]{1,0:T(8,128)(2,1)S(1)}, u32[]{:S(2)}, u32[]{:S(2)}) collective-permute-start(bf16[16,9216]{1,0:T(8,128)(2,1)S(1)} %get-tuple-element.20), channel_id=1, source_target_pairs={{0,2},{1,3},{4,0},{5,1},{8,4},{9,5},{12,8},{13,9},{14,12},{15,13},... | collective-permute-start | bytes 884744 | tf_op jit(solution)/shard_map/ppermute | solution.py:73
  89.0 15.6 %collective-permute-start.24 = (bf16[128,9216]{1,0:T(8,128)(2,1)S(1)}, bf16[128,9216]{1,0:T(8,128)(2,1)S(1)}, u32[]{:S(2)}, u32[]{:S(2)}) collective-permute-start(bf16[128,9216]{1,0:T(8,128)(2,1)S(1)} %convolution_convert_fusion), channel_id=1, source_target_pairs={{0,1},{1,0},{2,3},{3,2},{4,5},{5,4},{6,7},{7,6},{8,9},{9,8},{10,11... | collective-permute-start | bytes 7077896 | tf_op jit(solution)/shard_map/ppermute | solution.py:73
  89.1 9.4 %collective-permute-start.18 = (bf16[16,9216]{1,0:T(8,128)(2,1)S(1)}, bf16[16,9216]{1,0:T(8,128)(2,1)S(1)}, u32[]{:S(2)}, u32[]{:S(2)}) collective-permute-start(bf16[16,9216]{1,0:T(8,128)(2,1)S(1)} %get-tuple-element.19), channel_id=1, source_target_pairs={{0,4},{1,5},{4,8},{5,9},{8,12},{9,13},{12,14},{13,15},{14,10},{15,... | collective-permute-start | bytes 884744 | tf_op jit(solution)/shard_map/ppermute | solution.py:73
  94.4 6.8 %collective-permute-start.22 = (bf16[16,9216]{1,0:T(8,128)(2,1)S(1)}, bf16[16,9216]{1,0:T(8,128)(2,1)S(1)}, u32[]{:S(2)}, u32[]{:S(2)}) collective-permute-start(bf16[16,9216]{1,0:T(8,128)(2,1)S(1)} %fusion.5), channel_id=1, source_target_pairs={{0,2},{1,3},{4,0},{5,1},{8,4},{9,5},{12,8},{13,9},{14,12},{15,13},... | collective-permute-start | bytes 884744 | tf_op jit(solution)/shard_map/ppermute | solution.py:73
  102.4 1.4 %collective-permute-start.23 = (bf16[8,9216]{1,0:T(8,128)(2,1)S(1)}, bf16[8,9216]{1,0:T(8,128)(2,1)S(1)}, u32[]{:S(2)}, u32[]{:S(2)}) collective-permute-start(bf16[8,9216]{1,0:T(8,128)(2,1)S(1)} %get-tuple-element.30), channel_id=1, source_target_pairs={{0,1},{1,0},{2,3},{3,2},{4,5},{5,4},{6,7},{7,6},{8,9},{9,8},{10,11... | collective-permute-start | bytes 442376 | tf_op jit(solution)/shard_map/ppermute | solution.py:73

commit v2 on v0

v2 whole, which is shorter than its diff:
```python
import jax
import jax.numpy as jnp
from jax import lax
from jax.experimental import pallas as pl
from jax.experimental.pallas import tpu as pltpu
from jax.sharding import PartitionSpec as P

F32 = jnp.float32
BF16 = jnp.bfloat16


def chip_ring(chips):
    return list(range(0, chips, 2)) + list(reversed(range(1, chips, 2)))


def shift_pairs(ring, by):
    n = len(ring)
    return [(2 * ring[i] + c, 2 * ring[(i + by) % n] + c) for i in range(n) for c in (0, 1)]


def in_vmem(count):
    return [pl.BlockSpec(memory_space=pltpu.VMEM)] * count


def kernel_params():
    return pltpu.CompilerParams(vmem_limit_bytes=12 * 2**20)


def stack_heads(own, sib):
    ids, width = own.shape

    def body(own_ref, sib_ref, out_ref, sem):
        copies = [
            pltpu.make_async_copy(own_ref, out_ref.at[0:ids], sem.at[0]),
            pltpu.make_async_copy(sib_ref, out_ref.at[ids : 2 * ids], sem.at[1]),
        ]
        for c in copies:
            c.start()
        for c in copies:
            c.wait()

    return pl.pallas_call(
        body,
        out_shape=pltpu.VMEM((2 * ids, width), own.dtype),
        in_specs=[pl.BlockSpec(memory_space=pl.ANY)] * 2,
        out_specs=in_vmem(1)[0],
        scratch_shapes=[pltpu.SemaphoreType.DMA((2,))],
        compiler_params=kernel_params(),
        cost_estimate=pl.CostEstimate(
            flops=0, bytes_accessed=8 * ids * width, transcendentals=0
        ),
        name="stack_heads",
    )(own, sib)


def tile_of(width, most):
    tile = 128
    while tile * 2 <= most and width % (tile * 2) == 0:
        tile *= 2
    for factor in (3, 9):
        if tile * factor <= most and width % (tile * factor) == 0:
            return tile * factor
    return tile


def rows_of(group, start, size):
    parts = []
    for pieces in group:
        piece, at = pieces[0], start
        if start >= piece.shape[1]:
            piece, at = pieces[1], start - piece.shape[1]
        parts.append(piece[:, at : at + size])
    if len(parts) == 1:
        return parts[0]
    return jnp.concatenate([p.astype(F32) for p in parts]).astype(parts[0].dtype)


def whole_rows(group):
    return jnp.concatenate([jnp.concatenate(pieces, axis=1) for pieces in group])


def regroup(group, refs):
    refs = iter(refs)
    return [[next(refs) for _ in pieces] for pieces in group]


def logits(group, heads):
    tokens = group[0][0].shape[0]
    ids, width = heads.shape
    rows = tokens * len(group)
    if tokens % 8:
        return 3.0 * lax.dot_general(
            heads, whole_rows(group), (((1,), (1,)), ((), ())), preferred_element_type=F32
        )
    tile = tile_of(width // 2, 2304)
    flat = [x for pieces in group for x in pieces]

    def body(*refs):
        heads_ref, out_ref = refs[-2:]
        blocks = regroup(group, refs)
        acc = jnp.zeros((ids, rows), F32)
        for j in range(width // tile):
            x = rows_of(blocks, j * tile, tile)
            w = heads_ref[:, j * tile : (j + 1) * tile]
            acc += lax.dot_general(w, x, (((1,), (1,)), ((), ())), preferred_element_type=F32)
        out_ref[...] = 3.0 * acc

    return pl.pallas_call(
        body,
        out_shape=jax.ShapeDtypeStruct((ids, rows), F32),
        in_specs=in_vmem(len(flat) + 1),
        out_specs=in_vmem(1)[0],
        compiler_params=kernel_params(),
        cost_estimate=pl.CostEstimate(
            flops=2 * ids * max(rows, 256) * width,
            bytes_accessed=2 * ids * width,
            transcendentals=0,
        ),
        name="logits",
    )(*flat, heads)


def assemble(group):
    tokens, dtype = group[0][0].shape[0], group[0][0].dtype
    rows = tokens * len(group)
    width = sum(x.shape[1] for x in group[0])
    if tokens % 8:
        return whole_rows(group)
    flat = [x for pieces in group for x in pieces]

    def body(*refs):
        out_ref = refs[-1]
        blocks = regroup(group, refs)
        for start in (0, width // 2):
            for i in range(0, len(blocks), 2):
                two = blocks[i : i + 2]
                out_ref[
                    tokens * i : tokens * (i + len(two)), start : start + width // 2
                ] = rows_of(two, start, width // 2)

    return pl.pallas_call(
        body,
        out_shape=pltpu.VMEM((rows, width), dtype),
        in_specs=in_vmem(len(flat)),
        out_specs=in_vmem(1)[0],
        compiler_params=kernel_params(),
        cost_estimate=pl.CostEstimate(
            flops=0, bytes_accessed=4 * rows * width, transcendentals=0
        ),
        name="assemble",
    )(*flat)


def gradient_terms(dlogit, heads, late):
    ids, rows = dlogit.shape
    half = heads.shape[1] // 2
    early = rows - late
    if late % 8:
        term = lax.dot_general(dlogit, heads, (((0,), (0,)), ((), ())), preferred_element_type=F32)
        halves = term[:, :half], term[:, half:]
        return [h[:early] for h in halves] + [h[early:].astype(BF16) for h in halves]
    tile = tile_of(half, 1024)
    steps = half // tile

    def body(d_ref, heads_ref, *refs):
        d = d_ref[...].T
        for j in range(2 * steps):
            w = heads_ref[:, j * tile : (j + 1) * tile]
            term = jnp.dot(d, w, preferred_element_type=F32)
            cols = slice(j % steps * tile, (j % steps + 1) * tile)
            refs[j // steps][:, cols] = term[:early]
            refs[2 + j // steps][:, cols] = term[early:].astype(BF16)

    return pl.pallas_call(
        body,
        out_shape=[pltpu.VMEM((early, half), F32)] * 2 + [pltpu.VMEM((late, half), BF16)] * 2,
        in_specs=in_vmem(2),
        out_specs=in_vmem(4),
        compiler_params=kernel_params(),
        cost_estimate=pl.CostEstimate(
            flops=2 * ids * 256 * 2 * half, bytes_accessed=4 * ids * half, transcendentals=0
        ),
        name="gradient_terms",
    )(dlogit, heads)


def ring_sums(term, rows, flows):
    half = term.shape[1]
    given = [f for f in flows if f is not None]
    tokens = given[0].shape[0]

    def total(own, flow):
        return (own if flow is None else own + flow.astype(F32)).astype(BF16)

    if tokens % 8:
        return [total(term[r : r + tokens], f) for r, f in zip(rows, flows)]

    def body(term_ref, *refs):
        came = iter(refs[: len(given)])
        for i in (0, 1):
            flow = None if flows[i] is None else next(came)[...]
            refs[len(given) + i][...] = total(term_ref[rows[i] : rows[i] + tokens, :], flow)

    return pl.pallas_call(
        body,
        out_shape=[jax.ShapeDtypeStruct((tokens, half), BF16)] * 2,
        in_specs=in_vmem(1 + len(given)),
        out_specs=in_vmem(2),
        compiler_params=kernel_params(),
        cost_estimate=pl.CostEstimate(
            flops=2 * tokens * half, bytes_accessed=4 * tokens * half, transcendentals=0
        ),
        name="ring_sums",
    )(term, *given)


def local_stats(student, teach, onehot):
    sm = jnp.max(student, axis=0)
    tm = jnp.max(teach, axis=0)
    sexp = jnp.exp(student - sm)
    texp = jnp.exp(teach - tm)
    return jnp.stack(
        [
            sm,
            tm,
            jnp.sum(sexp, axis=0),
            jnp.sum(texp, axis=0),
            jnp.sum(texp * (teach - student), axis=0),
            jnp.sum(onehot * student, axis=0),
        ]
    )


def merge(every):
    sm = jnp.max(every[:, 0], axis=0)
    tm = jnp.max(every[:, 1], axis=0)
    s = jnp.exp(every[:, 0] - sm)
    t = jnp.exp(every[:, 1] - tm)
    return (
        sm,
        tm,
        jnp.sum(every[:, 2] * s, axis=0),
        jnp.sum(every[:, 3] * t, axis=0),
        jnp.sum(every[:, 4] * t, axis=0),
        jnp.sum(every[:, 5], axis=0),
    )


def from_every_chip(x, ring):
    n = len(ring)
    known = x[None]
    reach = 0
    while known.shape[0] < n:
        width = 2 * reach + 1
        missing = n - width
        right = min(width, (missing + 1) // 2)
        left = min(width, missing - right)
        ahead = lax.ppermute(known[:right], "pipe", shift_pairs(ring, -width))
        parts = [known, ahead]
        if left:
            parts.insert(0, lax.ppermute(known[width - left :], "pipe", shift_pairs(ring, width)))
        known = jnp.concatenate(parts)
        reach = 3 * reach + 1
    return known


def program(devices, hidden, head_rows, teacher, targets, token_weight):
    chips = devices // 2
    ring = chip_ring(chips)
    far = chips // 2
    tokens, width = hidden.shape
    half = width // 2
    ids = head_rows.shape[0]

    me = lax.axis_index("pipe")
    core = me % 2
    chip = me // 2
    place = jnp.where(chip % 2 == 0, chip // 2, chips - 1 - chip // 2)
    to_core = [(i, i ^ 1) for i in range(devices)]
    to_right, to_left = shift_pairs(ring, 1), shift_pairs(ring, -1)

    def send(x, perm):
        return lax.ppermute(x, "pipe", perm)

    sib_head = send(head_rows, to_core)
    heads = stack_heads(head_rows, sib_head)

    blocks = {0: hidden}
    for k in range(1, far):
        behind, ahead = blocks[1 - k], blocks[k - 1]
        if k == far - 1:
            behind, ahead, heads = lax.optimization_barrier((behind, ahead, heads))
        blocks[-k] = send(behind, to_right)
        blocks[k] = send(ahead, to_left)
    order = list(range(0, far)) + list(range(1 - far, 0)) + [far]
    order = [0] + [s * k for k in range(1, far) for s in (1, -1)] + [far]
    near = [k for k in order if abs(k) < far - 1]
    early = logits([[blocks[k]] for k in near], heads)
    rest = [k for k in order if k not in near and k != far]
    edge_left, edge_right, early = lax.optimization_barrier((blocks[1 - far], blocks[far - 1], early))
    last = (send(edge_left[:, :half], to_right), send(edge_right[:, half:], to_left))
    blocks = {k: [x] for k, x in blocks.items()}
    blocks[far] = last
    parts = [early, logits([blocks[k] for k in rest], heads), logits([blocks[far]], heads)]
    rows = len(order) * tokens

    steps = jnp.array(order, jnp.int32)
    at = (place + steps) % chips
    row_chip = jnp.where(at < chips // 2, 2 * at, 2 * (chips - 1 - at) + 1)
    inner = jnp.arange(tokens, dtype=jnp.int32)[None, :]
    row_token = (((2 * row_chip + core) * tokens)[:, None] + inner).reshape(rows)
    row_slot = ((row_chip * tokens)[:, None] + inner).reshape(rows)
    select = row_token[:, None] == jnp.arange(devices * tokens, dtype=jnp.int32)[None, :]
    slots = (row_slot[:, None] == jnp.arange(rows, dtype=jnp.int32)[None, :]).astype(F32)

    def pick(x):
        return jnp.sum(jnp.where(select, x[None, :], 0), axis=1, dtype=x.dtype)

    both_teacher = jnp.concatenate([teacher, send(teacher, to_core)], axis=1)
    teach = lax.dot_general(
        both_teacher, select.astype(BF16), (((0,), (1,)), ((), ())), preferred_element_type=F32
    )
    target = pick(targets)
    weight = pick(token_weight)
    lanes = jnp.arange(ids, dtype=jnp.int32)
    columns = jnp.concatenate([me * ids + lanes, (me ^ 1) * ids + lanes])
    onehot = (columns[:, None] == target[None, :]).astype(F32)

    student = jnp.concatenate(parts, axis=1)
    exact = lax.Precision.HIGHEST
    stats = jnp.dot(local_stats(student, teach, onehot), slots, precision=exact)
    merged = jnp.stack(merge(from_every_chip(stats, ring)))
    smax, tmax, szero, tzero, cross, picked = lax.dot_general(
        merged, slots, (((1,), (1,)), ((), ())), precision=exact
    )
    loss_rows = cross / tzero - (tmax + jnp.log(tzero)) + 2.0 * (smax + jnp.log(szero)) - picked
    loss = loss_rows[:tokens]

    sexp = jnp.exp(student - smax)
    texp = jnp.exp(teach - tmax)
    dlogit = (3.0 * weight * (2.0 * sexp / szero - texp / tzero - onehot)).astype(BF16)

    *term, first, second = gradient_terms(dlogit, heads, tokens)
    flows = [[send(first, to_right), None], [None, send(second, to_left)]]
    held, first = lax.optimization_barrier(([tuple(blocks[k]) for k in order], first))
    whole = assemble(held)
    sib_whole = send(whole, to_core)
    for k in range(far - 1, 0, -1):
        rows_at = [tokens * order.index(k), tokens * order.index(-k)]
        for i in (0, 1):
            sums = ring_sums(term[i], rows_at, flows[i])
            flows[i] = [send(sums[0], to_right), send(sums[1], to_left)]

    sib_dlogit = send(dlogit[ids:], to_core)
    grad_head = lax.dot_general(
        jnp.concatenate([dlogit[:ids], sib_dlogit], axis=1),
        jnp.concatenate([whole, sib_whole]),
        (((1,), (0,)), ((), ())),
        preferred_element_type=F32,
    ).astype(BF16)
    term, grad_head = lax.optimization_barrier((tuple(term), grad_head))
    grad_hidden = jnp.concatenate(
        [
            (t[:tokens] + f[0].astype(F32) + f[1].astype(F32)).astype(BF16)
            for t, f in zip(term, flows)
        ],
        axis=1,
    )
    return loss, grad_hidden, grad_head


def solution(mesh):
    devices = mesh.shape["pipe"]

    def per_device(*args):
        return program(devices, *args)

    placed = (
        P(("groups", "pipe"), None),
        P(("groups", "pipe"), None),
        P("groups", "pipe"),
        P("groups"),
        P("groups"),
    )
    return jax.shard_map(
        per_device,
        mesh=mesh,
        in_specs=placed,
        out_specs=(P(("groups", "pipe")), P(("groups", "pipe"), None), P(("groups", "pipe"), None)),
        check_vma=False,
    )
```

time: 258 us -> 92.9 us (0.36)
  waiting for transfers between devices: 159 us -> 27.7 us
  blocking collectives: 61.2 us -> 0 us
  starting transfers between devices: 0.08 us -> 29.6 us
  matrix products: 18.8 us -> 3.72 us
  between operations: 14.1 us -> 0.85 us
  Pallas kernels: 0 us -> 12.7 us
  local copies, waits for them, and re-layouts: 1.46 us -> 13.7 us
    reduce_scatter x1 -> x0, waiting for transfers between devices: 102 us -> none  [per_device(): summed = lax.psum_scatter(term, 'pipe', scatter_dimension=0, tiled=True)]
    all_gather x1 -> x0, waiting for transfers between devices: 55.9 us -> none  [per_device(): whole = lax.all_gather(hidden, 'pipe', axis=0, tiled=True)]
    pmax x1 -> x0, blocking collectives: 31.7 us -> none  [per_device(): lax.pmax((jnp.max(student, axis=1), jnp.max(teach, axis=1)), 'pipe')]
    ppermute x0 -> x30, starting transfers between devices: none -> 29.6 us  [the longest x26 22.9 us: send(): return lax.ppermute(x, 'pipe', perm)]
    psum x1 -> x0, blocking collectives: 29.5 us -> none  [per_device(): lax.psum((jnp.sum(sexp, axis=1), jnp.sum(texp, axis=1), jnp.sum(texp * (t...]
    ppermute x0 -> x30, waiting for transfers between devices: none -> 27.7 us  [the longest x26 22.1 us: send(): return lax.ppermute(x, 'pipe', perm)]
    dot_general x3 -> x4, matrix products: 18.8 us -> 3.72 us  [the longest x1 3.06 us: program(): lax.dot_general(jnp.concatenate([dlogit[:ids], sib_dlogit], axis=1), jnp....]
    pallas_call x0 -> x12, Pallas kernels: none -> 12.7 us  [the longest x3 7.69 us: logits(): pl.pallas_call(body, out_shape=jax.ShapeDtypeStruct((ids, rows), F32), in...]
  transfers between devices with their start and end apart: 2 -> 30, of which waited for: 2 -> 16; matrix products, arithmetic and copies ran while one was open for 4% -> 7% of each run, Pallas kernels for 0% -> 9%
where the time goes in v2:
time: 92.9 us; the launch traced here: 92.7 us
  starting transfers between devices  29.6 us (32%)
  waiting for transfers between devices  27.7 us (30%)
  local copies, waits for them, and re-layouts  13.7 us (15%)
  Pallas kernels  12.7 us (14%)
  other arithmetic  4.41 us (5%)
  matrix products  3.72 us (4%)
    ppermute x26, starting transfers between devices, send(): return lax.ppermute(x, 'pipe', perm)  22.9 us
    ppermute x26, waiting for transfers between devices, send(): return lax.ppermute(x, 'pipe', perm)  22.1 us
    unnamed x16, local copies, waits for them, and re-layouts  13.3 us
    pallas_call x3, Pallas kernels, logits(): pl.pallas_call(body, out_shape=jax.ShapeDtypeStruct((ids, rows), F32), in...  7.69 us
    ppermute x2, waiting for transfers between devices, from_every_chip(): ahead = lax.ppermute(known[:right], 'pipe', shift_pairs(ring, -width))  4.81 us
    ppermute x2, starting transfers between devices, from_every_chip(): lax.ppermute(known[width - left:], 'pipe', shift_pairs(ring, width))  3.59 us
    ppermute x2, starting transfers between devices, from_every_chip(): ahead = lax.ppermute(known[:right], 'pipe', shift_pairs(ring, -width))  3.08 us
    dot_general x1, matrix products, program(): lax.dot_general(jnp.concatenate([dlogit[:ids], sib_dlogit], axis=1), jnp....  3.06 us
  transfers between devices with their start and end apart: 30, of which 16 were waited for; matrix products, arithmetic and copies ran while one was open for 7% of the time, Pallas kernels for 9%

profile of v2, /device:TPU:0, one launch (start us, length us, event | category | flops | bytes accessed | tf_op | source)
XLA Modules:
  0.0 92.7 jit_solution(10950604239273029316)
XLA Ops:
  1.1 2.6 %collective-permute-start.2 = (bf16[8,18432]{1,0:T(8,128)(2,1)}, bf16[8,18432]{1,0:T(8,128)(2,1)S(1)}, u32[]{:S(2)}, u32[]{:S(2)}) collective-permute-start(bf16[8,18432]{1,0:T(8,128)(2,1)} %refs_0_.2), channel_id=1, source_target_pairs={{0,2},{1,3},{4,0},{5,1},{8,4},{9,5},{12,8},{13,9},{14,12},{15,13},... | collective-permute-start | bytes 884744 | tf_op jit(solution)/shard_map/ppermute | solution.py:283
  6.5 5.1 %collective-permute-done.2.refs_1_ = bf16[8,18432]{1,0:T(8,128)(2,1)S(1)} collective-permute-done((bf16[8,18432]{1,0:T(8,128)(2,1)}, bf16[8,18432]{1,0:T(8,128)(2,1)S(1)}, u32[]{:S(2)}, u32[]{:S(2)}) %collective-permute-start.2) | collective-permute-done | bytes 294944 | tf_op jit(solution)/shard_map/ppermute | solution.py:283
  11.6 1.7 %collective-permute-start.3 = (bf16[8,18432]{1,0:T(8,128)(2,1)S(1)}, bf16[8,18432]{1,0:T(8,128)(2,1)S(1)}, u32[]{:S(2)}, u32[]{:S(2)}) collective-permute-start(bf16[8,18432]{1,0:T(8,128)(2,1)S(1)} %collective-permute-done.2.refs_1_), channel_id=1, source_target_pairs={{0,2},{1,3},{4,0},{5,1},{8,4},{9,5},{12,8},{13,9},{14,12},{15,13},... | collective-permute-start | bytes 884744 | tf_op jit(solution)/shard_map/ppermute | solution.py:283
  13.8 2.3 %copy-done.3 = bf16[128,18432]{1,0:T(8,128)(2,1)S(1)} copy-done((bf16[128,18432]{1,0:T(8,128)(2,1)S(1)}, bf16[128,18432]{1,0:T(8,128)(2,1)}, u32[]{:S(2)}) %copy-start.3) | copy-done | bytes 4718616
  16.1 2.7 %stack_heads.1.refs_5_.refs_2_.heads_ref = bf16[256,18432]{1,0:T(8,128)(2,1)S(1)} custom-call(bf16[128,18432]{1,0:T(8,128)(2,1)S(1)} %copy-done.3, bf16[128,18432]{1,0:T(8,128)(2,1)} %collective-permute-done.4.sib_ref), custom_call_target="tpu_custom_call" | custom-call | bytes 18874368 | tf_op jit(solution)/shard_map/stack_heads/pallas_call | solution.py:42
  18.8 3.6 %copy-done = bf16[256,18432]{1,0:T(8,128)(2,1)} copy-done((bf16[256,18432]{1,0:T(8,128)(2,1)}, bf16[256,18432]{1,0:T(8,128)(2,1)S(1)}, u32[]{:S(2)}) %copy-start) | copy-done | bytes 9437208
  22.5 1.7 %collective-permute-start.5 = (bf16[8,18432]{1,0:T(8,128)(2,1)S(1)}, bf16[8,18432]{1,0:T(8,128)(2,1)S(1)}, u32[]{:S(2)}, u32[]{:S(2)}) collective-permute-start(bf16[8,18432]{1,0:T(8,128)(2,1)S(1)} %collective-permute-done.1.refs_4_), channel_id=1, source_target_pairs={{0,4},{1,5},{4,8},{5,9},{8,12},{9,13},{12,14},{13,15},{14,10},{15,... | collective-permute-start | bytes 884744 | tf_op jit(solution)/shard_map/ppermute | solution.py:283
  24.9 3.7 %copy-done.1 = bf16[256,18432]{1,0:T(8,128)(2,1)S(1)} copy-done((bf16[256,18432]{1,0:T(8,128)(2,1)S(1)}, bf16[256,18432]{1,0:T(8,128)(2,1)}, u32[]{:S(2)}) %copy-start.1) | copy-done | bytes 9437208
  28.6 2.6 %logits.3 = f32[256,40]{1,0:T(8,128)S(1)} custom-call(bf16[8,18432]{1,0:T(8,128)(2,1)S(1)} %copy-done.4, bf16[8,18432]{1,0:T(8,128)(2,1)S(1)} %collective-permute-done.2.refs_1_, bf16[8,18432]{1,0:T(8,128)(2,1)S(1)} %collective-permute-done.refs_2_, bf16[8,18432]{1,0:T(8,128)(2,1)S(1)} %collective-permute-done.3.refs_3_, ...), custom_call_target="tpu_custom_call" | custom-call | flops 2415919104 | bytes 9437184 | tf_op jit(solution)/shard_map/logits/pallas_call | solution.py:108
  32.9 1.1 %collective-permute-start.7 = (bf16[8,9216]{1,0:T(8,128)(2,1)S(1)}, bf16[8,9216]{1,0:T(8,128)(2,1)S(1)}, u32[]{:S(2)}, u32[]{:S(2)}) collective-permute-start(bf16[8,9216]{1,0:T(8,128)(2,1)S(1)} %slice.43), channel_id=1, source_target_pairs={{0,4},{1,5},{4,8},{5,9},{8,12},{9,13},{12,14},{13,15},{14,10},{15,... | collective-permute-start | bytes 442376 | tf_op jit(solution)/shard_map/ppermute | solution.py:283
  34.0 2.6 %logits.4 = f32[256,16]{1,0:T(8,128)S(1)} custom-call(bf16[8,18432]{1,0:T(8,128)(2,1)S(1)} %collective-permute-done.6.refs_0_.refs_5_, bf16[8,18432]{1,0:T(8,128)(2,1)S(1)} %collective-permute-done.5.refs_1_.refs_6_, bf16[256,18432]{1,0:T(8,128)(2,1)S(1)} %copy-done.1), custom_call_target="tpu_custom_call" | custom-call | flops 2415919104 | bytes 9437184 | tf_op jit(solution)/shard_map/logits/pallas_call | solution.py:108
  38.1 2.6 %logits.5 = f32[256,8]{1,0:T(8,128)S(1)} custom-call(bf16[8,9216]{1,0:T(8,128)(2,1)S(1)} %collective-permute-done.7.refs_0_.refs_7_, bf16[8,9216]{1,0:T(8,128)(2,1)S(1)} %collective-permute-done.8.refs_1_.refs_8_, bf16[256,18432]{1,0:T(8,128)(2,1)S(1)} %copy-done.1), custom_call_target="tpu_custom_call" | custom-call | flops 2415919104 | bytes 9437184 | tf_op jit(solution)/shard_map/logits/pallas_call | solution.py:108
  41.1 1.6 %collective-permute-start.10 = (f32[1,6,64]{2,1,0:T(8,128)S(1)}, f32[1,6,64]{2,1,0:T(8,128)S(1)}, u32[]{:S(2)}, u32[]{:S(2)}) collective-permute-start(f32[1,6,64]{2,1,0:T(8,128)S(1)} %convolution_bitcast_fusion), channel_id=1, source_target_pairs={{0,2},{1,3},{4,0},{5,1},{8,4},{9,5},{12,8},{13,9},{14,12},{15,13},... | collective-permute-start | bytes 4616 | tf_op jit(solution)/shard_map/ppermute | solution.py:258
  43.2 1.6 %collective-permute-done.10 = f32[1,6,64]{2,1,0:T(8,128)S(1)} collective-permute-done((f32[1,6,64]{2,1,0:T(8,128)S(1)}, f32[1,6,64]{2,1,0:T(8,128)S(1)}, u32[]{:S(2)}, u32[]{:S(2)}) %collective-permute-start.10) | collective-permute-done | bytes 1568 | tf_op jit(solution)/shard_map/ppermute | solution.py:258
  44.8 3.1 %collective-permute-start.11 = (f32[2,6,64]{2,1,0:T(8,128)S(1)}, f32[2,6,64]{2,1,0:T(8,128)S(1)}, u32[]{:S(2)}, u32[]{:S(2)}) collective-permute-start(f32[2,6,64]{2,1,0:T(8,128)S(1)} %pad_maximum_fusion.3), channel_id=1, source_target_pairs={{0,12},{1,13},{4,14},{5,15},{8,10},{9,11},{12,6},{13,7},{14,2},{15... | collective-permute-start | bytes 9224 | tf_op jit(solution)/shard_map/ppermute | solution.py:261
  47.9 1.5 %collective-permute-start.13 = (f32[3,6,64]{2,1,0:T(8,128)S(1)}, f32[3,6,64]{2,1,0:T(8,128)S(1)}, u32[]{:S(2)}, u32[]{:S(2)}) collective-permute-start(f32[3,6,64]{2,1,0:T(8,128)S(1)} %pad_maximum_fusion.2), channel_id=1, source_target_pairs={{0,10},{1,11},{4,6},{5,7},{8,2},{9,3},{12,0},{13,1},{14,4},{15,5},... | collective-permute-start | bytes 13832 | tf_op jit(solution)/shard_map/ppermute | solution.py:258
  50.2 3.2 %collective-permute-done.13 = f32[3,6,64]{2,1,0:T(8,128)S(1)} collective-permute-done((f32[3,6,64]{2,1,0:T(8,128)S(1)}, f32[3,6,64]{2,1,0:T(8,128)S(1)}, u32[]{:S(2)}, u32[]{:S(2)}) %collective-permute-start.13) | collective-permute-done | bytes 4640 | tf_op jit(solution)/shard_map/ppermute | solution.py:258
  54.0 3.7 %copy-done.2 = bf16[256,18432]{1,0:T(8,128)(2,1)S(1)} copy-done((bf16[256,18432]{1,0:T(8,128)(2,1)S(1)}, bf16[256,18432]{1,0:T(8,128)(2,1)}, u32[]{:S(2)}) %copy-start.2) | copy-done | bytes 9437208
  57.7 1.8 %gradient_terms.1 = (f32[56,9216]{1,0:T(8,128)S(1)}, f32[56,9216]{1,0:T(8,128)S(1)}, bf16[8,9216]{1,0:T(8,128)(2,1)S(1)}, bf16[8,9216]{1,0:T(8,128)(2,1)S(1)}) custom-call(bf16[256,64]{1,0:T(8,128)(2,1)S(1)} %fusion.6.d_ref, bf16[256,18432]{1,0:T(8,128)(2,1)S(1)} %copy-done.2), custom_call_target="tpu_custom_call" | custom-call | flops 2415919104 | bytes 9437184 | tf_op jit(solution)/shard_map/gradient_terms/pallas_call | solution.py:174
  60.2 1.6 %collective-permute-start.16 = (bf16[8,9216]{1,0:T(8,128)(2,1)S(1)}, bf16[8,9216]{1,0:T(8,128)(2,1)S(1)}, u32[]{:S(2)}, u32[]{:S(2)}) collective-permute-start(bf16[8,9216]{1,0:T(8,128)(2,1)S(1)} %get-tuple-element.45), channel_id=1, source_target_pairs={{0,4},{1,5},{4,8},{5,9},{8,12},{9,13},{12,14},{13,15},{14,10},{15,... | collective-permute-start | bytes 442376 | tf_op jit(solution)/shard_map/ppermute | solution.py:283
  61.8 4.2 %collective-permute-done.23.refs_0_ = bf16[8,9216]{1,0:T(8,128)(2,1)S(1)} collective-permute-done((bf16[8,9216]{1,0:T(8,128)(2,1)S(1)}, bf16[8,9216]{1,0:T(8,128)(2,1)S(1)}, u32[]{:S(2)}, u32[]{:S(2)}) %collective-permute-start.23) | collective-permute-done | bytes 147488 | tf_op jit(solution)/shard_map/ppermute | solution.py:283
  66.0 1.5 %collective-permute-start.24 = (bf16[8,9216]{1,0:T(8,128)(2,1)S(1)}, bf16[8,9216]{1,0:T(8,128)(2,1)S(1)}, u32[]{:S(2)}, u32[]{:S(2)}) collective-permute-start(bf16[8,9216]{1,0:T(8,128)(2,1)S(1)} %get-tuple-element.64), channel_id=1, source_target_pairs={{0,4},{1,5},{4,8},{5,9},{8,12},{9,13},{12,14},{13,15},{14,10},{15,... | collective-permute-start | bytes 442376 | tf_op jit(solution)/shard_map/ppermute | solution.py:283
  68.1 1.5 %collective-permute-start.17 = (bf16[8,9216]{1,0:T(8,128)(2,1)S(1)}, bf16[8,9216]{1,0:T(8,128)(2,1)S(1)}, u32[]{:S(2)}, u32[]{:S(2)}) collective-permute-start(bf16[8,9216]{1,0:T(8,128)(2,1)S(1)} %get-tuple-element.56), channel_id=1, source_target_pairs={{0,4},{1,5},{4,8},{5,9},{8,12},{9,13},{12,14},{13,15},{14,10},{15,... | collective-permute-start | bytes 442376 | tf_op jit(solution)/shard_map/ppermute | solution.py:283
  70.2 2.6 %collective-permute-done.24.refs_0_ = bf16[8,9216]{1,0:T(8,128)(2,1)S(1)} collective-permute-done((bf16[8,9216]{1,0:T(8,128)(2,1)S(1)}, bf16[8,9216]{1,0:T(8,128)(2,1)S(1)}, u32[]{:S(2)}, u32[]{:S(2)}) %collective-permute-start.24) | collective-permute-done | bytes 147488 | tf_op jit(solution)/shard_map/ppermute | solution.py:283
  72.8 1.4 %collective-permute-done.25.refs_1_ = bf16[8,9216]{1,0:T(8,128)(2,1)S(1)} collective-permute-done((bf16[8,9216]{1,0:T(8,128)(2,1)S(1)}, bf16[8,9216]{1,0:T(8,128)(2,1)S(1)}, u32[]{:S(2)}, u32[]{:S(2)}) %collective-permute-start.25) | collective-permute-done | bytes 147488 | tf_op jit(solution)/shard_map/ppermute | solution.py:283
  75.2 1.2 %collective-permute-start.27 = (bf16[8,9216]{1,0:T(8,128)(2,1)S(1)}, bf16[8,9216]{1,0:T(8,128)(2,1)S(1)}, u32[]{:S(2)}, u32[]{:S(2)}) collective-permute-start(bf16[8,9216]{1,0:T(8,128)(2,1)S(1)} %get-tuple-element.67), channel_id=1, source_target_pairs={{0,2},{1,3},{4,0},{5,1},{8,4},{9,5},{12,8},{13,9},{14,12},{15,13},... | collective-permute-start | bytes 442376 | tf_op jit(solution)/shard_map/ppermute | solution.py:283
  77.6 2.0 %collective-permute-done.26.refs_0_ = bf16[8,9216]{1,0:T(8,128)(2,1)S(1)} collective-permute-done((bf16[8,9216]{1,0:T(8,128)(2,1)S(1)}, bf16[8,9216]{1,0:T(8,128)(2,1)S(1)}, u32[]{:S(2)}, u32[]{:S(2)}) %collective-permute-start.26) | collective-permute-done | bytes 147488 | tf_op jit(solution)/shard_map/ppermute | solution.py:283
  80.7 1.4 %collective-permute-done.27.refs_1_ = bf16[8,9216]{1,0:T(8,128)(2,1)S(1)} collective-permute-done((bf16[8,9216]{1,0:T(8,128)(2,1)S(1)}, bf16[8,9216]{1,0:T(8,128)(2,1)S(1)}, u32[]{:S(2)}, u32[]{:S(2)}) %collective-permute-start.27) | collective-permute-done | bytes 147488 | tf_op jit(solution)/shard_map/ppermute | solution.py:283
  82.2 1.7 %collective-permute-start.28 = (bf16[8,9216]{1,0:T(8,128)(2,1)S(1)}, bf16[8,9216]{1,0:T(8,128)(2,1)S(1)}, u32[]{:S(2)}, u32[]{:S(2)}) collective-permute-start(bf16[8,9216]{1,0:T(8,128)(2,1)S(1)} %get-tuple-element.68), channel_id=1, source_target_pairs={{0,4},{1,5},{4,8},{5,9},{8,12},{9,13},{12,14},{13,15},{14,10},{15,... | collective-permute-start | bytes 442376 | tf_op jit(solution)/shard_map/ppermute | solution.py:283
  84.8 1.9 %collective-permute-start.21 = (bf16[8,9216]{1,0:T(8,128)(2,1)S(1)}, bf16[8,9216]{1,0:T(8,128)(2,1)S(1)}, u32[]{:S(2)}, u32[]{:S(2)}) collective-permute-start(bf16[8,9216]{1,0:T(8,128)(2,1)S(1)} %get-tuple-element.60), channel_id=1, source_target_pairs={{0,4},{1,5},{4,8},{5,9},{8,12},{9,13},{12,14},{13,15},{14,10},{15,... | collective-permute-start | bytes 442376 | tf_op jit(solution)/shard_map/ppermute | solution.py:283
  86.9 3.1 %convolution_convert_fusion = bf16[128,18432]{1,0:T(8,128)(2,1)} fusion(bf16[64,18432]{1,0:T(8,128)(2,1)S(1)} %collective-permute-done.15, bf16[64,18432]{1,0:T(8,128)(2,1)S(1)} %assemble.1, bf16[128,64]{1,0:T(8,128)(2,1)S(1)} %collective-permute-done.14, bf16[128,64]{1,0:T(8,128)(2,1)S(1)} %get-tuple-element.81), kind=kOutput, calls=%fused_computation | convolution fusion | flops 615841792 | bytes 9469952 | tf_op jit(solution)/shard_map/dot_general | solution.py:355
  90.5 1.3 %collective-permute-done.22 = bf16[8,9216]{1,0:T(8,128)(2,1)S(1)} collective-permute-done((bf16[8,9216]{1,0:T(8,128)(2,1)S(1)}, bf16[8,9216]{1,0:T(8,128)(2,1)S(1)}, u32[]{:S(2)}, u32[]{:S(2)}) %collective-permute-start.22) | collective-permute-done | bytes 147488 | tf_op jit(solution)/shard_map/ppermute | solution.py:283
  (93 shorter events, 17.6 us)
Async XLA Ops:
  0.6 13.2 %collective-permute-start.4 = (bf16[128,18432]{1,0:T(8,128)(2,1)}, bf16[128,18432]{1,0:T(8,128)(2,1)}, u32[]{:S(2)}, u32[]{:S(2)}) collective-permute-start(bf16[128,18432]{1,0:T(8,128)(2,1)} %own_ref.1), channel_id=1, source_target_pairs={{0,1},{1,0},{2,3},{3,2},{4,5},{5,4},{6,7},{7,6},{8,9},{9,8},{10,11... | collective-permute-start | bytes 14155784 | tf_op jit(solution)/shard_map/ppermute | solution.py:283
  1.1 10.5 %collective-permute-start.2 = (bf16[8,18432]{1,0:T(8,128)(2,1)}, bf16[8,18432]{1,0:T(8,128)(2,1)S(1)}, u32[]{:S(2)}, u32[]{:S(2)}) collective-permute-start(bf16[8,18432]{1,0:T(8,128)(2,1)} %refs_0_.2), channel_id=1, source_target_pairs={{0,2},{1,3},{4,0},{5,1},{8,4},{9,5},{12,8},{13,9},{14,12},{15,13},... | collective-permute-start | bytes 884744 | tf_op jit(solution)/shard_map/ppermute | solution.py:283
  3.7 9.6 %collective-permute-start = (bf16[8,18432]{1,0:T(8,128)(2,1)}, bf16[8,18432]{1,0:T(8,128)(2,1)S(1)}, u32[]{:S(2)}, u32[]{:S(2)}) collective-permute-start(bf16[8,18432]{1,0:T(8,128)(2,1)} %refs_0_.2), channel_id=1, source_target_pairs={{0,4},{1,5},{4,8},{5,9},{8,12},{9,13},{12,14},{13,15},{14,10},{15,... | collective-permute-start | bytes 884744 | tf_op jit(solution)/shard_map/ppermute | solution.py:283
  3.9 20.6 %collective-permute-start.9 = (bf16[128,128]{1,0:T(8,128)(2,1)}, bf16[128,128]{1,0:T(8,128)(2,1)S(1)}, u32[]{:S(2)}, u32[]{:S(2)}) collective-permute-start(bf16[128,128]{1,0:T(8,128)(2,1)} %param.8), channel_id=1, source_target_pairs={{0,1},{1,0},{2,3},{3,2},{4,5},{5,4},{6,7},{7,6},{8,9},{9,8},{10,11... | collective-permute-start | bytes 98312 | tf_op jit(solution)/shard_map/ppermute | solution.py:283
  11.6 10.9 %collective-permute-start.3 = (bf16[8,18432]{1,0:T(8,128)(2,1)S(1)}, bf16[8,18432]{1,0:T(8,128)(2,1)S(1)}, u32[]{:S(2)}, u32[]{:S(2)}) collective-permute-start(bf16[8,18432]{1,0:T(8,128)(2,1)S(1)} %collective-permute-done.2.refs_1_), channel_id=1, source_target_pairs={{0,2},{1,3},{4,0},{5,1},{8,4},{9,5},{12,8},{13,9},{14,12},{15,13},... | collective-permute-start | bytes 884744 | tf_op jit(solution)/shard_map/ppermute | solution.py:283
  13.3 9.2 %collective-permute-start.1 = (bf16[8,18432]{1,0:T(8,128)(2,1)S(1)}, bf16[8,18432]{1,0:T(8,128)(2,1)S(1)}, u32[]{:S(2)}, u32[]{:S(2)}) collective-permute-start(bf16[8,18432]{1,0:T(8,128)(2,1)S(1)} %collective-permute-done.refs_2_), channel_id=1, source_target_pairs={{0,4},{1,5},{4,8},{5,9},{8,12},{9,13},{12,14},{13,15},{14,10},{15,... | collective-permute-start | bytes 884744 | tf_op jit(solution)/shard_map/ppermute | solution.py:283
  16.1 8.4 %copy-start.5 = (bf16[128,128]{1,0:T(8,128)(2,1)S(1)}, bf16[128,128]{1,0:T(8,128)(2,1)}, u32[]{:S(2)}) copy-start(bf16[128,128]{1,0:T(8,128)(2,1)} %param.8) | copy-start | bytes 98308
  16.1 8.8 %copy-start.4 = (bf16[8,18432]{1,0:T(8,128)(2,1)S(1)}, bf16[8,18432]{1,0:T(8,128)(2,1)}, u32[]{:S(2)}) copy-start(bf16[8,18432]{1,0:T(8,128)(2,1)} %refs_0_.2) | copy-start | bytes 884740
  22.5 8.7 %collective-permute-start.5 = (bf16[8,18432]{1,0:T(8,128)(2,1)S(1)}, bf16[8,18432]{1,0:T(8,128)(2,1)S(1)}, u32[]{:S(2)}, u32[]{:S(2)}) collective-permute-start(bf16[8,18432]{1,0:T(8,128)(2,1)S(1)} %collective-permute-done.1.refs_4_), channel_id=1, source_target_pairs={{0,4},{1,5},{4,8},{5,9},{8,12},{9,13},{12,14},{13,15},{14,10},{15,... | collective-permute-start | bytes 884744 | tf_op jit(solution)/shard_map/ppermute | solution.py:283
  24.2 7.7 %collective-permute-start.6 = (bf16[8,18432]{1,0:T(8,128)(2,1)S(1)}, bf16[8,18432]{1,0:T(8,128)(2,1)S(1)}, u32[]{:S(2)}, u32[]{:S(2)}) collective-permute-start(bf16[8,18432]{1,0:T(8,128)(2,1)S(1)} %collective-permute-done.3.refs_3_), channel_id=1, source_target_pairs={{0,2},{1,3},{4,0},{5,1},{8,4},{9,5},{12,8},{13,9},{14,12},{15,13},... | collective-permute-start | bytes 884744 | tf_op jit(solution)/shard_map/ppermute | solution.py:283
  32.0 5.2 %collective-permute-start.8 = (bf16[8,9216]{1,0:T(8,128)(2,1)S(1)}, bf16[8,9216]{1,0:T(8,128)(2,1)S(1)}, u32[]{:S(2)}, u32[]{:S(2)}) collective-permute-start(bf16[8,9216]{1,0:T(8,128)(2,1)S(1)} %slice.44), channel_id=1, source_target_pairs={{0,2},{1,3},{4,0},{5,1},{8,4},{9,5},{12,8},{13,9},{14,12},{15,13},... | collective-permute-start | bytes 442376 | tf_op jit(solution)/shard_map/ppermute | solution.py:283
  32.9 5.1 %collective-permute-start.7 = (bf16[8,9216]{1,0:T(8,128)(2,1)S(1)}, bf16[8,9216]{1,0:T(8,128)(2,1)S(1)}, u32[]{:S(2)}, u32[]{:S(2)}) collective-permute-start(bf16[8,9216]{1,0:T(8,128)(2,1)S(1)} %slice.43), channel_id=1, source_target_pairs={{0,4},{1,5},{4,8},{5,9},{8,12},{9,13},{12,14},{13,15},{14,10},{15,... | collective-permute-start | bytes 442376 | tf_op jit(solution)/shard_map/ppermute | solution.py:283
  41.1 3.6 %collective-permute-start.10 = (f32[1,6,64]{2,1,0:T(8,128)S(1)}, f32[1,6,64]{2,1,0:T(8,128)S(1)}, u32[]{:S(2)}, u32[]{:S(2)}) collective-permute-start(f32[1,6,64]{2,1,0:T(8,128)S(1)} %convolution_bitcast_fusion), channel_id=1, source_target_pairs={{0,2},{1,3},{4,0},{5,1},{8,4},{9,5},{12,8},{13,9},{14,12},{15,13},... | collective-permute-start | bytes 4616 | tf_op jit(solution)/shard_map/ppermute | solution.py:258
  42.7 5.2 %collective-permute-start.12 = (f32[1,6,64]{2,1,0:T(8,128)S(1)}, f32[1,6,64]{2,1,0:T(8,128)S(1)}, u32[]{:S(2)}, u32[]{:S(2)}) collective-permute-start(f32[1,6,64]{2,1,0:T(8,128)S(1)} %convolution_bitcast_fusion), channel_id=1, source_target_pairs={{0,4},{1,5},{4,8},{5,9},{8,12},{9,13},{12,14},{13,15},{14,10},{15,... | collective-permute-start | bytes 4616 | tf_op jit(solution)/shard_map/ppermute | solution.py:261
  44.8 5.4 %collective-permute-start.11 = (f32[2,6,64]{2,1,0:T(8,128)S(1)}, f32[2,6,64]{2,1,0:T(8,128)S(1)}, u32[]{:S(2)}, u32[]{:S(2)}) collective-permute-start(f32[2,6,64]{2,1,0:T(8,128)S(1)} %pad_maximum_fusion.3), channel_id=1, source_target_pairs={{0,12},{1,13},{4,14},{5,15},{8,10},{9,11},{12,6},{13,7},{14,2},{15... | collective-permute-start | bytes 9224 | tf_op jit(solution)/shard_map/ppermute | solution.py:261
  47.9 5.5 %collective-permute-start.13 = (f32[3,6,64]{2,1,0:T(8,128)S(1)}, f32[3,6,64]{2,1,0:T(8,128)S(1)}, u32[]{:S(2)}, u32[]{:S(2)}) collective-permute-start(f32[3,6,64]{2,1,0:T(8,128)S(1)} %pad_maximum_fusion.2), channel_id=1, source_target_pairs={{0,10},{1,11},{4,6},{5,7},{8,2},{9,3},{12,0},{13,1},{14,4},{15,5},... | collective-permute-start | bytes 13832 | tf_op jit(solution)/shard_map/ppermute | solution.py:258
  59.6 27.3 %collective-permute-start.15 = (bf16[64,18432]{1,0:T(8,128)(2,1)S(1)}, bf16[64,18432]{1,0:T(8,128)(2,1)S(1)}, u32[]{:S(2)}, u32[]{:S(2)}) collective-permute-start(bf16[64,18432]{1,0:T(8,128)(2,1)S(1)} %assemble.1), channel_id=1, source_target_pairs={{0,1},{1,0},{2,3},{3,2},{4,5},{5,4},{6,7},{7,6},{8,9},{9,8},{10,11... | collective-permute-start | bytes 7077896 | tf_op jit(solution)/shard_map/ppermute | solution.py:283
  59.7 6.2 %collective-permute-start.23 = (bf16[8,9216]{1,0:T(8,128)(2,1)S(1)}, bf16[8,9216]{1,0:T(8,128)(2,1)S(1)}, u32[]{:S(2)}, u32[]{:S(2)}) collective-permute-start(bf16[8,9216]{1,0:T(8,128)(2,1)S(1)} %get-tuple-element.63), channel_id=1, source_target_pairs={{0,2},{1,3},{4,0},{5,1},{8,4},{9,5},{12,8},{13,9},{14,12},{15,13},... | collective-permute-start | bytes 442376 | tf_op jit(solution)/shard_map/ppermute | solution.py:283
  60.2 7.9 %collective-permute-start.16 = (bf16[8,9216]{1,0:T(8,128)(2,1)S(1)}, bf16[8,9216]{1,0:T(8,128)(2,1)S(1)}, u32[]{:S(2)}, u32[]{:S(2)}) collective-permute-start(bf16[8,9216]{1,0:T(8,128)(2,1)S(1)} %get-tuple-element.45), channel_id=1, source_target_pairs={{0,4},{1,5},{4,8},{5,9},{8,12},{9,13},{12,14},{13,15},{14,10},{15,... | collective-permute-start | bytes 442376 | tf_op jit(solution)/shard_map/ppermute | solution.py:283
  66.0 6.8 %collective-permute-start.24 = (bf16[8,9216]{1,0:T(8,128)(2,1)S(1)}, bf16[8,9216]{1,0:T(8,128)(2,1)S(1)}, u32[]{:S(2)}, u32[]{:S(2)}) collective-permute-start(bf16[8,9216]{1,0:T(8,128)(2,1)S(1)} %get-tuple-element.64), channel_id=1, source_target_pairs={{0,4},{1,5},{4,8},{5,9},{8,12},{9,13},{12,14},{13,15},{14,10},{15,... | collective-permute-start | bytes 442376 | tf_op jit(solution)/shard_map/ppermute | solution.py:283
  67.5 6.7 %collective-permute-start.25 = (bf16[8,9216]{1,0:T(8,128)(2,1)S(1)}, bf16[8,9216]{1,0:T(8,128)(2,1)S(1)}, u32[]{:S(2)}, u32[]{:S(2)}) collective-permute-start(bf16[8,9216]{1,0:T(8,128)(2,1)S(1)} %get-tuple-element.65), channel_id=1, source_target_pairs={{0,2},{1,3},{4,0},{5,1},{8,4},{9,5},{12,8},{13,9},{14,12},{15,13},... | collective-permute-start | bytes 442376 | tf_op jit(solution)/shard_map/ppermute | solution.py:283
  68.1 7.1 %collective-permute-start.17 = (bf16[8,9216]{1,0:T(8,128)(2,1)S(1)}, bf16[8,9216]{1,0:T(8,128)(2,1)S(1)}, u32[]{:S(2)}, u32[]{:S(2)}) collective-permute-start(bf16[8,9216]{1,0:T(8,128)(2,1)S(1)} %get-tuple-element.56), channel_id=1, source_target_pairs={{0,4},{1,5},{4,8},{5,9},{8,12},{9,13},{12,14},{13,15},{14,10},{15,... | collective-permute-start | bytes 442376 | tf_op jit(solution)/shard_map/ppermute | solution.py:283
  69.7 6.8 %collective-permute-start.18 = (bf16[8,9216]{1,0:T(8,128)(2,1)S(1)}, bf16[8,9216]{1,0:T(8,128)(2,1)S(1)}, u32[]{:S(2)}, u32[]{:S(2)}) collective-permute-start(bf16[8,9216]{1,0:T(8,128)(2,1)S(1)} %get-tuple-element.57), channel_id=1, source_target_pairs={{0,2},{1,3},{4,0},{5,1},{8,4},{9,5},{12,8},{13,9},{14,12},{15,13},... | collective-permute-start | bytes 442376 | tf_op jit(solution)/shard_map/ppermute | solution.py:283
  74.3 5.3 %collective-permute-start.26 = (bf16[8,9216]{1,0:T(8,128)(2,1)S(1)}, bf16[8,9216]{1,0:T(8,128)(2,1)S(1)}, u32[]{:S(2)}, u32[]{:S(2)}) collective-permute-start(bf16[8,9216]{1,0:T(8,128)(2,1)S(1)} %get-tuple-element.66), channel_id=1, source_target_pairs={{0,4},{1,5},{4,8},{5,9},{8,12},{9,13},{12,14},{13,15},{14,10},{15,... | collective-permute-start | bytes 442376 | tf_op jit(solution)/shard_map/ppermute | solution.py:283
  74.5 12.2 %collective-permute-start.14 = (bf16[128,64]{1,0:T(8,128)(2,1)S(1)}, bf16[128,64]{1,0:T(8,128)(2,1)S(1)}, u32[]{:S(2)}, u32[]{:S(2)}) collective-permute-start(bf16[128,64]{1,0:T(8,128)(2,1)S(1)} %get-tuple-element.82), channel_id=1, source_target_pairs={{0,1},{1,0},{2,3},{3,2},{4,5},{5,4},{6,7},{7,6},{8,9},{9,8},{10,11... | collective-permute-start | bytes 49160 | tf_op jit(solution)/shard_map/ppermute | solution.py:283
  75.2 6.8 %collective-permute-start.27 = (bf16[8,9216]{1,0:T(8,128)(2,1)S(1)}, bf16[8,9216]{1,0:T(8,128)(2,1)S(1)}, u32[]{:S(2)}, u32[]{:S(2)}) collective-permute-start(bf16[8,9216]{1,0:T(8,128)(2,1)S(1)} %get-tuple-element.67), channel_id=1, source_target_pairs={{0,2},{1,3},{4,0},{5,1},{8,4},{9,5},{12,8},{13,9},{14,12},{15,13},... | collective-permute-start | bytes 442376 | tf_op jit(solution)/shard_map/ppermute | solution.py:283
  76.6 7.3 %collective-permute-start.19 = (bf16[8,9216]{1,0:T(8,128)(2,1)S(1)}, bf16[8,9216]{1,0:T(8,128)(2,1)S(1)}, u32[]{:S(2)}, u32[]{:S(2)}) collective-permute-start(bf16[8,9216]{1,0:T(8,128)(2,1)S(1)} %get-tuple-element.58), channel_id=1, source_target_pairs={{0,4},{1,5},{4,8},{5,9},{8,12},{9,13},{12,14},{13,15},{14,10},{15,... | collective-permute-start | bytes 442376 | tf_op jit(solution)/shard_map/ppermute | solution.py:283
  79.6 5.1 %collective-permute-start.20 = (bf16[8,9216]{1,0:T(8,128)(2,1)S(1)}, bf16[8,9216]{1,0:T(8,128)(2,1)S(1)}, u32[]{:S(2)}, u32[]{:S(2)}) collective-permute-start(bf16[8,9216]{1,0:T(8,128)(2,1)S(1)} %get-tuple-element.59), channel_id=1, source_target_pairs={{0,2},{1,3},{4,0},{5,1},{8,4},{9,5},{12,8},{13,9},{14,12},{15,13},... | collective-permute-start | bytes 442376 | tf_op jit(solution)/shard_map/ppermute | solution.py:283
  82.2 7.8 %collective-permute-start.28 = (bf16[8,9216]{1,0:T(8,128)(2,1)S(1)}, bf16[8,9216]{1,0:T(8,128)(2,1)S(1)}, u32[]{:S(2)}, u32[]{:S(2)}) collective-permute-start(bf16[8,9216]{1,0:T(8,128)(2,1)S(1)} %get-tuple-element.68), channel_id=1, source_target_pairs={{0,4},{1,5},{4,8},{5,9},{8,12},{9,13},{12,14},{13,15},{14,10},{15,... | collective-permute-start | bytes 442376 | tf_op jit(solution)/shard_map/ppermute | solution.py:283
  83.9 6.1 %collective-permute-start.29 = (bf16[8,9216]{1,0:T(8,128)(2,1)S(1)}, bf16[8,9216]{1,0:T(8,128)(2,1)S(1)}, u32[]{:S(2)}, u32[]{:S(2)}) collective-permute-start(bf16[8,9216]{1,0:T(8,128)(2,1)S(1)} %get-tuple-element.69), channel_id=1, source_target_pairs={{0,2},{1,3},{4,0},{5,1},{8,4},{9,5},{12,8},{13,9},{14,12},{15,13},... | collective-permute-start | bytes 442376 | tf_op jit(solution)/shard_map/ppermute | solution.py:283
  84.8 5.7 %collective-permute-start.21 = (bf16[8,9216]{1,0:T(8,128)(2,1)S(1)}, bf16[8,9216]{1,0:T(8,128)(2,1)S(1)}, u32[]{:S(2)}, u32[]{:S(2)}) collective-permute-start(bf16[8,9216]{1,0:T(8,128)(2,1)S(1)} %get-tuple-element.60), channel_id=1, source_target_pairs={{0,4},{1,5},{4,8},{5,9},{8,12},{9,13},{12,14},{13,15},{14,10},{15,... | collective-permute-start | bytes 442376 | tf_op jit(solution)/shard_map/ppermute | solution.py:283
  86.7 5.1 %collective-permute-start.22 = (bf16[8,9216]{1,0:T(8,128)(2,1)S(1)}, bf16[8,9216]{1,0:T(8,128)(2,1)S(1)}, u32[]{:S(2)}, u32[]{:S(2)}) collective-permute-start(bf16[8,9216]{1,0:T(8,128)(2,1)S(1)} %get-tuple-element.61), channel_id=1, source_target_pairs={{0,2},{1,3},{4,0},{5,1},{8,4},{9,5},{12,8},{13,9},{14,12},{15,13},... | collective-permute-start | bytes 442376 | tf_op jit(solution)/shard_map/ppermute | solution.py:283
  (4 other events, 13.3 us)

commit v3 on v2

--- a/solution.py
+++ b/solution.py
@@ -20,6 +20,12 @@
 
 def in_vmem(count):
     return [pl.BlockSpec(memory_space=pltpu.VMEM)] * count
+
+
+def cost(flops, bytes_accessed, transcendentals):
+    return pl.CostEstimate(
+        flops=10 * flops, bytes_accessed=1 * bytes_accessed, transcendentals=transcendentals
+    )
 
 
 def kernel_params():
@@ -46,7 +52,7 @@
         out_specs=in_vmem(1)[0],
         scratch_shapes=[pltpu.SemaphoreType.DMA((2,))],
         compiler_params=kernel_params(),
-        cost_estimate=pl.CostEstimate(
+        cost_estimate=cost(
             flops=0, bytes_accessed=8 * ids * width, transcendentals=0
         ),
         name="stack_heads",
@@ -111,7 +117,7 @@
         in_specs=in_vmem(len(flat) + 1),
         out_specs=in_vmem(1)[0],
         compiler_params=kernel_params(),
-        cost_estimate=pl.CostEstimate(
+        cost_estimate=cost(
             flops=2 * ids * max(rows, 256) * width,
             bytes_accessed=2 * ids * width,
             transcendentals=0,
@@ -144,7 +150,7 @@
         in_specs=in_vmem(len(flat)),
         out_specs=in_vmem(1)[0],
         compiler_params=kernel_params(),
-        cost_estimate=pl.CostEstimate(
+        cost_estimate=cost(
             flops=0, bytes_accessed=4 * rows * width, transcendentals=0
         ),
         name="assemble",
@@ -177,7 +183,7 @@
         in_specs=in_vmem(2),
         out_specs=in_vmem(4),
         compiler_params=kernel_params(),
-        cost_estimate=pl.CostEstimate(
+        cost_estimate=cost(
             flops=2 * ids * 256 * 2 * half, bytes_accessed=4 * ids * half, transcendentals=0
         ),
         name="gradient_terms",
@@ -207,7 +213,7 @@
         in_specs=in_vmem(1 + len(given)),
         out_specs=in_vmem(2),
         compiler_params=kernel_params(),
-        cost_estimate=pl.CostEstimate(
+        cost_estimate=cost(
             flops=2 * tokens * half, bytes_accessed=4 * tokens * half, transcendentals=0
         ),
         name="ring_sums",

time: 92.9 us -> 90.7 us (0.976)
  local copies, waits for them, and re-layouts: 13.7 us -> 6.36 us
  waiting for transfers between devices: 27.7 us -> 32.2 us
    unnamed x16 -> x12, local copies, waits for them, and re-layouts: 13.3 us -> 6.02 us
    ppermute x26, waiting for transfers between devices: 22.1 us -> 26.6 us  [send(): return lax.ppermute(x, 'pipe', perm)]
  transfers between devices with their start and end apart: 30 -> 30, of which waited for: 16 -> 19; matrix products, arithmetic and copies ran while one was open for 7% -> 8% of each run, Pallas kernels for 9% -> 9%
where the time goes in v3:
time: 90.7 us; the launch traced here: 90.4 us
  waiting for transfers between devices  32.2 us (36%)
  starting transfers between devices  29.3 us (32%)
  Pallas kernels  12.7 us (14%)
  local copies, waits for them, and re-layouts  6.36 us (7%)
  matrix products  4.51 us (5%)
  other arithmetic  4.42 us (5%)
    ppermute x26, waiting for transfers between devices, send(): return lax.ppermute(x, 'pipe', perm)  26.6 us
    ppermute x26, starting transfers between devices, send(): return lax.ppermute(x, 'pipe', perm)  22.9 us
    pallas_call x3, Pallas kernels, logits(): pl.pallas_call(body, out_shape=jax.ShapeDtypeStruct((ids, rows), F32), in...  7.69 us
    unnamed x12, local copies, waits for them, and re-layouts  6.02 us
    ppermute x2, waiting for transfers between devices, from_every_chip(): ahead = lax.ppermute(known[:right], 'pipe', shift_pairs(ring, -width))  4.53 us
    ppermute x2, starting transfers between devices, from_every_chip(): lax.ppermute(known[width - left:], 'pipe', shift_pairs(ring, width))  3.31 us
    ppermute x2, starting transfers between devices, from_every_chip(): ahead = lax.ppermute(known[:right], 'pipe', shift_pairs(ring, -width))  3.08 us
    dot_general x1, matrix products, program(): lax.dot_general(jnp.concatenate([dlogit[:ids], sib_dlogit], axis=1), jnp....  3.07 us
  transfers between devices with their start and end apart: 30, of which 19 were waited for; matrix products, arithmetic and copies ran while one was open for 8% of the time, Pallas kernels for 9%

profile of v3, /device:TPU:0, one launch (start us, length us, event | category | flops | bytes accessed | tf_op | source)
XLA Modules:
  0.0 90.4 jit_solution(7585720304781244914)
XLA Ops:
  1.1 2.6 %collective-permute-start.2 = (bf16[8,18432]{1,0:T(8,128)(2,1)}, bf16[8,18432]{1,0:T(8,128)(2,1)S(1)}, u32[]{:S(2)}, u32[]{:S(2)}) collective-permute-start(bf16[8,18432]{1,0:T(8,128)(2,1)} %refs_0_.2), channel_id=1, source_target_pairs={{0,2},{1,3},{4,0},{5,1},{8,4},{9,5},{12,8},{13,9},{14,12},{15,13},... | collective-permute-start | bytes 884744 | tf_op jit(solution)/shard_map/ppermute | solution.py:289
  6.6 5.1 %collective-permute-done.2.refs_1_ = bf16[8,18432]{1,0:T(8,128)(2,1)S(1)} collective-permute-done((bf16[8,18432]{1,0:T(8,128)(2,1)}, bf16[8,18432]{1,0:T(8,128)(2,1)S(1)}, u32[]{:S(2)}, u32[]{:S(2)}) %collective-permute-start.2) | collective-permute-done | bytes 294944 | tf_op jit(solution)/shard_map/ppermute | solution.py:289
  11.6 1.7 %collective-permute-start.3 = (bf16[8,18432]{1,0:T(8,128)(2,1)S(1)}, bf16[8,18432]{1,0:T(8,128)(2,1)S(1)}, u32[]{:S(2)}, u32[]{:S(2)}) collective-permute-start(bf16[8,18432]{1,0:T(8,128)(2,1)S(1)} %collective-permute-done.2.refs_1_), channel_id=1, source_target_pairs={{0,2},{1,3},{4,0},{5,1},{8,4},{9,5},{12,8},{13,9},{14,12},{15,13},... | collective-permute-start | bytes 884744 | tf_op jit(solution)/shard_map/ppermute | solution.py:289
  14.9 2.3 %copy-done.2 = bf16[128,18432]{1,0:T(8,128)(2,1)S(1)} copy-done((bf16[128,18432]{1,0:T(8,128)(2,1)S(1)}, bf16[128,18432]{1,0:T(8,128)(2,1)}, u32[]{:S(2)}) %copy-start.2) | copy-done | bytes 4718616
  17.2 2.7 %stack_heads.1.refs_5_.refs_2_.heads_ref = bf16[256,18432]{1,0:T(8,128)(2,1)S(1)} custom-call(bf16[128,18432]{1,0:T(8,128)(2,1)S(1)} %copy-done.2, bf16[128,18432]{1,0:T(8,128)(2,1)} %collective-permute-done.4.sib_ref), custom_call_target="tpu_custom_call" | custom-call | bytes 18874368 | tf_op jit(solution)/shard_map/stack_heads/pallas_call | solution.py:48
  22.1 1.4 %collective-permute-start.6 = (bf16[8,18432]{1,0:T(8,128)(2,1)S(1)}, bf16[8,18432]{1,0:T(8,128)(2,1)S(1)}, u32[]{:S(2)}, u32[]{:S(2)}) collective-permute-start(bf16[8,18432]{1,0:T(8,128)(2,1)S(1)} %collective-permute-done.3.refs_3_), channel_id=1, source_target_pairs={{0,2},{1,3},{4,0},{5,1},{8,4},{9,5},{12,8},{13,9},{14,12},{15,13},... | collective-permute-start | bytes 884744 | tf_op jit(solution)/shard_map/ppermute | solution.py:289
  23.6 2.6 %logits.3 = f32[256,40]{1,0:T(8,128)S(1)} custom-call(bf16[8,18432]{1,0:T(8,128)(2,1)S(1)} %copy-done.3, bf16[8,18432]{1,0:T(8,128)(2,1)S(1)} %collective-permute-done.2.refs_1_, bf16[8,18432]{1,0:T(8,128)(2,1)S(1)} %collective-permute-done.refs_2_, bf16[8,18432]{1,0:T(8,128)(2,1)S(1)} %collective-permute-done.3.refs_3_, ...), custom_call_target="tpu_custom_call" | custom-call | flops 24159191040 | bytes 9437184 | tf_op jit(solution)/shard_map/logits/pallas_call | solution.py:114
  26.2 2.8 %collective-permute-done.5.refs_1_.refs_6_ = bf16[8,18432]{1,0:T(8,128)(2,1)S(1)} collective-permute-done((bf16[8,18432]{1,0:T(8,128)(2,1)S(1)}, bf16[8,18432]{1,0:T(8,128)(2,1)S(1)}, u32[]{:S(2)}, u32[]{:S(2)}) %collective-permute-start.5) | collective-permute-done | bytes 294944 | tf_op jit(solution)/shard_map/ppermute | solution.py:289
  29.5 1.2 %collective-permute-start.8 = (bf16[8,9216]{1,0:T(8,128)(2,1)S(1)}, bf16[8,9216]{1,0:T(8,128)(2,1)S(1)}, u32[]{:S(2)}, u32[]{:S(2)}) collective-permute-start(bf16[8,9216]{1,0:T(8,128)(2,1)S(1)} %slice.44), channel_id=1, source_target_pairs={{0,2},{1,3},{4,0},{5,1},{8,4},{9,5},{12,8},{13,9},{14,12},{15,13},... | collective-permute-start | bytes 442376 | tf_op jit(solution)/shard_map/ppermute | solution.py:289
  31.6 2.6 %logits.4 = f32[256,16]{1,0:T(8,128)S(1)} custom-call(bf16[8,18432]{1,0:T(8,128)(2,1)S(1)} %collective-permute-done.6.refs_0_.refs_5_, bf16[8,18432]{1,0:T(8,128)(2,1)S(1)} %collective-permute-done.5.refs_1_.refs_6_, bf16[256,18432]{1,0:T(8,128)(2,1)S(1)} %stack_heads.1.refs_5_.refs_2_.heads_ref), custom_call_target="tpu_custom_call" | custom-call | flops 24159191040 | bytes 9437184 | tf_op jit(solution)/shard_map/logits/pallas_call | solution.py:114
  34.7 1.2 %collective-permute-done.7.refs_0_.refs_7_ = bf16[8,9216]{1,0:T(8,128)(2,1)S(1)} collective-permute-done((bf16[8,9216]{1,0:T(8,128)(2,1)S(1)}, bf16[8,9216]{1,0:T(8,128)(2,1)S(1)}, u32[]{:S(2)}, u32[]{:S(2)}) %collective-permute-start.7) | collective-permute-done | bytes 147488 | tf_op jit(solution)/shard_map/ppermute | solution.py:289
  35.9 2.6 %logits.5 = f32[256,8]{1,0:T(8,128)S(1)} custom-call(bf16[8,9216]{1,0:T(8,128)(2,1)S(1)} %collective-permute-done.7.refs_0_.refs_7_, bf16[8,9216]{1,0:T(8,128)(2,1)S(1)} %collective-permute-done.8.refs_1_.refs_8_, bf16[256,18432]{1,0:T(8,128)(2,1)S(1)} %stack_heads.1.refs_5_.refs_2_.heads_ref), custom_call_target="tpu_custom_call" | custom-call | flops 24159191040 | bytes 9437184 | tf_op jit(solution)/shard_map/logits/pallas_call | solution.py:114
  39.0 1.6 %collective-permute-start.10 = (f32[1,6,64]{2,1,0:T(8,128)S(1)}, f32[1,6,64]{2,1,0:T(8,128)S(1)}, u32[]{:S(2)}, u32[]{:S(2)}) collective-permute-start(f32[1,6,64]{2,1,0:T(8,128)S(1)} %convolution_bitcast_fusion), channel_id=1, source_target_pairs={{0,2},{1,3},{4,0},{5,1},{8,4},{9,5},{12,8},{13,9},{14,12},{15,13},... | collective-permute-start | bytes 4616 | tf_op jit(solution)/shard_map/ppermute | solution.py:264
  41.0 1.6 %collective-permute-done.10 = f32[1,6,64]{2,1,0:T(8,128)S(1)} collective-permute-done((f32[1,6,64]{2,1,0:T(8,128)S(1)}, f32[1,6,64]{2,1,0:T(8,128)S(1)}, u32[]{:S(2)}, u32[]{:S(2)}) %collective-permute-start.10) | collective-permute-done | bytes 1568 | tf_op jit(solution)/shard_map/ppermute | solution.py:264
  42.6 2.9 %collective-permute-start.11 = (f32[2,6,64]{2,1,0:T(8,128)S(1)}, f32[2,6,64]{2,1,0:T(8,128)S(1)}, u32[]{:S(2)}, u32[]{:S(2)}) collective-permute-start(f32[2,6,64]{2,1,0:T(8,128)S(1)} %pad_maximum_fusion.3), channel_id=1, source_target_pairs={{0,12},{1,13},{4,14},{5,15},{8,10},{9,11},{12,6},{13,7},{14,2},{15... | collective-permute-start | bytes 9224 | tf_op jit(solution)/shard_map/ppermute | solution.py:267
  45.5 1.5 %collective-permute-start.13 = (f32[3,6,64]{2,1,0:T(8,128)S(1)}, f32[3,6,64]{2,1,0:T(8,128)S(1)}, u32[]{:S(2)}, u32[]{:S(2)}) collective-permute-start(f32[3,6,64]{2,1,0:T(8,128)S(1)} %pad_maximum_fusion.2), channel_id=1, source_target_pairs={{0,10},{1,11},{4,6},{5,7},{8,2},{9,3},{12,0},{13,1},{14,4},{15,5},... | collective-permute-start | bytes 13832 | tf_op jit(solution)/shard_map/ppermute | solution.py:264
  48.0 3.0 %collective-permute-done.13 = f32[3,6,64]{2,1,0:T(8,128)S(1)} collective-permute-done((f32[3,6,64]{2,1,0:T(8,128)S(1)}, f32[3,6,64]{2,1,0:T(8,128)S(1)}, u32[]{:S(2)}, u32[]{:S(2)}) %collective-permute-start.13) | collective-permute-done | bytes 4640 | tf_op jit(solution)/shard_map/ppermute | solution.py:264
  51.5 3.7 %copy-done.1 = bf16[256,18432]{1,0:T(8,128)(2,1)S(1)} copy-done((bf16[256,18432]{1,0:T(8,128)(2,1)S(1)}, bf16[256,18432]{1,0:T(8,128)(2,1)}, u32[]{:S(2)}) %copy-start.1) | copy-done | bytes 9437208
  55.2 1.8 %gradient_terms.1 = (f32[56,9216]{1,0:T(8,128)S(1)}, f32[56,9216]{1,0:T(8,128)S(1)}, bf16[8,9216]{1,0:T(8,128)(2,1)S(1)}, bf16[8,9216]{1,0:T(8,128)(2,1)S(1)}) custom-call(bf16[256,64]{1,0:T(8,128)(2,1)S(1)} %fusion.6.d_ref, bf16[256,18432]{1,0:T(8,128)(2,1)S(1)} %copy-done.1), custom_call_target="tpu_custom_call" | custom-call | flops 24159191040 | bytes 9437184 | tf_op jit(solution)/shard_map/gradient_terms/pallas_call | solution.py:180
  57.7 1.6 %collective-permute-start.16 = (bf16[8,9216]{1,0:T(8,128)(2,1)S(1)}, bf16[8,9216]{1,0:T(8,128)(2,1)S(1)}, u32[]{:S(2)}, u32[]{:S(2)}) collective-permute-start(bf16[8,9216]{1,0:T(8,128)(2,1)S(1)} %get-tuple-element.45), channel_id=1, source_target_pairs={{0,4},{1,5},{4,8},{5,9},{8,12},{9,13},{12,14},{13,15},{14,10},{15,... | collective-permute-start | bytes 442376 | tf_op jit(solution)/shard_map/ppermute | solution.py:289
  59.3 4.2 %collective-permute-done.23.refs_0_ = bf16[8,9216]{1,0:T(8,128)(2,1)S(1)} collective-permute-done((bf16[8,9216]{1,0:T(8,128)(2,1)S(1)}, bf16[8,9216]{1,0:T(8,128)(2,1)S(1)}, u32[]{:S(2)}, u32[]{:S(2)}) %collective-permute-start.23) | collective-permute-done | bytes 147488 | tf_op jit(solution)/shard_map/ppermute | solution.py:289
  63.5 1.5 %collective-permute-start.24 = (bf16[8,9216]{1,0:T(8,128)(2,1)S(1)}, bf16[8,9216]{1,0:T(8,128)(2,1)S(1)}, u32[]{:S(2)}, u32[]{:S(2)}) collective-permute-start(bf16[8,9216]{1,0:T(8,128)(2,1)S(1)} %get-tuple-element.64), channel_id=1, source_target_pairs={{0,4},{1,5},{4,8},{5,9},{8,12},{9,13},{12,14},{13,15},{14,10},{15,... | collective-permute-start | bytes 442376 | tf_op jit(solution)/shard_map/ppermute | solution.py:289
  65.7 1.5 %collective-permute-start.17 = (bf16[8,9216]{1,0:T(8,128)(2,1)S(1)}, bf16[8,9216]{1,0:T(8,128)(2,1)S(1)}, u32[]{:S(2)}, u32[]{:S(2)}) collective-permute-start(bf16[8,9216]{1,0:T(8,128)(2,1)S(1)} %get-tuple-element.56), channel_id=1, source_target_pairs={{0,4},{1,5},{4,8},{5,9},{8,12},{9,13},{12,14},{13,15},{14,10},{15,... | collective-permute-start | bytes 442376 | tf_op jit(solution)/shard_map/ppermute | solution.py:289
  67.8 2.6 %collective-permute-done.24.refs_0_ = bf16[8,9216]{1,0:T(8,128)(2,1)S(1)} collective-permute-done((bf16[8,9216]{1,0:T(8,128)(2,1)S(1)}, bf16[8,9216]{1,0:T(8,128)(2,1)S(1)}, u32[]{:S(2)}, u32[]{:S(2)}) %collective-permute-start.24) | collective-permute-done | bytes 147488 | tf_op jit(solution)/shard_map/ppermute | solution.py:289
  70.3 1.4 %collective-permute-done.25.refs_1_ = bf16[8,9216]{1,0:T(8,128)(2,1)S(1)} collective-permute-done((bf16[8,9216]{1,0:T(8,128)(2,1)S(1)}, bf16[8,9216]{1,0:T(8,128)(2,1)S(1)}, u32[]{:S(2)}, u32[]{:S(2)}) %collective-permute-start.25) | collective-permute-done | bytes 147488 | tf_op jit(solution)/shard_map/ppermute | solution.py:289
  72.8 1.3 %collective-permute-start.27 = (bf16[8,9216]{1,0:T(8,128)(2,1)S(1)}, bf16[8,9216]{1,0:T(8,128)(2,1)S(1)}, u32[]{:S(2)}, u32[]{:S(2)}) collective-permute-start(bf16[8,9216]{1,0:T(8,128)(2,1)S(1)} %get-tuple-element.67), channel_id=1, source_target_pairs={{0,2},{1,3},{4,0},{5,1},{8,4},{9,5},{12,8},{13,9},{14,12},{15,13},... | collective-permute-start | bytes 442376 | tf_op jit(solution)/shard_map/ppermute | solution.py:289
  75.1 2.0 %collective-permute-done.26.refs_0_ = bf16[8,9216]{1,0:T(8,128)(2,1)S(1)} collective-permute-done((bf16[8,9216]{1,0:T(8,128)(2,1)S(1)}, bf16[8,9216]{1,0:T(8,128)(2,1)S(1)}, u32[]{:S(2)}, u32[]{:S(2)}) %collective-permute-start.26) | collective-permute-done | bytes 147488 | tf_op jit(solution)/shard_map/ppermute | solution.py:289
  78.2 1.4 %collective-permute-done.27.refs_1_ = bf16[8,9216]{1,0:T(8,128)(2,1)S(1)} collective-permute-done((bf16[8,9216]{1,0:T(8,128)(2,1)S(1)}, bf16[8,9216]{1,0:T(8,128)(2,1)S(1)}, u32[]{:S(2)}, u32[]{:S(2)}) %collective-permute-start.27) | collective-permute-done | bytes 147488 | tf_op jit(solution)/shard_map/ppermute | solution.py:289
  79.7 2.0 %collective-permute-start.28 = (bf16[8,9216]{1,0:T(8,128)(2,1)S(1)}, bf16[8,9216]{1,0:T(8,128)(2,1)S(1)}, u32[]{:S(2)}, u32[]{:S(2)}) collective-permute-start(bf16[8,9216]{1,0:T(8,128)(2,1)S(1)} %get-tuple-element.68), channel_id=1, source_target_pairs={{0,4},{1,5},{4,8},{5,9},{8,12},{9,13},{12,14},{13,15},{14,10},{15,... | collective-permute-start | bytes 442376 | tf_op jit(solution)/shard_map/ppermute | solution.py:289
  82.4 2.1 %collective-permute-start.21 = (bf16[8,9216]{1,0:T(8,128)(2,1)S(1)}, bf16[8,9216]{1,0:T(8,128)(2,1)S(1)}, u32[]{:S(2)}, u32[]{:S(2)}) collective-permute-start(bf16[8,9216]{1,0:T(8,128)(2,1)S(1)} %get-tuple-element.60), channel_id=1, source_target_pairs={{0,4},{1,5},{4,8},{5,9},{8,12},{9,13},{12,14},{13,15},{14,10},{15,... | collective-permute-start | bytes 442376 | tf_op jit(solution)/shard_map/ppermute | solution.py:289
  84.5 3.1 %convolution_convert_fusion = bf16[128,18432]{1,0:T(8,128)(2,1)} fusion(bf16[64,18432]{1,0:T(8,128)(2,1)S(1)} %collective-permute-done.15, bf16[64,18432]{1,0:T(8,128)(2,1)S(1)} %assemble.1, bf16[128,64]{1,0:T(8,128)(2,1)S(1)} %collective-permute-done.14, bf16[128,64]{1,0:T(8,128)(2,1)S(1)} %get-tuple-element.81), kind=kOutput, calls=%fused_computation | convolution fusion | flops 615841792 | bytes 9469952 | tf_op jit(solution)/shard_map/dot_general | solution.py:361
  88.1 1.5 %collective-permute-done.22 = bf16[8,9216]{1,0:T(8,128)(2,1)S(1)} collective-permute-done((bf16[8,9216]{1,0:T(8,128)(2,1)S(1)}, bf16[8,9216]{1,0:T(8,128)(2,1)S(1)}, u32[]{:S(2)}, u32[]{:S(2)}) %collective-permute-start.22) | collective-permute-done | bytes 147488 | tf_op jit(solution)/shard_map/ppermute | solution.py:289
  (89 shorter events, 18.8 us)
Async XLA Ops:
  0.6 14.3 %collective-permute-start.4 = (bf16[128,18432]{1,0:T(8,128)(2,1)}, bf16[128,18432]{1,0:T(8,128)(2,1)}, u32[]{:S(2)}, u32[]{:S(2)}) collective-permute-start(bf16[128,18432]{1,0:T(8,128)(2,1)} %own_ref.1), channel_id=1, source_target_pairs={{0,1},{1,0},{2,3},{3,2},{4,5},{5,4},{6,7},{7,6},{8,9},{9,8},{10,11... | collective-permute-start | bytes 14155784 | tf_op jit(solution)/shard_map/ppermute | solution.py:289
  1.1 10.5 %collective-permute-start.2 = (bf16[8,18432]{1,0:T(8,128)(2,1)}, bf16[8,18432]{1,0:T(8,128)(2,1)S(1)}, u32[]{:S(2)}, u32[]{:S(2)}) collective-permute-start(bf16[8,18432]{1,0:T(8,128)(2,1)} %refs_0_.2), channel_id=1, source_target_pairs={{0,2},{1,3},{4,0},{5,1},{8,4},{9,5},{12,8},{13,9},{14,12},{15,13},... | collective-permute-start | bytes 884744 | tf_op jit(solution)/shard_map/ppermute | solution.py:289
  3.7 9.6 %collective-permute-start = (bf16[8,18432]{1,0:T(8,128)(2,1)}, bf16[8,18432]{1,0:T(8,128)(2,1)S(1)}, u32[]{:S(2)}, u32[]{:S(2)}) collective-permute-start(bf16[8,18432]{1,0:T(8,128)(2,1)} %refs_0_.2), channel_id=1, source_target_pairs={{0,4},{1,5},{4,8},{5,9},{8,12},{9,13},{12,14},{13,15},{14,10},{15,... | collective-permute-start | bytes 884744 | tf_op jit(solution)/shard_map/ppermute | solution.py:289
  3.9 9.9 %collective-permute-start.9 = (bf16[128,128]{1,0:T(8,128)(2,1)}, bf16[128,128]{1,0:T(8,128)(2,1)S(1)}, u32[]{:S(2)}, u32[]{:S(2)}) collective-permute-start(bf16[128,128]{1,0:T(8,128)(2,1)} %param.8), channel_id=1, source_target_pairs={{0,1},{1,0},{2,3},{3,2},{4,5},{5,4},{6,7},{7,6},{8,9},{9,8},{10,11... | collective-permute-start | bytes 98312 | tf_op jit(solution)/shard_map/ppermute | solution.py:289
  11.6 8.8 %collective-permute-start.3 = (bf16[8,18432]{1,0:T(8,128)(2,1)S(1)}, bf16[8,18432]{1,0:T(8,128)(2,1)S(1)}, u32[]{:S(2)}, u32[]{:S(2)}) collective-permute-start(bf16[8,18432]{1,0:T(8,128)(2,1)S(1)} %collective-permute-done.2.refs_1_), channel_id=1, source_target_pairs={{0,2},{1,3},{4,0},{5,1},{8,4},{9,5},{12,8},{13,9},{14,12},{15,13},... | collective-permute-start | bytes 884744 | tf_op jit(solution)/shard_map/ppermute | solution.py:289
  13.3 8.3 %collective-permute-start.1 = (bf16[8,18432]{1,0:T(8,128)(2,1)S(1)}, bf16[8,18432]{1,0:T(8,128)(2,1)S(1)}, u32[]{:S(2)}, u32[]{:S(2)}) collective-permute-start(bf16[8,18432]{1,0:T(8,128)(2,1)S(1)} %collective-permute-done.refs_2_), channel_id=1, source_target_pairs={{0,4},{1,5},{4,8},{5,9},{8,12},{9,13},{12,14},{13,15},{14,10},{15,... | collective-permute-start | bytes 884744 | tf_op jit(solution)/shard_map/ppermute | solution.py:289
  17.2 6.3 %copy-start.3 = (bf16[8,18432]{1,0:T(8,128)(2,1)S(1)}, bf16[8,18432]{1,0:T(8,128)(2,1)}, u32[]{:S(2)}) copy-start(bf16[8,18432]{1,0:T(8,128)(2,1)} %refs_0_.2) | copy-start | bytes 884740
  19.9 16.0 %copy-start = (bf16[256,18432]{1,0:T(8,128)(2,1)}, bf16[256,18432]{1,0:T(8,128)(2,1)S(1)}, u32[]{:S(2)}) copy-start(bf16[256,18432]{1,0:T(8,128)(2,1)S(1)} %stack_heads.1.refs_5_.refs_2_.heads_ref) | copy-start | bytes 28311556
  21.6 7.4 %collective-permute-start.5 = (bf16[8,18432]{1,0:T(8,128)(2,1)S(1)}, bf16[8,18432]{1,0:T(8,128)(2,1)S(1)}, u32[]{:S(2)}, u32[]{:S(2)}) collective-permute-start(bf16[8,18432]{1,0:T(8,128)(2,1)S(1)} %collective-permute-done.1.refs_4_), channel_id=1, source_target_pairs={{0,4},{1,5},{4,8},{5,9},{8,12},{9,13},{12,14},{13,15},{14,10},{15,... | collective-permute-start | bytes 884744 | tf_op jit(solution)/shard_map/ppermute | solution.py:289
  22.1 7.3 %collective-permute-start.6 = (bf16[8,18432]{1,0:T(8,128)(2,1)S(1)}, bf16[8,18432]{1,0:T(8,128)(2,1)S(1)}, u32[]{:S(2)}, u32[]{:S(2)}) collective-permute-start(bf16[8,18432]{1,0:T(8,128)(2,1)S(1)} %collective-permute-done.3.refs_3_), channel_id=1, source_target_pairs={{0,2},{1,3},{4,0},{5,1},{8,4},{9,5},{12,8},{13,9},{14,12},{15,13},... | collective-permute-start | bytes 884744 | tf_op jit(solution)/shard_map/ppermute | solution.py:289
  29.5 5.2 %collective-permute-start.8 = (bf16[8,9216]{1,0:T(8,128)(2,1)S(1)}, bf16[8,9216]{1,0:T(8,128)(2,1)S(1)}, u32[]{:S(2)}, u32[]{:S(2)}) collective-permute-start(bf16[8,9216]{1,0:T(8,128)(2,1)S(1)} %slice.44), channel_id=1, source_target_pairs={{0,2},{1,3},{4,0},{5,1},{8,4},{9,5},{12,8},{13,9},{14,12},{15,13},... | collective-permute-start | bytes 442376 | tf_op jit(solution)/shard_map/ppermute | solution.py:289
  30.7 5.1 %collective-permute-start.7 = (bf16[8,9216]{1,0:T(8,128)(2,1)S(1)}, bf16[8,9216]{1,0:T(8,128)(2,1)S(1)}, u32[]{:S(2)}, u32[]{:S(2)}) collective-permute-start(bf16[8,9216]{1,0:T(8,128)(2,1)S(1)} %slice.43), channel_id=1, source_target_pairs={{0,4},{1,5},{4,8},{5,9},{8,12},{9,13},{12,14},{13,15},{14,10},{15,... | collective-permute-start | bytes 442376 | tf_op jit(solution)/shard_map/ppermute | solution.py:289
  39.0 3.6 %collective-permute-start.10 = (f32[1,6,64]{2,1,0:T(8,128)S(1)}, f32[1,6,64]{2,1,0:T(8,128)S(1)}, u32[]{:S(2)}, u32[]{:S(2)}) collective-permute-start(f32[1,6,64]{2,1,0:T(8,128)S(1)} %convolution_bitcast_fusion), channel_id=1, source_target_pairs={{0,2},{1,3},{4,0},{5,1},{8,4},{9,5},{12,8},{13,9},{14,12},{15,13},... | collective-permute-start | bytes 4616 | tf_op jit(solution)/shard_map/ppermute | solution.py:264
  40.6 4.9 %collective-permute-start.12 = (f32[1,6,64]{2,1,0:T(8,128)S(1)}, f32[1,6,64]{2,1,0:T(8,128)S(1)}, u32[]{:S(2)}, u32[]{:S(2)}) collective-permute-start(f32[1,6,64]{2,1,0:T(8,128)S(1)} %convolution_bitcast_fusion), channel_id=1, source_target_pairs={{0,4},{1,5},{4,8},{5,9},{8,12},{9,13},{12,14},{13,15},{14,10},{15,... | collective-permute-start | bytes 4616 | tf_op jit(solution)/shard_map/ppermute | solution.py:267
  42.6 5.4 %collective-permute-start.11 = (f32[2,6,64]{2,1,0:T(8,128)S(1)}, f32[2,6,64]{2,1,0:T(8,128)S(1)}, u32[]{:S(2)}, u32[]{:S(2)}) collective-permute-start(f32[2,6,64]{2,1,0:T(8,128)S(1)} %pad_maximum_fusion.3), channel_id=1, source_target_pairs={{0,12},{1,13},{4,14},{5,15},{8,10},{9,11},{12,6},{13,7},{14,2},{15... | collective-permute-start | bytes 9224 | tf_op jit(solution)/shard_map/ppermute | solution.py:267
  45.5 5.5 %collective-permute-start.13 = (f32[3,6,64]{2,1,0:T(8,128)S(1)}, f32[3,6,64]{2,1,0:T(8,128)S(1)}, u32[]{:S(2)}, u32[]{:S(2)}) collective-permute-start(f32[3,6,64]{2,1,0:T(8,128)S(1)} %pad_maximum_fusion.2), channel_id=1, source_target_pairs={{0,10},{1,11},{4,6},{5,7},{8,2},{9,3},{12,0},{13,1},{14,4},{15,5},... | collective-permute-start | bytes 13832 | tf_op jit(solution)/shard_map/ppermute | solution.py:264
  57.1 27.3 %collective-permute-start.15 = (bf16[64,18432]{1,0:T(8,128)(2,1)S(1)}, bf16[64,18432]{1,0:T(8,128)(2,1)S(1)}, u32[]{:S(2)}, u32[]{:S(2)}) collective-permute-start(bf16[64,18432]{1,0:T(8,128)(2,1)S(1)} %assemble.1), channel_id=1, source_target_pairs={{0,1},{1,0},{2,3},{3,2},{4,5},{5,4},{6,7},{7,6},{8,9},{9,8},{10,11... | collective-permute-start | bytes 7077896 | tf_op jit(solution)/shard_map/ppermute | solution.py:289
  57.2 6.2 %collective-permute-start.23 = (bf16[8,9216]{1,0:T(8,128)(2,1)S(1)}, bf16[8,9216]{1,0:T(8,128)(2,1)S(1)}, u32[]{:S(2)}, u32[]{:S(2)}) collective-permute-start(bf16[8,9216]{1,0:T(8,128)(2,1)S(1)} %get-tuple-element.63), channel_id=1, source_target_pairs={{0,2},{1,3},{4,0},{5,1},{8,4},{9,5},{12,8},{13,9},{14,12},{15,13},... | collective-permute-start | bytes 442376 | tf_op jit(solution)/shard_map/ppermute | solution.py:289
  57.7 7.9 %collective-permute-start.16 = (bf16[8,9216]{1,0:T(8,128)(2,1)S(1)}, bf16[8,9216]{1,0:T(8,128)(2,1)S(1)}, u32[]{:S(2)}, u32[]{:S(2)}) collective-permute-start(bf16[8,9216]{1,0:T(8,128)(2,1)S(1)} %get-tuple-element.45), channel_id=1, source_target_pairs={{0,4},{1,5},{4,8},{5,9},{8,12},{9,13},{12,14},{13,15},{14,10},{15,... | collective-permute-start | bytes 442376 | tf_op jit(solution)/shard_map/ppermute | solution.py:289
  63.5 6.8 %collective-permute-start.24 = (bf16[8,9216]{1,0:T(8,128)(2,1)S(1)}, bf16[8,9216]{1,0:T(8,128)(2,1)S(1)}, u32[]{:S(2)}, u32[]{:S(2)}) collective-permute-start(bf16[8,9216]{1,0:T(8,128)(2,1)S(1)} %get-tuple-element.64), channel_id=1, source_target_pairs={{0,4},{1,5},{4,8},{5,9},{8,12},{9,13},{12,14},{13,15},{14,10},{15,... | collective-permute-start | bytes 442376 | tf_op jit(solution)/shard_map/ppermute | solution.py:289
  65.1 6.7 %collective-permute-start.25 = (bf16[8,9216]{1,0:T(8,128)(2,1)S(1)}, bf16[8,9216]{1,0:T(8,128)(2,1)S(1)}, u32[]{:S(2)}, u32[]{:S(2)}) collective-permute-start(bf16[8,9216]{1,0:T(8,128)(2,1)S(1)} %get-tuple-element.65), channel_id=1, source_target_pairs={{0,2},{1,3},{4,0},{5,1},{8,4},{9,5},{12,8},{13,9},{14,12},{15,13},... | collective-permute-start | bytes 442376 | tf_op jit(solution)/shard_map/ppermute | solution.py:289
  65.7 7.1 %collective-permute-start.17 = (bf16[8,9216]{1,0:T(8,128)(2,1)S(1)}, bf16[8,9216]{1,0:T(8,128)(2,1)S(1)}, u32[]{:S(2)}, u32[]{:S(2)}) collective-permute-start(bf16[8,9216]{1,0:T(8,128)(2,1)S(1)} %get-tuple-element.56), channel_id=1, source_target_pairs={{0,4},{1,5},{4,8},{5,9},{8,12},{9,13},{12,14},{13,15},{14,10},{15,... | collective-permute-start | bytes 442376 | tf_op jit(solution)/shard_map/ppermute | solution.py:289
  67.2 6.8 %collective-permute-start.18 = (bf16[8,9216]{1,0:T(8,128)(2,1)S(1)}, bf16[8,9216]{1,0:T(8,128)(2,1)S(1)}, u32[]{:S(2)}, u32[]{:S(2)}) collective-permute-start(bf16[8,9216]{1,0:T(8,128)(2,1)S(1)} %get-tuple-element.57), channel_id=1, source_target_pairs={{0,2},{1,3},{4,0},{5,1},{8,4},{9,5},{12,8},{13,9},{14,12},{15,13},... | collective-permute-start | bytes 442376 | tf_op jit(solution)/shard_map/ppermute | solution.py:289
  71.9 5.3 %collective-permute-start.26 = (bf16[8,9216]{1,0:T(8,128)(2,1)S(1)}, bf16[8,9216]{1,0:T(8,128)(2,1)S(1)}, u32[]{:S(2)}, u32[]{:S(2)}) collective-permute-start(bf16[8,9216]{1,0:T(8,128)(2,1)S(1)} %get-tuple-element.66), channel_id=1, source_target_pairs={{0,4},{1,5},{4,8},{5,9},{8,12},{9,13},{12,14},{13,15},{14,10},{15,... | collective-permute-start | bytes 442376 | tf_op jit(solution)/shard_map/ppermute | solution.py:289
  72.0 12.4 %collective-permute-start.14 = (bf16[128,64]{1,0:T(8,128)(2,1)S(1)}, bf16[128,64]{1,0:T(8,128)(2,1)S(1)}, u32[]{:S(2)}, u32[]{:S(2)}) collective-permute-start(bf16[128,64]{1,0:T(8,128)(2,1)S(1)} %get-tuple-element.82), channel_id=1, source_target_pairs={{0,1},{1,0},{2,3},{3,2},{4,5},{5,4},{6,7},{7,6},{8,9},{9,8},{10,11... | collective-permute-start | bytes 49160 | tf_op jit(solution)/shard_map/ppermute | solution.py:289
  72.8 6.8 %collective-permute-start.27 = (bf16[8,9216]{1,0:T(8,128)(2,1)S(1)}, bf16[8,9216]{1,0:T(8,128)(2,1)S(1)}, u32[]{:S(2)}, u32[]{:S(2)}) collective-permute-start(bf16[8,9216]{1,0:T(8,128)(2,1)S(1)} %get-tuple-element.67), channel_id=1, source_target_pairs={{0,2},{1,3},{4,0},{5,1},{8,4},{9,5},{12,8},{13,9},{14,12},{15,13},... | collective-permute-start | bytes 442376 | tf_op jit(solution)/shard_map/ppermute | solution.py:289
  74.1 7.6 %collective-permute-start.19 = (bf16[8,9216]{1,0:T(8,128)(2,1)S(1)}, bf16[8,9216]{1,0:T(8,128)(2,1)S(1)}, u32[]{:S(2)}, u32[]{:S(2)}) collective-permute-start(bf16[8,9216]{1,0:T(8,128)(2,1)S(1)} %get-tuple-element.58), channel_id=1, source_target_pairs={{0,4},{1,5},{4,8},{5,9},{8,12},{9,13},{12,14},{13,15},{14,10},{15,... | collective-permute-start | bytes 442376 | tf_op jit(solution)/shard_map/ppermute | solution.py:289
  77.2 5.1 %collective-permute-start.20 = (bf16[8,9216]{1,0:T(8,128)(2,1)S(1)}, bf16[8,9216]{1,0:T(8,128)(2,1)S(1)}, u32[]{:S(2)}, u32[]{:S(2)}) collective-permute-start(bf16[8,9216]{1,0:T(8,128)(2,1)S(1)} %get-tuple-element.59), channel_id=1, source_target_pairs={{0,2},{1,3},{4,0},{5,1},{8,4},{9,5},{12,8},{13,9},{14,12},{15,13},... | collective-permute-start | bytes 442376 | tf_op jit(solution)/shard_map/ppermute | solution.py:289
  79.7 7.8 %collective-permute-start.28 = (bf16[8,9216]{1,0:T(8,128)(2,1)S(1)}, bf16[8,9216]{1,0:T(8,128)(2,1)S(1)}, u32[]{:S(2)}, u32[]{:S(2)}) collective-permute-start(bf16[8,9216]{1,0:T(8,128)(2,1)S(1)} %get-tuple-element.68), channel_id=1, source_target_pairs={{0,4},{1,5},{4,8},{5,9},{8,12},{9,13},{12,14},{13,15},{14,10},{15,... | collective-permute-start | bytes 442376 | tf_op jit(solution)/shard_map/ppermute | solution.py:289
  81.7 5.9 %collective-permute-start.29 = (bf16[8,9216]{1,0:T(8,128)(2,1)S(1)}, bf16[8,9216]{1,0:T(8,128)(2,1)S(1)}, u32[]{:S(2)}, u32[]{:S(2)}) collective-permute-start(bf16[8,9216]{1,0:T(8,128)(2,1)S(1)} %get-tuple-element.69), channel_id=1, source_target_pairs={{0,2},{1,3},{4,0},{5,1},{8,4},{9,5},{12,8},{13,9},{14,12},{15,13},... | collective-permute-start | bytes 442376 | tf_op jit(solution)/shard_map/ppermute | solution.py:289
  82.4 5.7 %collective-permute-start.21 = (bf16[8,9216]{1,0:T(8,128)(2,1)S(1)}, bf16[8,9216]{1,0:T(8,128)(2,1)S(1)}, u32[]{:S(2)}, u32[]{:S(2)}) collective-permute-start(bf16[8,9216]{1,0:T(8,128)(2,1)S(1)} %get-tuple-element.60), channel_id=1, source_target_pairs={{0,4},{1,5},{4,8},{5,9},{8,12},{9,13},{12,14},{13,15},{14,10},{15,... | collective-permute-start | bytes 442376 | tf_op jit(solution)/shard_map/ppermute | solution.py:289
  84.5 5.1 %collective-permute-start.22 = (bf16[8,9216]{1,0:T(8,128)(2,1)S(1)}, bf16[8,9216]{1,0:T(8,128)(2,1)S(1)}, u32[]{:S(2)}, u32[]{:S(2)}) collective-permute-start(bf16[8,9216]{1,0:T(8,128)(2,1)S(1)} %get-tuple-element.61), channel_id=1, source_target_pairs={{0,2},{1,3},{4,0},{5,1},{8,4},{9,5},{12,8},{13,9},{14,12},{15,13},... | collective-permute-start | bytes 442376 | tf_op jit(solution)/shard_map/ppermute | solution.py:289
  (2 other events, 6.0 us)

commit v4 on v3

--- a/solution.py
+++ b/solution.py
@@ -303,7 +303,8 @@
     near = [k for k in order if abs(k) < far - 1]
     early = logits([[blocks[k]] for k in near], heads)
     rest = [k for k in order if k not in near and k != far]
-    edge_left, edge_right, early = lax.optimization_barrier((blocks[1 - far], blocks[far - 1], early))
+    edge_left, early = lax.optimization_barrier((blocks[1 - far], early))
+    edge_right = blocks[far - 1]
     last = (send(edge_left[:, :half], to_right), send(edge_right[:, half:], to_left))
     blocks = {k: [x] for k, x in blocks.items()}
     blocks[far] = last

time: 90.7 us -> 89.3 us (0.985)
  waiting for transfers between devices: 32.2 us -> 30.4 us
    ppermute x26, waiting for transfers between devices: 26.6 us -> 24.6 us  [send(): return lax.ppermute(x, 'pipe', perm)]
    ppermute x2, starting transfers between devices: 3.31 us -> 4.35 us  [from_every_chip(): lax.ppermute(known[width - left:], 'pipe', shift_pairs(ring, width))]
  transfers between devices with their start and end apart: 30 -> 30, of which waited for: 19 -> 18; matrix products, arithmetic and copies ran while one was open for 8% -> 8% of each run, Pallas kernels for 9% -> 9%
where the time goes in v4:
time: 89.3 us; the launch traced here: 89 us
  waiting for transfers between devices  30.4 us (34%)
  starting transfers between devices  29.8 us (33%)
  Pallas kernels  12.7 us (14%)
  local copies, waits for them, and re-layouts  6.36 us (7%)
  matrix products  4.49 us (5%)
  other arithmetic  4.42 us (5%)
    ppermute x26, waiting for transfers between devices, send(): return lax.ppermute(x, 'pipe', perm)  24.6 us
    ppermute x26, starting transfers between devices, send(): return lax.ppermute(x, 'pipe', perm)  23 us
    pallas_call x3, Pallas kernels, logits(): pl.pallas_call(body, out_shape=jax.ShapeDtypeStruct((ids, rows), F32), in...  7.69 us
    unnamed x12, local copies, waits for them, and re-layouts  6.02 us
    ppermute x2, waiting for transfers between devices, from_every_chip(): ahead = lax.ppermute(known[:right], 'pipe', shift_pairs(ring, -width))  5.19 us
    ppermute x2, starting transfers between devices, from_every_chip(): lax.ppermute(known[width - left:], 'pipe', shift_pairs(ring, width))  4.35 us
    dot_general x1, matrix products, program(): lax.dot_general(jnp.concatenate([dlogit[:ids], sib_dlogit], axis=1), jnp....  3.06 us
    pallas_call x1, Pallas kernels, stack_heads(): pl.pallas_call(body, out_shape=pltpu.VMEM((2 * ids, width), own.dtype), i...  2.67 us
  transfers between devices with their start and end apart: 30, of which 18 were waited for; matrix products, arithmetic and copies ran while one was open for 8% of the time, Pallas kernels for 9%

profile of v4, /device:TPU:0, one launch (start us, length us, event | category | flops | bytes accessed | tf_op | source)
XLA Modules:
  0.0 89.0 jit_solution(7472935946450949117)
XLA Ops:
  1.1 2.6 %collective-permute-start.2 = (bf16[8,18432]{1,0:T(8,128)(2,1)}, bf16[8,18432]{1,0:T(8,128)(2,1)S(1)}, u32[]{:S(2)}, u32[]{:S(2)}) collective-permute-start(bf16[8,18432]{1,0:T(8,128)(2,1)} %refs_0_.2), channel_id=1, source_target_pairs={{0,2},{1,3},{4,0},{5,1},{8,4},{9,5},{12,8},{13,9},{14,12},{15,13},... | collective-permute-start | bytes 884744 | tf_op jit(solution)/shard_map/ppermute | solution.py:289
  6.6 5.1 %collective-permute-done.2.refs_1_ = bf16[8,18432]{1,0:T(8,128)(2,1)S(1)} collective-permute-done((bf16[8,18432]{1,0:T(8,128)(2,1)}, bf16[8,18432]{1,0:T(8,128)(2,1)S(1)}, u32[]{:S(2)}, u32[]{:S(2)}) %collective-permute-start.2) | collective-permute-done | bytes 294944 | tf_op jit(solution)/shard_map/ppermute | solution.py:289
  11.6 1.7 %collective-permute-start.3 = (bf16[8,18432]{1,0:T(8,128)(2,1)S(1)}, bf16[8,18432]{1,0:T(8,128)(2,1)S(1)}, u32[]{:S(2)}, u32[]{:S(2)}) collective-permute-start(bf16[8,18432]{1,0:T(8,128)(2,1)S(1)} %collective-permute-done.2.refs_1_), channel_id=1, source_target_pairs={{0,2},{1,3},{4,0},{5,1},{8,4},{9,5},{12,8},{13,9},{14,12},{15,13},... | collective-permute-start | bytes 884744 | tf_op jit(solution)/shard_map/ppermute | solution.py:289
  14.9 2.3 %copy-done.2 = bf16[128,18432]{1,0:T(8,128)(2,1)S(1)} copy-done((bf16[128,18432]{1,0:T(8,128)(2,1)S(1)}, bf16[128,18432]{1,0:T(8,128)(2,1)}, u32[]{:S(2)}) %copy-start.2) | copy-done | bytes 4718616
  17.2 2.7 %stack_heads.1.refs_5_.refs_2_.heads_ref = bf16[256,18432]{1,0:T(8,128)(2,1)S(1)} custom-call(bf16[128,18432]{1,0:T(8,128)(2,1)S(1)} %copy-done.2, bf16[128,18432]{1,0:T(8,128)(2,1)} %collective-permute-done.4.sib_ref), custom_call_target="tpu_custom_call" | custom-call | bytes 18874368 | tf_op jit(solution)/shard_map/stack_heads/pallas_call | solution.py:48
  20.4 1.2 %collective-permute-done.1.refs_4_ = bf16[8,18432]{1,0:T(8,128)(2,1)S(1)} collective-permute-done((bf16[8,18432]{1,0:T(8,128)(2,1)S(1)}, bf16[8,18432]{1,0:T(8,128)(2,1)S(1)}, u32[]{:S(2)}, u32[]{:S(2)}) %collective-permute-start.1) | collective-permute-done | bytes 294944 | tf_op jit(solution)/shard_map/ppermute | solution.py:289
  22.1 1.4 %collective-permute-start.6 = (bf16[8,18432]{1,0:T(8,128)(2,1)S(1)}, bf16[8,18432]{1,0:T(8,128)(2,1)S(1)}, u32[]{:S(2)}, u32[]{:S(2)}) collective-permute-start(bf16[8,18432]{1,0:T(8,128)(2,1)S(1)} %collective-permute-done.3.refs_3_), channel_id=1, source_target_pairs={{0,2},{1,3},{4,0},{5,1},{8,4},{9,5},{12,8},{13,9},{14,12},{15,13},... | collective-permute-start | bytes 884744 | tf_op jit(solution)/shard_map/ppermute | solution.py:289
  23.6 2.6 %logits.3 = f32[256,40]{1,0:T(8,128)S(1)} custom-call(bf16[8,18432]{1,0:T(8,128)(2,1)S(1)} %copy-done.3, bf16[8,18432]{1,0:T(8,128)(2,1)S(1)} %collective-permute-done.2.refs_1_, bf16[8,18432]{1,0:T(8,128)(2,1)S(1)} %collective-permute-done.refs_2_, bf16[8,18432]{1,0:T(8,128)(2,1)S(1)} %collective-permute-done.3.refs_3_, ...), custom_call_target="tpu_custom_call" | custom-call | flops 24159191040 | bytes 9437184 | tf_op jit(solution)/shard_map/logits/pallas_call | solution.py:114
  26.2 2.8 %collective-permute-done.5.refs_1_.refs_6_ = bf16[8,18432]{1,0:T(8,128)(2,1)S(1)} collective-permute-done((bf16[8,18432]{1,0:T(8,128)(2,1)S(1)}, bf16[8,18432]{1,0:T(8,128)(2,1)S(1)}, u32[]{:S(2)}, u32[]{:S(2)}) %collective-permute-start.5) | collective-permute-done | bytes 294944 | tf_op jit(solution)/shard_map/ppermute | solution.py:289
  29.8 1.2 %collective-permute-start.8 = (bf16[8,9216]{1,0:T(8,128)(2,1)S(1)}, bf16[8,9216]{1,0:T(8,128)(2,1)S(1)}, u32[]{:S(2)}, u32[]{:S(2)}) collective-permute-start(bf16[8,9216]{1,0:T(8,128)(2,1)S(1)} %slice.56), channel_id=1, source_target_pairs={{0,2},{1,3},{4,0},{5,1},{8,4},{9,5},{12,8},{13,9},{14,12},{15,13},... | collective-permute-start | bytes 442376 | tf_op jit(solution)/shard_map/ppermute | solution.py:289
  31.1 2.6 %logits.4 = f32[256,16]{1,0:T(8,128)S(1)} custom-call(bf16[8,18432]{1,0:T(8,128)(2,1)S(1)} %collective-permute-done.6.refs_0_.refs_5_, bf16[8,18432]{1,0:T(8,128)(2,1)S(1)} %collective-permute-done.5.refs_1_.refs_6_, bf16[256,18432]{1,0:T(8,128)(2,1)S(1)} %stack_heads.1.refs_5_.refs_2_.heads_ref), custom_call_target="tpu_custom_call" | custom-call | flops 24159191040 | bytes 9437184 | tf_op jit(solution)/shard_map/logits/pallas_call | solution.py:114
  35.0 2.6 %logits.5 = f32[256,8]{1,0:T(8,128)S(1)} custom-call(bf16[8,9216]{1,0:T(8,128)(2,1)S(1)} %collective-permute-done.7.refs_0_.refs_7_, bf16[8,9216]{1,0:T(8,128)(2,1)S(1)} %collective-permute-done.8.refs_1_.refs_8_, bf16[256,18432]{1,0:T(8,128)(2,1)S(1)} %stack_heads.1.refs_5_.refs_2_.heads_ref), custom_call_target="tpu_custom_call" | custom-call | flops 24159191040 | bytes 9437184 | tf_op jit(solution)/shard_map/logits/pallas_call | solution.py:114
  38.1 1.2 %collective-permute-start.10 = (f32[1,6,64]{2,1,0:T(8,128)S(1)}, f32[1,6,64]{2,1,0:T(8,128)S(1)}, u32[]{:S(2)}, u32[]{:S(2)}) collective-permute-start(f32[1,6,64]{2,1,0:T(8,128)S(1)} %convolution_bitcast_fusion), channel_id=1, source_target_pairs={{0,2},{1,3},{4,0},{5,1},{8,4},{9,5},{12,8},{13,9},{14,12},{15,13},... | collective-permute-start | bytes 4616 | tf_op jit(solution)/shard_map/ppermute | solution.py:264
  40.1 1.6 %collective-permute-done.10 = f32[1,6,64]{2,1,0:T(8,128)S(1)} collective-permute-done((f32[1,6,64]{2,1,0:T(8,128)S(1)}, f32[1,6,64]{2,1,0:T(8,128)S(1)}, u32[]{:S(2)}, u32[]{:S(2)}) %collective-permute-start.10) | collective-permute-done | bytes 1568 | tf_op jit(solution)/shard_map/ppermute | solution.py:264
  41.7 3.5 %collective-permute-start.11 = (f32[2,6,64]{2,1,0:T(8,128)S(1)}, f32[2,6,64]{2,1,0:T(8,128)S(1)}, u32[]{:S(2)}, u32[]{:S(2)}) collective-permute-start(f32[2,6,64]{2,1,0:T(8,128)S(1)} %pad_maximum_fusion.3), channel_id=1, source_target_pairs={{0,12},{1,13},{4,14},{5,15},{8,10},{9,11},{12,6},{13,7},{14,2},{15... | collective-permute-start | bytes 9224 | tf_op jit(solution)/shard_map/ppermute | solution.py:267
  45.3 1.3 %collective-permute-start.13 = (f32[3,6,64]{2,1,0:T(8,128)S(1)}, f32[3,6,64]{2,1,0:T(8,128)S(1)}, u32[]{:S(2)}, u32[]{:S(2)}) collective-permute-start(f32[3,6,64]{2,1,0:T(8,128)S(1)} %pad_maximum_fusion.2), channel_id=1, source_target_pairs={{0,10},{1,11},{4,6},{5,7},{8,2},{9,3},{12,0},{13,1},{14,4},{15,5},... | collective-permute-start | bytes 13832 | tf_op jit(solution)/shard_map/ppermute | solution.py:264
  47.2 3.6 %collective-permute-done.13 = f32[3,6,64]{2,1,0:T(8,128)S(1)} collective-permute-done((f32[3,6,64]{2,1,0:T(8,128)S(1)}, f32[3,6,64]{2,1,0:T(8,128)S(1)}, u32[]{:S(2)}, u32[]{:S(2)}) %collective-permute-start.13) | collective-permute-done | bytes 4640 | tf_op jit(solution)/shard_map/ppermute | solution.py:264
  51.3 3.7 %copy-done.1 = bf16[256,18432]{1,0:T(8,128)(2,1)S(1)} copy-done((bf16[256,18432]{1,0:T(8,128)(2,1)S(1)}, bf16[256,18432]{1,0:T(8,128)(2,1)}, u32[]{:S(2)}) %copy-start.1) | copy-done | bytes 9437208
  55.0 1.8 %gradient_terms.1 = (f32[56,9216]{1,0:T(8,128)S(1)}, f32[56,9216]{1,0:T(8,128)S(1)}, bf16[8,9216]{1,0:T(8,128)(2,1)S(1)}, bf16[8,9216]{1,0:T(8,128)(2,1)S(1)}) custom-call(bf16[256,64]{1,0:T(8,128)(2,1)S(1)} %fusion.6.d_ref, bf16[256,18432]{1,0:T(8,128)(2,1)S(1)} %copy-done.1), custom_call_target="tpu_custom_call" | custom-call | flops 24159191040 | bytes 9437184 | tf_op jit(solution)/shard_map/gradient_terms/pallas_call | solution.py:180
  57.6 1.5 %collective-permute-start.16 = (bf16[8,9216]{1,0:T(8,128)(2,1)S(1)}, bf16[8,9216]{1,0:T(8,128)(2,1)S(1)}, u32[]{:S(2)}, u32[]{:S(2)}) collective-permute-start(bf16[8,9216]{1,0:T(8,128)(2,1)S(1)} %get-tuple-element.43), channel_id=1, source_target_pairs={{0,4},{1,5},{4,8},{5,9},{8,12},{9,13},{12,14},{13,15},{14,10},{15,... | collective-permute-start | bytes 442376 | tf_op jit(solution)/shard_map/ppermute | solution.py:289
  59.1 4.2 %collective-permute-done.23.refs_0_ = bf16[8,9216]{1,0:T(8,128)(2,1)S(1)} collective-permute-done((bf16[8,9216]{1,0:T(8,128)(2,1)S(1)}, bf16[8,9216]{1,0:T(8,128)(2,1)S(1)}, u32[]{:S(2)}, u32[]{:S(2)}) %collective-permute-start.23) | collective-permute-done | bytes 147488 | tf_op jit(solution)/shard_map/ppermute | solution.py:289
  63.3 1.3 %collective-permute-start.24 = (bf16[8,9216]{1,0:T(8,128)(2,1)S(1)}, bf16[8,9216]{1,0:T(8,128)(2,1)S(1)}, u32[]{:S(2)}, u32[]{:S(2)}) collective-permute-start(bf16[8,9216]{1,0:T(8,128)(2,1)S(1)} %get-tuple-element.62), channel_id=1, source_target_pairs={{0,4},{1,5},{4,8},{5,9},{8,12},{9,13},{12,14},{13,15},{14,10},{15,... | collective-permute-start | bytes 442376 | tf_op jit(solution)/shard_map/ppermute | solution.py:289
  65.5 1.3 %collective-permute-start.17 = (bf16[8,9216]{1,0:T(8,128)(2,1)S(1)}, bf16[8,9216]{1,0:T(8,128)(2,1)S(1)}, u32[]{:S(2)}, u32[]{:S(2)}) collective-permute-start(bf16[8,9216]{1,0:T(8,128)(2,1)S(1)} %get-tuple-element.54), channel_id=1, source_target_pairs={{0,4},{1,5},{4,8},{5,9},{8,12},{9,13},{12,14},{13,15},{14,10},{15,... | collective-permute-start | bytes 442376 | tf_op jit(solution)/shard_map/ppermute | solution.py:289
  67.5 2.6 %collective-permute-done.24.refs_0_ = bf16[8,9216]{1,0:T(8,128)(2,1)S(1)} collective-permute-done((bf16[8,9216]{1,0:T(8,128)(2,1)S(1)}, bf16[8,9216]{1,0:T(8,128)(2,1)S(1)}, u32[]{:S(2)}, u32[]{:S(2)}) %collective-permute-start.24) | collective-permute-done | bytes 147488 | tf_op jit(solution)/shard_map/ppermute | solution.py:289
  70.1 1.2 %collective-permute-done.25.refs_1_ = bf16[8,9216]{1,0:T(8,128)(2,1)S(1)} collective-permute-done((bf16[8,9216]{1,0:T(8,128)(2,1)S(1)}, bf16[8,9216]{1,0:T(8,128)(2,1)S(1)}, u32[]{:S(2)}, u32[]{:S(2)}) %collective-permute-start.25) | collective-permute-done | bytes 147488 | tf_op jit(solution)/shard_map/ppermute | solution.py:289
  71.6 1.2 %collective-permute-done.17.refs_0_ = bf16[8,9216]{1,0:T(8,128)(2,1)S(1)} collective-permute-done((bf16[8,9216]{1,0:T(8,128)(2,1)S(1)}, bf16[8,9216]{1,0:T(8,128)(2,1)S(1)}, u32[]{:S(2)}, u32[]{:S(2)}) %collective-permute-start.17) | collective-permute-done | bytes 147488 | tf_op jit(solution)/shard_map/ppermute | solution.py:289
  73.7 1.3 %collective-permute-start.19 = (bf16[8,9216]{1,0:T(8,128)(2,1)S(1)}, bf16[8,9216]{1,0:T(8,128)(2,1)S(1)}, u32[]{:S(2)}, u32[]{:S(2)}) collective-permute-start(bf16[8,9216]{1,0:T(8,128)(2,1)S(1)} %get-tuple-element.56), channel_id=1, source_target_pairs={{0,4},{1,5},{4,8},{5,9},{8,12},{9,13},{12,14},{13,15},{14,10},{15,... | collective-permute-start | bytes 442376 | tf_op jit(solution)/shard_map/ppermute | solution.py:289
  75.0 1.8 %collective-permute-done.26.refs_0_ = bf16[8,9216]{1,0:T(8,128)(2,1)S(1)} collective-permute-done((bf16[8,9216]{1,0:T(8,128)(2,1)S(1)}, bf16[8,9216]{1,0:T(8,128)(2,1)S(1)}, u32[]{:S(2)}, u32[]{:S(2)}) %collective-permute-start.26) | collective-permute-done | bytes 147488 | tf_op jit(solution)/shard_map/ppermute | solution.py:289
  78.0 1.3 %collective-permute-done.27.refs_1_ = bf16[8,9216]{1,0:T(8,128)(2,1)S(1)} collective-permute-done((bf16[8,9216]{1,0:T(8,128)(2,1)S(1)}, bf16[8,9216]{1,0:T(8,128)(2,1)S(1)}, u32[]{:S(2)}, u32[]{:S(2)}) %collective-permute-start.27) | collective-permute-done | bytes 147488 | tf_op jit(solution)/shard_map/ppermute | solution.py:289
  79.4 1.2 %collective-permute-start.28 = (bf16[8,9216]{1,0:T(8,128)(2,1)S(1)}, bf16[8,9216]{1,0:T(8,128)(2,1)S(1)}, u32[]{:S(2)}, u32[]{:S(2)}) collective-permute-start(bf16[8,9216]{1,0:T(8,128)(2,1)S(1)} %get-tuple-element.66), channel_id=1, source_target_pairs={{0,4},{1,5},{4,8},{5,9},{8,12},{9,13},{12,14},{13,15},{14,10},{15,... | collective-permute-start | bytes 442376 | tf_op jit(solution)/shard_map/ppermute | solution.py:289
  82.0 1.1 %collective-permute-start.21 = (bf16[8,9216]{1,0:T(8,128)(2,1)S(1)}, bf16[8,9216]{1,0:T(8,128)(2,1)S(1)}, u32[]{:S(2)}, u32[]{:S(2)}) collective-permute-start(bf16[8,9216]{1,0:T(8,128)(2,1)S(1)} %get-tuple-element.58), channel_id=1, source_target_pairs={{0,4},{1,5},{4,8},{5,9},{8,12},{9,13},{12,14},{13,15},{14,10},{15,... | collective-permute-start | bytes 442376 | tf_op jit(solution)/shard_map/ppermute | solution.py:289
  84.0 3.1 %convolution_convert_fusion = bf16[128,18432]{1,0:T(8,128)(2,1)} fusion(bf16[64,18432]{1,0:T(8,128)(2,1)S(1)} %collective-permute-done.15, bf16[64,18432]{1,0:T(8,128)(2,1)S(1)} %assemble.1, bf16[128,64]{1,0:T(8,128)(2,1)S(1)} %collective-permute-done.14, bf16[128,64]{1,0:T(8,128)(2,1)S(1)} %get-tuple-element.79), kind=kOutput, calls=%fused_computation | convolution fusion | flops 615841792 | bytes 9469952 | tf_op jit(solution)/shard_map/dot_general | solution.py:362
  (89 shorter events, 20.0 us)
Async XLA Ops:
  0.6 14.3 %collective-permute-start.4 = (bf16[128,18432]{1,0:T(8,128)(2,1)}, bf16[128,18432]{1,0:T(8,128)(2,1)}, u32[]{:S(2)}, u32[]{:S(2)}) collective-permute-start(bf16[128,18432]{1,0:T(8,128)(2,1)} %own_ref.1), channel_id=1, source_target_pairs={{0,1},{1,0},{2,3},{3,2},{4,5},{5,4},{6,7},{7,6},{8,9},{9,8},{10,11... | collective-permute-start | bytes 14155784 | tf_op jit(solution)/shard_map/ppermute | solution.py:289
  1.1 10.5 %collective-permute-start.2 = (bf16[8,18432]{1,0:T(8,128)(2,1)}, bf16[8,18432]{1,0:T(8,128)(2,1)S(1)}, u32[]{:S(2)}, u32[]{:S(2)}) collective-permute-start(bf16[8,18432]{1,0:T(8,128)(2,1)} %refs_0_.2), channel_id=1, source_target_pairs={{0,2},{1,3},{4,0},{5,1},{8,4},{9,5},{12,8},{13,9},{14,12},{15,13},... | collective-permute-start | bytes 884744 | tf_op jit(solution)/shard_map/ppermute | solution.py:289
  3.7 9.6 %collective-permute-start = (bf16[8,18432]{1,0:T(8,128)(2,1)}, bf16[8,18432]{1,0:T(8,128)(2,1)S(1)}, u32[]{:S(2)}, u32[]{:S(2)}) collective-permute-start(bf16[8,18432]{1,0:T(8,128)(2,1)} %refs_0_.2), channel_id=1, source_target_pairs={{0,4},{1,5},{4,8},{5,9},{8,12},{9,13},{12,14},{13,15},{14,10},{15,... | collective-permute-start | bytes 884744 | tf_op jit(solution)/shard_map/ppermute | solution.py:289
  3.9 9.9 %collective-permute-start.9 = (bf16[128,128]{1,0:T(8,128)(2,1)}, bf16[128,128]{1,0:T(8,128)(2,1)S(1)}, u32[]{:S(2)}, u32[]{:S(2)}) collective-permute-start(bf16[128,128]{1,0:T(8,128)(2,1)} %param.8), channel_id=1, source_target_pairs={{0,1},{1,0},{2,3},{3,2},{4,5},{5,4},{6,7},{7,6},{8,9},{9,8},{10,11... | collective-permute-start | bytes 98312 | tf_op jit(solution)/shard_map/ppermute | solution.py:289
  11.6 8.8 %collective-permute-start.3 = (bf16[8,18432]{1,0:T(8,128)(2,1)S(1)}, bf16[8,18432]{1,0:T(8,128)(2,1)S(1)}, u32[]{:S(2)}, u32[]{:S(2)}) collective-permute-start(bf16[8,18432]{1,0:T(8,128)(2,1)S(1)} %collective-permute-done.2.refs_1_), channel_id=1, source_target_pairs={{0,2},{1,3},{4,0},{5,1},{8,4},{9,5},{12,8},{13,9},{14,12},{15,13},... | collective-permute-start | bytes 884744 | tf_op jit(solution)/shard_map/ppermute | solution.py:289
  13.3 8.3 %collective-permute-start.1 = (bf16[8,18432]{1,0:T(8,128)(2,1)S(1)}, bf16[8,18432]{1,0:T(8,128)(2,1)S(1)}, u32[]{:S(2)}, u32[]{:S(2)}) collective-permute-start(bf16[8,18432]{1,0:T(8,128)(2,1)S(1)} %collective-permute-done.refs_2_), channel_id=1, source_target_pairs={{0,4},{1,5},{4,8},{5,9},{8,12},{9,13},{12,14},{13,15},{14,10},{15,... | collective-permute-start | bytes 884744 | tf_op jit(solution)/shard_map/ppermute | solution.py:289
  17.2 6.3 %copy-start.3 = (bf16[8,18432]{1,0:T(8,128)(2,1)S(1)}, bf16[8,18432]{1,0:T(8,128)(2,1)}, u32[]{:S(2)}) copy-start(bf16[8,18432]{1,0:T(8,128)(2,1)} %refs_0_.2) | copy-start | bytes 884740
  19.9 15.1 %copy-start = (bf16[256,18432]{1,0:T(8,128)(2,1)}, bf16[256,18432]{1,0:T(8,128)(2,1)S(1)}, u32[]{:S(2)}) copy-start(bf16[256,18432]{1,0:T(8,128)(2,1)S(1)} %stack_heads.1.refs_5_.refs_2_.heads_ref) | copy-start | bytes 28311556
  21.6 7.4 %collective-permute-start.5 = (bf16[8,18432]{1,0:T(8,128)(2,1)S(1)}, bf16[8,18432]{1,0:T(8,128)(2,1)S(1)}, u32[]{:S(2)}, u32[]{:S(2)}) collective-permute-start(bf16[8,18432]{1,0:T(8,128)(2,1)S(1)} %collective-permute-done.1.refs_4_), channel_id=1, source_target_pairs={{0,4},{1,5},{4,8},{5,9},{8,12},{9,13},{12,14},{13,15},{14,10},{15,... | collective-permute-start | bytes 884744 | tf_op jit(solution)/shard_map/ppermute | solution.py:289
  22.1 7.7 %collective-permute-start.6 = (bf16[8,18432]{1,0:T(8,128)(2,1)S(1)}, bf16[8,18432]{1,0:T(8,128)(2,1)S(1)}, u32[]{:S(2)}, u32[]{:S(2)}) collective-permute-start(bf16[8,18432]{1,0:T(8,128)(2,1)S(1)} %collective-permute-done.3.refs_3_), channel_id=1, source_target_pairs={{0,2},{1,3},{4,0},{5,1},{8,4},{9,5},{12,8},{13,9},{14,12},{15,13},... | collective-permute-start | bytes 884744 | tf_op jit(solution)/shard_map/ppermute | solution.py:289
  28.9 5.2 %collective-permute-start.7 = (bf16[8,9216]{1,0:T(8,128)(2,1)S(1)}, bf16[8,9216]{1,0:T(8,128)(2,1)S(1)}, u32[]{:S(2)}, u32[]{:S(2)}) collective-permute-start(bf16[8,9216]{1,0:T(8,128)(2,1)S(1)} %slice.43), channel_id=1, source_target_pairs={{0,4},{1,5},{4,8},{5,9},{8,12},{9,13},{12,14},{13,15},{14,10},{15,... | collective-permute-start | bytes 442376 | tf_op jit(solution)/shard_map/ppermute | solution.py:289
  29.8 5.2 %collective-permute-start.8 = (bf16[8,9216]{1,0:T(8,128)(2,1)S(1)}, bf16[8,9216]{1,0:T(8,128)(2,1)S(1)}, u32[]{:S(2)}, u32[]{:S(2)}) collective-permute-start(bf16[8,9216]{1,0:T(8,128)(2,1)S(1)} %slice.56), channel_id=1, source_target_pairs={{0,2},{1,3},{4,0},{5,1},{8,4},{9,5},{12,8},{13,9},{14,12},{15,13},... | collective-permute-start | bytes 442376 | tf_op jit(solution)/shard_map/ppermute | solution.py:289
  38.1 3.6 %collective-permute-start.10 = (f32[1,6,64]{2,1,0:T(8,128)S(1)}, f32[1,6,64]{2,1,0:T(8,128)S(1)}, u32[]{:S(2)}, u32[]{:S(2)}) collective-permute-start(f32[1,6,64]{2,1,0:T(8,128)S(1)} %convolution_bitcast_fusion), channel_id=1, source_target_pairs={{0,2},{1,3},{4,0},{5,1},{8,4},{9,5},{12,8},{13,9},{14,12},{15,13},... | collective-permute-start | bytes 4616 | tf_op jit(solution)/shard_map/ppermute | solution.py:264
  39.3 5.9 %collective-permute-start.12 = (f32[1,6,64]{2,1,0:T(8,128)S(1)}, f32[1,6,64]{2,1,0:T(8,128)S(1)}, u32[]{:S(2)}, u32[]{:S(2)}) collective-permute-start(f32[1,6,64]{2,1,0:T(8,128)S(1)} %convolution_bitcast_fusion), channel_id=1, source_target_pairs={{0,4},{1,5},{4,8},{5,9},{8,12},{9,13},{12,14},{13,15},{14,10},{15,... | collective-permute-start | bytes 4616 | tf_op jit(solution)/shard_map/ppermute | solution.py:267
  41.7 5.4 %collective-permute-start.11 = (f32[2,6,64]{2,1,0:T(8,128)S(1)}, f32[2,6,64]{2,1,0:T(8,128)S(1)}, u32[]{:S(2)}, u32[]{:S(2)}) collective-permute-start(f32[2,6,64]{2,1,0:T(8,128)S(1)} %pad_maximum_fusion.3), channel_id=1, source_target_pairs={{0,12},{1,13},{4,14},{5,15},{8,10},{9,11},{12,6},{13,7},{14,2},{15... | collective-permute-start | bytes 9224 | tf_op jit(solution)/shard_map/ppermute | solution.py:267
  45.3 5.5 %collective-permute-start.13 = (f32[3,6,64]{2,1,0:T(8,128)S(1)}, f32[3,6,64]{2,1,0:T(8,128)S(1)}, u32[]{:S(2)}, u32[]{:S(2)}) collective-permute-start(f32[3,6,64]{2,1,0:T(8,128)S(1)} %pad_maximum_fusion.2), channel_id=1, source_target_pairs={{0,10},{1,11},{4,6},{5,7},{8,2},{9,3},{12,0},{13,1},{14,4},{15,5},... | collective-permute-start | bytes 13832 | tf_op jit(solution)/shard_map/ppermute | solution.py:264
  56.9 27.1 %collective-permute-start.15 = (bf16[64,18432]{1,0:T(8,128)(2,1)S(1)}, bf16[64,18432]{1,0:T(8,128)(2,1)S(1)}, u32[]{:S(2)}, u32[]{:S(2)}) collective-permute-start(bf16[64,18432]{1,0:T(8,128)(2,1)S(1)} %assemble.1), channel_id=1, source_target_pairs={{0,1},{1,0},{2,3},{3,2},{4,5},{5,4},{6,7},{7,6},{8,9},{9,8},{10,11... | collective-permute-start | bytes 7077896 | tf_op jit(solution)/shard_map/ppermute | solution.py:289
  57.0 6.2 %collective-permute-start.23 = (bf16[8,9216]{1,0:T(8,128)(2,1)S(1)}, bf16[8,9216]{1,0:T(8,128)(2,1)S(1)}, u32[]{:S(2)}, u32[]{:S(2)}) collective-permute-start(bf16[8,9216]{1,0:T(8,128)(2,1)S(1)} %get-tuple-element.61), channel_id=1, source_target_pairs={{0,2},{1,3},{4,0},{5,1},{8,4},{9,5},{12,8},{13,9},{14,12},{15,13},... | collective-permute-start | bytes 442376 | tf_op jit(solution)/shard_map/ppermute | solution.py:289
  57.6 7.8 %collective-permute-start.16 = (bf16[8,9216]{1,0:T(8,128)(2,1)S(1)}, bf16[8,9216]{1,0:T(8,128)(2,1)S(1)}, u32[]{:S(2)}, u32[]{:S(2)}) collective-permute-start(bf16[8,9216]{1,0:T(8,128)(2,1)S(1)} %get-tuple-element.43), channel_id=1, source_target_pairs={{0,4},{1,5},{4,8},{5,9},{8,12},{9,13},{12,14},{13,15},{14,10},{15,... | collective-permute-start | bytes 442376 | tf_op jit(solution)/shard_map/ppermute | solution.py:289
  63.3 6.8 %collective-permute-start.24 = (bf16[8,9216]{1,0:T(8,128)(2,1)S(1)}, bf16[8,9216]{1,0:T(8,128)(2,1)S(1)}, u32[]{:S(2)}, u32[]{:S(2)}) collective-permute-start(bf16[8,9216]{1,0:T(8,128)(2,1)S(1)} %get-tuple-element.62), channel_id=1, source_target_pairs={{0,4},{1,5},{4,8},{5,9},{8,12},{9,13},{12,14},{13,15},{14,10},{15,... | collective-permute-start | bytes 442376 | tf_op jit(solution)/shard_map/ppermute | solution.py:289
  64.7 6.7 %collective-permute-start.25 = (bf16[8,9216]{1,0:T(8,128)(2,1)S(1)}, bf16[8,9216]{1,0:T(8,128)(2,1)S(1)}, u32[]{:S(2)}, u32[]{:S(2)}) collective-permute-start(bf16[8,9216]{1,0:T(8,128)(2,1)S(1)} %get-tuple-element.63), channel_id=1, source_target_pairs={{0,2},{1,3},{4,0},{5,1},{8,4},{9,5},{12,8},{13,9},{14,12},{15,13},... | collective-permute-start | bytes 442376 | tf_op jit(solution)/shard_map/ppermute | solution.py:289
  65.5 7.3 %collective-permute-start.17 = (bf16[8,9216]{1,0:T(8,128)(2,1)S(1)}, bf16[8,9216]{1,0:T(8,128)(2,1)S(1)}, u32[]{:S(2)}, u32[]{:S(2)}) collective-permute-start(bf16[8,9216]{1,0:T(8,128)(2,1)S(1)} %get-tuple-element.54), channel_id=1, source_target_pairs={{0,4},{1,5},{4,8},{5,9},{8,12},{9,13},{12,14},{13,15},{14,10},{15,... | collective-permute-start | bytes 442376 | tf_op jit(solution)/shard_map/ppermute | solution.py:289
  66.8 6.8 %collective-permute-start.18 = (bf16[8,9216]{1,0:T(8,128)(2,1)S(1)}, bf16[8,9216]{1,0:T(8,128)(2,1)S(1)}, u32[]{:S(2)}, u32[]{:S(2)}) collective-permute-start(bf16[8,9216]{1,0:T(8,128)(2,1)S(1)} %get-tuple-element.55), channel_id=1, source_target_pairs={{0,2},{1,3},{4,0},{5,1},{8,4},{9,5},{12,8},{13,9},{14,12},{15,13},... | collective-permute-start | bytes 442376 | tf_op jit(solution)/shard_map/ppermute | solution.py:289
  71.5 5.3 %collective-permute-start.26 = (bf16[8,9216]{1,0:T(8,128)(2,1)S(1)}, bf16[8,9216]{1,0:T(8,128)(2,1)S(1)}, u32[]{:S(2)}, u32[]{:S(2)}) collective-permute-start(bf16[8,9216]{1,0:T(8,128)(2,1)S(1)} %get-tuple-element.64), channel_id=1, source_target_pairs={{0,4},{1,5},{4,8},{5,9},{8,12},{9,13},{12,14},{13,15},{14,10},{15,... | collective-permute-start | bytes 442376 | tf_op jit(solution)/shard_map/ppermute | solution.py:289
  71.6 11.4 %collective-permute-start.14 = (bf16[128,64]{1,0:T(8,128)(2,1)S(1)}, bf16[128,64]{1,0:T(8,128)(2,1)S(1)}, u32[]{:S(2)}, u32[]{:S(2)}) collective-permute-start(bf16[128,64]{1,0:T(8,128)(2,1)S(1)} %get-tuple-element.80), channel_id=1, source_target_pairs={{0,1},{1,0},{2,3},{3,2},{4,5},{5,4},{6,7},{7,6},{8,9},{9,8},{10,11... | collective-permute-start | bytes 49160 | tf_op jit(solution)/shard_map/ppermute | solution.py:289
  72.8 6.5 %collective-permute-start.27 = (bf16[8,9216]{1,0:T(8,128)(2,1)S(1)}, bf16[8,9216]{1,0:T(8,128)(2,1)S(1)}, u32[]{:S(2)}, u32[]{:S(2)}) collective-permute-start(bf16[8,9216]{1,0:T(8,128)(2,1)S(1)} %get-tuple-element.65), channel_id=1, source_target_pairs={{0,2},{1,3},{4,0},{5,1},{8,4},{9,5},{12,8},{13,9},{14,12},{15,13},... | collective-permute-start | bytes 442376 | tf_op jit(solution)/shard_map/ppermute | solution.py:289
  73.7 6.9 %collective-permute-start.19 = (bf16[8,9216]{1,0:T(8,128)(2,1)S(1)}, bf16[8,9216]{1,0:T(8,128)(2,1)S(1)}, u32[]{:S(2)}, u32[]{:S(2)}) collective-permute-start(bf16[8,9216]{1,0:T(8,128)(2,1)S(1)} %get-tuple-element.56), channel_id=1, source_target_pairs={{0,4},{1,5},{4,8},{5,9},{8,12},{9,13},{12,14},{13,15},{14,10},{15,... | collective-permute-start | bytes 442376 | tf_op jit(solution)/shard_map/ppermute | solution.py:289
  76.7 5.1 %collective-permute-start.20 = (bf16[8,9216]{1,0:T(8,128)(2,1)S(1)}, bf16[8,9216]{1,0:T(8,128)(2,1)S(1)}, u32[]{:S(2)}, u32[]{:S(2)}) collective-permute-start(bf16[8,9216]{1,0:T(8,128)(2,1)S(1)} %get-tuple-element.57), channel_id=1, source_target_pairs={{0,2},{1,3},{4,0},{5,1},{8,4},{9,5},{12,8},{13,9},{14,12},{15,13},... | collective-permute-start | bytes 442376 | tf_op jit(solution)/shard_map/ppermute | solution.py:289
  79.4 7.7 %collective-permute-start.28 = (bf16[8,9216]{1,0:T(8,128)(2,1)S(1)}, bf16[8,9216]{1,0:T(8,128)(2,1)S(1)}, u32[]{:S(2)}, u32[]{:S(2)}) collective-permute-start(bf16[8,9216]{1,0:T(8,128)(2,1)S(1)} %get-tuple-element.66), channel_id=1, source_target_pairs={{0,4},{1,5},{4,8},{5,9},{8,12},{9,13},{12,14},{13,15},{14,10},{15,... | collective-permute-start | bytes 442376 | tf_op jit(solution)/shard_map/ppermute | solution.py:289
  80.6 6.5 %collective-permute-start.29 = (bf16[8,9216]{1,0:T(8,128)(2,1)S(1)}, bf16[8,9216]{1,0:T(8,128)(2,1)S(1)}, u32[]{:S(2)}, u32[]{:S(2)}) collective-permute-start(bf16[8,9216]{1,0:T(8,128)(2,1)S(1)} %get-tuple-element.67), channel_id=1, source_target_pairs={{0,2},{1,3},{4,0},{5,1},{8,4},{9,5},{12,8},{13,9},{14,12},{15,13},... | collective-permute-start | bytes 442376 | tf_op jit(solution)/shard_map/ppermute | solution.py:289
  82.0 5.5 %collective-permute-start.21 = (bf16[8,9216]{1,0:T(8,128)(2,1)S(1)}, bf16[8,9216]{1,0:T(8,128)(2,1)S(1)}, u32[]{:S(2)}, u32[]{:S(2)}) collective-permute-start(bf16[8,9216]{1,0:T(8,128)(2,1)S(1)} %get-tuple-element.58), channel_id=1, source_target_pairs={{0,4},{1,5},{4,8},{5,9},{8,12},{9,13},{12,14},{13,15},{14,10},{15,... | collective-permute-start | bytes 442376 | tf_op jit(solution)/shard_map/ppermute | solution.py:289
  83.0 5.2 %collective-permute-start.22 = (bf16[8,9216]{1,0:T(8,128)(2,1)S(1)}, bf16[8,9216]{1,0:T(8,128)(2,1)S(1)}, u32[]{:S(2)}, u32[]{:S(2)}) collective-permute-start(bf16[8,9216]{1,0:T(8,128)(2,1)S(1)} %get-tuple-element.59), channel_id=1, source_target_pairs={{0,2},{1,3},{4,0},{5,1},{8,4},{9,5},{12,8},{13,9},{14,12},{15,13},... | collective-permute-start | bytes 442376 | tf_op jit(solution)/shard_map/ppermute | solution.py:289
  (2 other events, 6.0 us)

commit v5 on v4

--- a/solution.py
+++ b/solution.py
@@ -214,7 +214,7 @@
         out_specs=in_vmem(2),
         compiler_params=kernel_params(),
         cost_estimate=cost(
-            flops=2 * tokens * half, bytes_accessed=4 * tokens * half, transcendentals=0
+            flops=200 * tokens * half, bytes_accessed=4 * tokens * half, transcendentals=0
         ),
         name="ring_sums",
     )(term, *given)

time: 89.3 us -> 88.4 us (0.990)
  transfers between devices with their start and end apart: 30 -> 30, of which waited for: 18 -> 20; matrix products, arithmetic and copies ran while one was open for 8% -> 9% of each run, Pallas kernels for 9% -> 9%
where the time goes in v5:
time: 88.4 us; the launch traced here: 88.1 us
  waiting for transfers between devices  29.7 us (34%)
  starting transfers between devices  29.5 us (33%)
  Pallas kernels  12.7 us (14%)
  local copies, waits for them, and re-layouts  6.36 us (7%)
  matrix products  4.49 us (5%)
  other arithmetic  4.42 us (5%)
    ppermute x26, waiting for transfers between devices, send(): return lax.ppermute(x, 'pipe', perm)  23.9 us
    ppermute x26, starting transfers between devices, send(): return lax.ppermute(x, 'pipe', perm)  22.7 us
    pallas_call x3, Pallas kernels, logits(): pl.pallas_call(body, out_shape=jax.ShapeDtypeStruct((ids, rows), F32), in...  7.69 us
    unnamed x12, local copies, waits for them, and re-layouts  6.02 us
    ppermute x2, waiting for transfers between devices, from_every_chip(): ahead = lax.ppermute(known[:right], 'pipe', shift_pairs(ring, -width))  5.19 us
    ppermute x2, starting transfers between devices, from_every_chip(): lax.ppermute(known[width - left:], 'pipe', shift_pairs(ring, width))  4.35 us
    dot_general x1, matrix products, program(): lax.dot_general(jnp.concatenate([dlogit[:ids], sib_dlogit], axis=1), jnp....  3.06 us
    pallas_call x1, Pallas kernels, stack_heads(): pl.pallas_call(body, out_shape=pltpu.VMEM((2 * ids, width), own.dtype), i...  2.67 us
  transfers between devices with their start and end apart: 30, of which 20 were waited for; matrix products, arithmetic and copies ran while one was open for 9% of the time, Pallas kernels for 9%

profile of v5, /device:TPU:0, one launch (start us, length us, event | category | flops | bytes accessed | tf_op | source)
XLA Modules:
  0.0 88.1 jit_solution(11506826265423117051)
XLA Ops:
  1.1 2.6 %collective-permute-start.2 = (bf16[8,18432]{1,0:T(8,128)(2,1)}, bf16[8,18432]{1,0:T(8,128)(2,1)S(1)}, u32[]{:S(2)}, u32[]{:S(2)}) collective-permute-start(bf16[8,18432]{1,0:T(8,128)(2,1)} %refs_0_.2), channel_id=1, source_target_pairs={{0,2},{1,3},{4,0},{5,1},{8,4},{9,5},{12,8},{13,9},{14,12},{15,13},... | collective-permute-start | bytes 884744 | tf_op jit(solution)/shard_map/ppermute | solution.py:289
  6.6 5.1 %collective-permute-done.2.refs_1_ = bf16[8,18432]{1,0:T(8,128)(2,1)S(1)} collective-permute-done((bf16[8,18432]{1,0:T(8,128)(2,1)}, bf16[8,18432]{1,0:T(8,128)(2,1)S(1)}, u32[]{:S(2)}, u32[]{:S(2)}) %collective-permute-start.2) | collective-permute-done | bytes 294944 | tf_op jit(solution)/shard_map/ppermute | solution.py:289
  11.6 1.7 %collective-permute-start.3 = (bf16[8,18432]{1,0:T(8,128)(2,1)S(1)}, bf16[8,18432]{1,0:T(8,128)(2,1)S(1)}, u32[]{:S(2)}, u32[]{:S(2)}) collective-permute-start(bf16[8,18432]{1,0:T(8,128)(2,1)S(1)} %collective-permute-done.2.refs_1_), channel_id=1, source_target_pairs={{0,2},{1,3},{4,0},{5,1},{8,4},{9,5},{12,8},{13,9},{14,12},{15,13},... | collective-permute-start | bytes 884744 | tf_op jit(solution)/shard_map/ppermute | solution.py:289
  13.7 1.1 %fusion.25 = (f32[64]{0:T(128)S(1)}, f32[256,64]{0,1:T(8,128)S(1)}) fusion(s32[64]{0:T(128)S(1)} %add.114, bf16[128,128]{1,0:T(8,128)(2,1)S(1)} %collective-permute-done.9, bf16[128,128]{1,0:T(8,128)(2,1)} %param.8), kind=kOutput, calls=%fused_computation.70 | convolution fusion | flops 4349888 | bytes 131584 | tf_op jit(solution)/shard_map/dot_general | solution.py:327
  14.9 2.3 %copy-done.2 = bf16[128,18432]{1,0:T(8,128)(2,1)S(1)} copy-done((bf16[128,18432]{1,0:T(8,128)(2,1)S(1)}, bf16[128,18432]{1,0:T(8,128)(2,1)}, u32[]{:S(2)}) %copy-start.2) | copy-done | bytes 4718616
  17.2 2.7 %stack_heads.1.refs_5_.refs_2_.heads_ref = bf16[256,18432]{1,0:T(8,128)(2,1)S(1)} custom-call(bf16[128,18432]{1,0:T(8,128)(2,1)S(1)} %copy-done.2, bf16[128,18432]{1,0:T(8,128)(2,1)} %collective-permute-done.4.sib_ref), custom_call_target="tpu_custom_call" | custom-call | bytes 18874368 | tf_op jit(solution)/shard_map/stack_heads/pallas_call | solution.py:48
  20.4 1.2 %collective-permute-done.1.refs_4_ = bf16[8,18432]{1,0:T(8,128)(2,1)S(1)} collective-permute-done((bf16[8,18432]{1,0:T(8,128)(2,1)S(1)}, bf16[8,18432]{1,0:T(8,128)(2,1)S(1)}, u32[]{:S(2)}, u32[]{:S(2)}) %collective-permute-start.1) | collective-permute-done | bytes 294944 | tf_op jit(solution)/shard_map/ppermute | solution.py:289
  22.1 1.4 %collective-permute-start.6 = (bf16[8,18432]{1,0:T(8,128)(2,1)S(1)}, bf16[8,18432]{1,0:T(8,128)(2,1)S(1)}, u32[]{:S(2)}, u32[]{:S(2)}) collective-permute-start(bf16[8,18432]{1,0:T(8,128)(2,1)S(1)} %collective-permute-done.3.refs_3_), channel_id=1, source_target_pairs={{0,2},{1,3},{4,0},{5,1},{8,4},{9,5},{12,8},{13,9},{14,12},{15,13},... | collective-permute-start | bytes 884744 | tf_op jit(solution)/shard_map/ppermute | solution.py:289
  23.6 2.6 %logits.3 = f32[256,40]{1,0:T(8,128)S(1)} custom-call(bf16[8,18432]{1,0:T(8,128)(2,1)S(1)} %copy-done.3, bf16[8,18432]{1,0:T(8,128)(2,1)S(1)} %collective-permute-done.2.refs_1_, bf16[8,18432]{1,0:T(8,128)(2,1)S(1)} %collective-permute-done.refs_2_, bf16[8,18432]{1,0:T(8,128)(2,1)S(1)} %collective-permute-done.3.refs_3_, ...), custom_call_target="tpu_custom_call" | custom-call | flops 24159191040 | bytes 9437184 | tf_op jit(solution)/shard_map/logits/pallas_call | solution.py:114
  26.2 2.8 %collective-permute-done.5.refs_1_.refs_6_ = bf16[8,18432]{1,0:T(8,128)(2,1)S(1)} collective-permute-done((bf16[8,18432]{1,0:T(8,128)(2,1)S(1)}, bf16[8,18432]{1,0:T(8,128)(2,1)S(1)}, u32[]{:S(2)}, u32[]{:S(2)}) %collective-permute-start.5) | collective-permute-done | bytes 294944 | tf_op jit(solution)/shard_map/ppermute | solution.py:289
  29.8 1.2 %collective-permute-start.8 = (bf16[8,9216]{1,0:T(8,128)(2,1)S(1)}, bf16[8,9216]{1,0:T(8,128)(2,1)S(1)}, u32[]{:S(2)}, u32[]{:S(2)}) collective-permute-start(bf16[8,9216]{1,0:T(8,128)(2,1)S(1)} %slice.56), channel_id=1, source_target_pairs={{0,2},{1,3},{4,0},{5,1},{8,4},{9,5},{12,8},{13,9},{14,12},{15,13},... | collective-permute-start | bytes 442376 | tf_op jit(solution)/shard_map/ppermute | solution.py:289
  31.1 2.6 %logits.4 = f32[256,16]{1,0:T(8,128)S(1)} custom-call(bf16[8,18432]{1,0:T(8,128)(2,1)S(1)} %collective-permute-done.6.refs_0_.refs_5_, bf16[8,18432]{1,0:T(8,128)(2,1)S(1)} %collective-permute-done.5.refs_1_.refs_6_, bf16[256,18432]{1,0:T(8,128)(2,1)S(1)} %stack_heads.1.refs_5_.refs_2_.heads_ref), custom_call_target="tpu_custom_call" | custom-call | flops 24159191040 | bytes 9437184 | tf_op jit(solution)/shard_map/logits/pallas_call | solution.py:114
  35.0 2.6 %logits.5 = f32[256,8]{1,0:T(8,128)S(1)} custom-call(bf16[8,9216]{1,0:T(8,128)(2,1)S(1)} %collective-permute-done.7.refs_0_.refs_7_, bf16[8,9216]{1,0:T(8,128)(2,1)S(1)} %collective-permute-done.8.refs_1_.refs_8_, bf16[256,18432]{1,0:T(8,128)(2,1)S(1)} %stack_heads.1.refs_5_.refs_2_.heads_ref), custom_call_target="tpu_custom_call" | custom-call | flops 24159191040 | bytes 9437184 | tf_op jit(solution)/shard_map/logits/pallas_call | solution.py:114
  38.1 1.2 %collective-permute-start.10 = (f32[1,6,64]{2,1,0:T(8,128)S(1)}, f32[1,6,64]{2,1,0:T(8,128)S(1)}, u32[]{:S(2)}, u32[]{:S(2)}) collective-permute-start(f32[1,6,64]{2,1,0:T(8,128)S(1)} %convolution_bitcast_fusion), channel_id=1, source_target_pairs={{0,2},{1,3},{4,0},{5,1},{8,4},{9,5},{12,8},{13,9},{14,12},{15,13},... | collective-permute-start | bytes 4616 | tf_op jit(solution)/shard_map/ppermute | solution.py:264
  40.1 1.6 %collective-permute-done.10 = f32[1,6,64]{2,1,0:T(8,128)S(1)} collective-permute-done((f32[1,6,64]{2,1,0:T(8,128)S(1)}, f32[1,6,64]{2,1,0:T(8,128)S(1)}, u32[]{:S(2)}, u32[]{:S(2)}) %collective-permute-start.10) | collective-permute-done | bytes 1568 | tf_op jit(solution)/shard_map/ppermute | solution.py:264
  41.7 3.5 %collective-permute-start.11 = (f32[2,6,64]{2,1,0:T(8,128)S(1)}, f32[2,6,64]{2,1,0:T(8,128)S(1)}, u32[]{:S(2)}, u32[]{:S(2)}) collective-permute-start(f32[2,6,64]{2,1,0:T(8,128)S(1)} %pad_maximum_fusion.3), channel_id=1, source_target_pairs={{0,12},{1,13},{4,14},{5,15},{8,10},{9,11},{12,6},{13,7},{14,2},{15... | collective-permute-start | bytes 9224 | tf_op jit(solution)/shard_map/ppermute | solution.py:267
  45.3 1.3 %collective-permute-start.13 = (f32[3,6,64]{2,1,0:T(8,128)S(1)}, f32[3,6,64]{2,1,0:T(8,128)S(1)}, u32[]{:S(2)}, u32[]{:S(2)}) collective-permute-start(f32[3,6,64]{2,1,0:T(8,128)S(1)} %pad_maximum_fusion.2), channel_id=1, source_target_pairs={{0,10},{1,11},{4,6},{5,7},{8,2},{9,3},{12,0},{13,1},{14,4},{15,5},... | collective-permute-start | bytes 13832 | tf_op jit(solution)/shard_map/ppermute | solution.py:264
  47.2 3.6 %collective-permute-done.13 = f32[3,6,64]{2,1,0:T(8,128)S(1)} collective-permute-done((f32[3,6,64]{2,1,0:T(8,128)S(1)}, f32[3,6,64]{2,1,0:T(8,128)S(1)}, u32[]{:S(2)}, u32[]{:S(2)}) %collective-permute-start.13) | collective-permute-done | bytes 4640 | tf_op jit(solution)/shard_map/ppermute | solution.py:264
  51.3 3.7 %copy-done.1 = bf16[256,18432]{1,0:T(8,128)(2,1)S(1)} copy-done((bf16[256,18432]{1,0:T(8,128)(2,1)S(1)}, bf16[256,18432]{1,0:T(8,128)(2,1)}, u32[]{:S(2)}) %copy-start.1) | copy-done | bytes 9437208
  55.0 1.8 %gradient_terms.1 = (f32[56,9216]{1,0:T(8,128)S(1)}, f32[56,9216]{1,0:T(8,128)S(1)}, bf16[8,9216]{1,0:T(8,128)(2,1)S(1)}, bf16[8,9216]{1,0:T(8,128)(2,1)S(1)}) custom-call(bf16[256,64]{1,0:T(8,128)(2,1)S(1)} %fusion.6.d_ref, bf16[256,18432]{1,0:T(8,128)(2,1)S(1)} %copy-done.1), custom_call_target="tpu_custom_call" | custom-call | flops 24159191040 | bytes 9437184 | tf_op jit(solution)/shard_map/gradient_terms/pallas_call | solution.py:180
  57.6 1.5 %collective-permute-start.16 = (bf16[8,9216]{1,0:T(8,128)(2,1)S(1)}, bf16[8,9216]{1,0:T(8,128)(2,1)S(1)}, u32[]{:S(2)}, u32[]{:S(2)}) collective-permute-start(bf16[8,9216]{1,0:T(8,128)(2,1)S(1)} %get-tuple-element.43), channel_id=1, source_target_pairs={{0,4},{1,5},{4,8},{5,9},{8,12},{9,13},{12,14},{13,15},{14,10},{15,... | collective-permute-start | bytes 442376 | tf_op jit(solution)/shard_map/ppermute | solution.py:289
  59.1 4.2 %collective-permute-done.23.refs_0_ = bf16[8,9216]{1,0:T(8,128)(2,1)S(1)} collective-permute-done((bf16[8,9216]{1,0:T(8,128)(2,1)S(1)}, bf16[8,9216]{1,0:T(8,128)(2,1)S(1)}, u32[]{:S(2)}, u32[]{:S(2)}) %collective-permute-start.23) | collective-permute-done | bytes 147488 | tf_op jit(solution)/shard_map/ppermute | solution.py:289
  63.3 1.3 %collective-permute-start.24 = (bf16[8,9216]{1,0:T(8,128)(2,1)S(1)}, bf16[8,9216]{1,0:T(8,128)(2,1)S(1)}, u32[]{:S(2)}, u32[]{:S(2)}) collective-permute-start(bf16[8,9216]{1,0:T(8,128)(2,1)S(1)} %get-tuple-element.62), channel_id=1, source_target_pairs={{0,4},{1,5},{4,8},{5,9},{8,12},{9,13},{12,14},{13,15},{14,10},{15,... | collective-permute-start | bytes 442376 | tf_op jit(solution)/shard_map/ppermute | solution.py:289
  65.5 1.3 %collective-permute-start.17 = (bf16[8,9216]{1,0:T(8,128)(2,1)S(1)}, bf16[8,9216]{1,0:T(8,128)(2,1)S(1)}, u32[]{:S(2)}, u32[]{:S(2)}) collective-permute-start(bf16[8,9216]{1,0:T(8,128)(2,1)S(1)} %get-tuple-element.54), channel_id=1, source_target_pairs={{0,4},{1,5},{4,8},{5,9},{8,12},{9,13},{12,14},{13,15},{14,10},{15,... | collective-permute-start | bytes 442376 | tf_op jit(solution)/shard_map/ppermute | solution.py:289
  67.6 2.6 %collective-permute-done.24.refs_0_ = bf16[8,9216]{1,0:T(8,128)(2,1)S(1)} collective-permute-done((bf16[8,9216]{1,0:T(8,128)(2,1)S(1)}, bf16[8,9216]{1,0:T(8,128)(2,1)S(1)}, u32[]{:S(2)}, u32[]{:S(2)}) %collective-permute-start.24) | collective-permute-done | bytes 147488 | tf_op jit(solution)/shard_map/ppermute | solution.py:289
  70.1 1.2 %collective-permute-done.25.refs_1_ = bf16[8,9216]{1,0:T(8,128)(2,1)S(1)} collective-permute-done((bf16[8,9216]{1,0:T(8,128)(2,1)S(1)}, bf16[8,9216]{1,0:T(8,128)(2,1)S(1)}, u32[]{:S(2)}, u32[]{:S(2)}) %collective-permute-start.25) | collective-permute-done | bytes 147488 | tf_op jit(solution)/shard_map/ppermute | solution.py:289
  71.6 1.9 %collective-permute-start.27 = (bf16[8,9216]{1,0:T(8,128)(2,1)S(1)}, bf16[8,9216]{1,0:T(8,128)(2,1)S(1)}, u32[]{:S(2)}, u32[]{:S(2)}) collective-permute-start(bf16[8,9216]{1,0:T(8,128)(2,1)S(1)} %get-tuple-element.65), channel_id=1, source_target_pairs={{0,2},{1,3},{4,0},{5,1},{8,4},{9,5},{12,8},{13,9},{14,12},{15,13},... | collective-permute-start | bytes 442376 | tf_op jit(solution)/shard_map/ppermute | solution.py:289
  74.8 1.9 %collective-permute-start.20 = (bf16[8,9216]{1,0:T(8,128)(2,1)S(1)}, bf16[8,9216]{1,0:T(8,128)(2,1)S(1)}, u32[]{:S(2)}, u32[]{:S(2)}) collective-permute-start(bf16[8,9216]{1,0:T(8,128)(2,1)S(1)} %get-tuple-element.57), channel_id=1, source_target_pairs={{0,2},{1,3},{4,0},{5,1},{8,4},{9,5},{12,8},{13,9},{14,12},{15,13},... | collective-permute-start | bytes 442376 | tf_op jit(solution)/shard_map/ppermute | solution.py:289
  78.4 1.4 %collective-permute-done.19.refs_0_ = bf16[8,9216]{1,0:T(8,128)(2,1)S(1)} collective-permute-done((bf16[8,9216]{1,0:T(8,128)(2,1)S(1)}, bf16[8,9216]{1,0:T(8,128)(2,1)S(1)}, u32[]{:S(2)}, u32[]{:S(2)}) %collective-permute-start.19) | collective-permute-done | bytes 147488 | tf_op jit(solution)/shard_map/ppermute | solution.py:289
  80.0 1.9 %collective-permute-start.21 = (bf16[8,9216]{1,0:T(8,128)(2,1)S(1)}, bf16[8,9216]{1,0:T(8,128)(2,1)S(1)}, u32[]{:S(2)}, u32[]{:S(2)}) collective-permute-start(bf16[8,9216]{1,0:T(8,128)(2,1)S(1)} %get-tuple-element.58), channel_id=1, source_target_pairs={{0,4},{1,5},{4,8},{5,9},{8,12},{9,13},{12,14},{13,15},{14,10},{15,... | collective-permute-start | bytes 442376 | tf_op jit(solution)/shard_map/ppermute | solution.py:289
  82.1 3.1 %convolution_convert_fusion = bf16[128,18432]{1,0:T(8,128)(2,1)} fusion(bf16[64,18432]{1,0:T(8,128)(2,1)S(1)} %collective-permute-done.15, bf16[64,18432]{1,0:T(8,128)(2,1)S(1)} %assemble.1, bf16[128,64]{1,0:T(8,128)(2,1)S(1)} %collective-permute-done.14, bf16[128,64]{1,0:T(8,128)(2,1)S(1)} %get-tuple-element.79), kind=kOutput, calls=%fused_computation | convolution fusion | flops 615841792 | bytes 9469952 | tf_op jit(solution)/shard_map/dot_general | solution.py:362
  85.8 1.1 %collective-permute-done.21 = bf16[8,9216]{1,0:T(8,128)(2,1)S(1)} collective-permute-done((bf16[8,9216]{1,0:T(8,128)(2,1)S(1)}, bf16[8,9216]{1,0:T(8,128)(2,1)S(1)}, u32[]{:S(2)}, u32[]{:S(2)}) %collective-permute-start.21) | collective-permute-done | bytes 147488 | tf_op jit(solution)/shard_map/ppermute | solution.py:289
  (89 shorter events, 17.5 us)
Async XLA Ops:
  0.6 14.3 %collective-permute-start.4 = (bf16[128,18432]{1,0:T(8,128)(2,1)}, bf16[128,18432]{1,0:T(8,128)(2,1)}, u32[]{:S(2)}, u32[]{:S(2)}) collective-permute-start(bf16[128,18432]{1,0:T(8,128)(2,1)} %own_ref.1), channel_id=1, source_target_pairs={{0,1},{1,0},{2,3},{3,2},{4,5},{5,4},{6,7},{7,6},{8,9},{9,8},{10,11... | collective-permute-start | bytes 14155784 | tf_op jit(solution)/shard_map/ppermute | solution.py:289
  1.1 10.5 %collective-permute-start.2 = (bf16[8,18432]{1,0:T(8,128)(2,1)}, bf16[8,18432]{1,0:T(8,128)(2,1)S(1)}, u32[]{:S(2)}, u32[]{:S(2)}) collective-permute-start(bf16[8,18432]{1,0:T(8,128)(2,1)} %refs_0_.2), channel_id=1, source_target_pairs={{0,2},{1,3},{4,0},{5,1},{8,4},{9,5},{12,8},{13,9},{14,12},{15,13},... | collective-permute-start | bytes 884744 | tf_op jit(solution)/shard_map/ppermute | solution.py:289
  3.7 9.6 %collective-permute-start = (bf16[8,18432]{1,0:T(8,128)(2,1)}, bf16[8,18432]{1,0:T(8,128)(2,1)S(1)}, u32[]{:S(2)}, u32[]{:S(2)}) collective-permute-start(bf16[8,18432]{1,0:T(8,128)(2,1)} %refs_0_.2), channel_id=1, source_target_pairs={{0,4},{1,5},{4,8},{5,9},{8,12},{9,13},{12,14},{13,15},{14,10},{15,... | collective-permute-start | bytes 884744 | tf_op jit(solution)/shard_map/ppermute | solution.py:289
  3.9 9.9 %collective-permute-start.9 = (bf16[128,128]{1,0:T(8,128)(2,1)}, bf16[128,128]{1,0:T(8,128)(2,1)S(1)}, u32[]{:S(2)}, u32[]{:S(2)}) collective-permute-start(bf16[128,128]{1,0:T(8,128)(2,1)} %param.8), channel_id=1, source_target_pairs={{0,1},{1,0},{2,3},{3,2},{4,5},{5,4},{6,7},{7,6},{8,9},{9,8},{10,11... | collective-permute-start | bytes 98312 | tf_op jit(solution)/shard_map/ppermute | solution.py:289
  11.6 8.8 %collective-permute-start.3 = (bf16[8,18432]{1,0:T(8,128)(2,1)S(1)}, bf16[8,18432]{1,0:T(8,128)(2,1)S(1)}, u32[]{:S(2)}, u32[]{:S(2)}) collective-permute-start(bf16[8,18432]{1,0:T(8,128)(2,1)S(1)} %collective-permute-done.2.refs_1_), channel_id=1, source_target_pairs={{0,2},{1,3},{4,0},{5,1},{8,4},{9,5},{12,8},{13,9},{14,12},{15,13},... | collective-permute-start | bytes 884744 | tf_op jit(solution)/shard_map/ppermute | solution.py:289
  13.3 8.3 %collective-permute-start.1 = (bf16[8,18432]{1,0:T(8,128)(2,1)S(1)}, bf16[8,18432]{1,0:T(8,128)(2,1)S(1)}, u32[]{:S(2)}, u32[]{:S(2)}) collective-permute-start(bf16[8,18432]{1,0:T(8,128)(2,1)S(1)} %collective-permute-done.refs_2_), channel_id=1, source_target_pairs={{0,4},{1,5},{4,8},{5,9},{8,12},{9,13},{12,14},{13,15},{14,10},{15,... | collective-permute-start | bytes 884744 | tf_op jit(solution)/shard_map/ppermute | solution.py:289
  17.2 6.3 %copy-start.3 = (bf16[8,18432]{1,0:T(8,128)(2,1)S(1)}, bf16[8,18432]{1,0:T(8,128)(2,1)}, u32[]{:S(2)}) copy-start(bf16[8,18432]{1,0:T(8,128)(2,1)} %refs_0_.2) | copy-start | bytes 884740
  19.9 15.1 %copy-start = (bf16[256,18432]{1,0:T(8,128)(2,1)}, bf16[256,18432]{1,0:T(8,128)(2,1)S(1)}, u32[]{:S(2)}) copy-start(bf16[256,18432]{1,0:T(8,128)(2,1)S(1)} %stack_heads.1.refs_5_.refs_2_.heads_ref) | copy-start | bytes 28311556
  21.6 7.4 %collective-permute-start.5 = (bf16[8,18432]{1,0:T(8,128)(2,1)S(1)}, bf16[8,18432]{1,0:T(8,128)(2,1)S(1)}, u32[]{:S(2)}, u32[]{:S(2)}) collective-permute-start(bf16[8,18432]{1,0:T(8,128)(2,1)S(1)} %collective-permute-done.1.refs_4_), channel_id=1, source_target_pairs={{0,4},{1,5},{4,8},{5,9},{8,12},{9,13},{12,14},{13,15},{14,10},{15,... | collective-permute-start | bytes 884744 | tf_op jit(solution)/shard_map/ppermute | solution.py:289
  22.1 7.7 %collective-permute-start.6 = (bf16[8,18432]{1,0:T(8,128)(2,1)S(1)}, bf16[8,18432]{1,0:T(8,128)(2,1)S(1)}, u32[]{:S(2)}, u32[]{:S(2)}) collective-permute-start(bf16[8,18432]{1,0:T(8,128)(2,1)S(1)} %collective-permute-done.3.refs_3_), channel_id=1, source_target_pairs={{0,2},{1,3},{4,0},{5,1},{8,4},{9,5},{12,8},{13,9},{14,12},{15,13},... | collective-permute-start | bytes 884744 | tf_op jit(solution)/shard_map/ppermute | solution.py:289
  28.9 5.2 %collective-permute-start.7 = (bf16[8,9216]{1,0:T(8,128)(2,1)S(1)}, bf16[8,9216]{1,0:T(8,128)(2,1)S(1)}, u32[]{:S(2)}, u32[]{:S(2)}) collective-permute-start(bf16[8,9216]{1,0:T(8,128)(2,1)S(1)} %slice.43), channel_id=1, source_target_pairs={{0,4},{1,5},{4,8},{5,9},{8,12},{9,13},{12,14},{13,15},{14,10},{15,... | collective-permute-start | bytes 442376 | tf_op jit(solution)/shard_map/ppermute | solution.py:289
  29.8 5.2 %collective-permute-start.8 = (bf16[8,9216]{1,0:T(8,128)(2,1)S(1)}, bf16[8,9216]{1,0:T(8,128)(2,1)S(1)}, u32[]{:S(2)}, u32[]{:S(2)}) collective-permute-start(bf16[8,9216]{1,0:T(8,128)(2,1)S(1)} %slice.56), channel_id=1, source_target_pairs={{0,2},{1,3},{4,0},{5,1},{8,4},{9,5},{12,8},{13,9},{14,12},{15,13},... | collective-permute-start | bytes 442376 | tf_op jit(solution)/shard_map/ppermute | solution.py:289
  38.1 3.6 %collective-permute-start.10 = (f32[1,6,64]{2,1,0:T(8,128)S(1)}, f32[1,6,64]{2,1,0:T(8,128)S(1)}, u32[]{:S(2)}, u32[]{:S(2)}) collective-permute-start(f32[1,6,64]{2,1,0:T(8,128)S(1)} %convolution_bitcast_fusion), channel_id=1, source_target_pairs={{0,2},{1,3},{4,0},{5,1},{8,4},{9,5},{12,8},{13,9},{14,12},{15,13},... | collective-permute-start | bytes 4616 | tf_op jit(solution)/shard_map/ppermute | solution.py:264
  39.3 5.9 %collective-permute-start.12 = (f32[1,6,64]{2,1,0:T(8,128)S(1)}, f32[1,6,64]{2,1,0:T(8,128)S(1)}, u32[]{:S(2)}, u32[]{:S(2)}) collective-permute-start(f32[1,6,64]{2,1,0:T(8,128)S(1)} %convolution_bitcast_fusion), channel_id=1, source_target_pairs={{0,4},{1,5},{4,8},{5,9},{8,12},{9,13},{12,14},{13,15},{14,10},{15,... | collective-permute-start | bytes 4616 | tf_op jit(solution)/shard_map/ppermute | solution.py:267
  41.7 5.4 %collective-permute-start.11 = (f32[2,6,64]{2,1,0:T(8,128)S(1)}, f32[2,6,64]{2,1,0:T(8,128)S(1)}, u32[]{:S(2)}, u32[]{:S(2)}) collective-permute-start(f32[2,6,64]{2,1,0:T(8,128)S(1)} %pad_maximum_fusion.3), channel_id=1, source_target_pairs={{0,12},{1,13},{4,14},{5,15},{8,10},{9,11},{12,6},{13,7},{14,2},{15... | collective-permute-start | bytes 9224 | tf_op jit(solution)/shard_map/ppermute | solution.py:267
  45.3 5.5 %collective-permute-start.13 = (f32[3,6,64]{2,1,0:T(8,128)S(1)}, f32[3,6,64]{2,1,0:T(8,128)S(1)}, u32[]{:S(2)}, u32[]{:S(2)}) collective-permute-start(f32[3,6,64]{2,1,0:T(8,128)S(1)} %pad_maximum_fusion.2), channel_id=1, source_target_pairs={{0,10},{1,11},{4,6},{5,7},{8,2},{9,3},{12,0},{13,1},{14,4},{15,5},... | collective-permute-start | bytes 13832 | tf_op jit(solution)/shard_map/ppermute | solution.py:264
  56.9 25.1 %collective-permute-start.15 = (bf16[64,18432]{1,0:T(8,128)(2,1)S(1)}, bf16[64,18432]{1,0:T(8,128)(2,1)S(1)}, u32[]{:S(2)}, u32[]{:S(2)}) collective-permute-start(bf16[64,18432]{1,0:T(8,128)(2,1)S(1)} %assemble.1), channel_id=1, source_target_pairs={{0,1},{1,0},{2,3},{3,2},{4,5},{5,4},{6,7},{7,6},{8,9},{9,8},{10,11... | collective-permute-start | bytes 7077896 | tf_op jit(solution)/shard_map/ppermute | solution.py:289
  57.0 6.2 %collective-permute-start.23 = (bf16[8,9216]{1,0:T(8,128)(2,1)S(1)}, bf16[8,9216]{1,0:T(8,128)(2,1)S(1)}, u32[]{:S(2)}, u32[]{:S(2)}) collective-permute-start(bf16[8,9216]{1,0:T(8,128)(2,1)S(1)} %get-tuple-element.61), channel_id=1, source_target_pairs={{0,2},{1,3},{4,0},{5,1},{8,4},{9,5},{12,8},{13,9},{14,12},{15,13},... | collective-permute-start | bytes 442376 | tf_op jit(solution)/shard_map/ppermute | solution.py:289
  57.6 7.8 %collective-permute-start.16 = (bf16[8,9216]{1,0:T(8,128)(2,1)S(1)}, bf16[8,9216]{1,0:T(8,128)(2,1)S(1)}, u32[]{:S(2)}, u32[]{:S(2)}) collective-permute-start(bf16[8,9216]{1,0:T(8,128)(2,1)S(1)} %get-tuple-element.43), channel_id=1, source_target_pairs={{0,4},{1,5},{4,8},{5,9},{8,12},{9,13},{12,14},{13,15},{14,10},{15,... | collective-permute-start | bytes 442376 | tf_op jit(solution)/shard_map/ppermute | solution.py:289
  63.3 6.8 %collective-permute-start.24 = (bf16[8,9216]{1,0:T(8,128)(2,1)S(1)}, bf16[8,9216]{1,0:T(8,128)(2,1)S(1)}, u32[]{:S(2)}, u32[]{:S(2)}) collective-permute-start(bf16[8,9216]{1,0:T(8,128)(2,1)S(1)} %get-tuple-element.62), channel_id=1, source_target_pairs={{0,4},{1,5},{4,8},{5,9},{8,12},{9,13},{12,14},{13,15},{14,10},{15,... | collective-permute-start | bytes 442376 | tf_op jit(solution)/shard_map/ppermute | solution.py:289
  64.7 6.7 %collective-permute-start.25 = (bf16[8,9216]{1,0:T(8,128)(2,1)S(1)}, bf16[8,9216]{1,0:T(8,128)(2,1)S(1)}, u32[]{:S(2)}, u32[]{:S(2)}) collective-permute-start(bf16[8,9216]{1,0:T(8,128)(2,1)S(1)} %get-tuple-element.63), channel_id=1, source_target_pairs={{0,2},{1,3},{4,0},{5,1},{8,4},{9,5},{12,8},{13,9},{14,12},{15,13},... | collective-permute-start | bytes 442376 | tf_op jit(solution)/shard_map/ppermute | solution.py:289
  65.5 8.1 %collective-permute-start.17 = (bf16[8,9216]{1,0:T(8,128)(2,1)S(1)}, bf16[8,9216]{1,0:T(8,128)(2,1)S(1)}, u32[]{:S(2)}, u32[]{:S(2)}) collective-permute-start(bf16[8,9216]{1,0:T(8,128)(2,1)S(1)} %get-tuple-element.54), channel_id=1, source_target_pairs={{0,4},{1,5},{4,8},{5,9},{8,12},{9,13},{12,14},{13,15},{14,10},{15,... | collective-permute-start | bytes 442376 | tf_op jit(solution)/shard_map/ppermute | solution.py:289
  66.8 7.7 %collective-permute-start.18 = (bf16[8,9216]{1,0:T(8,128)(2,1)S(1)}, bf16[8,9216]{1,0:T(8,128)(2,1)S(1)}, u32[]{:S(2)}, u32[]{:S(2)}) collective-permute-start(bf16[8,9216]{1,0:T(8,128)(2,1)S(1)} %get-tuple-element.55), channel_id=1, source_target_pairs={{0,2},{1,3},{4,0},{5,1},{8,4},{9,5},{12,8},{13,9},{14,12},{15,13},... | collective-permute-start | bytes 442376 | tf_op jit(solution)/shard_map/ppermute | solution.py:289
  71.5 5.8 %collective-permute-start.26 = (bf16[8,9216]{1,0:T(8,128)(2,1)S(1)}, bf16[8,9216]{1,0:T(8,128)(2,1)S(1)}, u32[]{:S(2)}, u32[]{:S(2)}) collective-permute-start(bf16[8,9216]{1,0:T(8,128)(2,1)S(1)} %get-tuple-element.64), channel_id=1, source_target_pairs={{0,4},{1,5},{4,8},{5,9},{8,12},{9,13},{12,14},{13,15},{14,10},{15,... | collective-permute-start | bytes 442376 | tf_op jit(solution)/shard_map/ppermute | solution.py:289
  71.6 6.1 %collective-permute-start.27 = (bf16[8,9216]{1,0:T(8,128)(2,1)S(1)}, bf16[8,9216]{1,0:T(8,128)(2,1)S(1)}, u32[]{:S(2)}, u32[]{:S(2)}) collective-permute-start(bf16[8,9216]{1,0:T(8,128)(2,1)S(1)} %get-tuple-element.65), channel_id=1, source_target_pairs={{0,2},{1,3},{4,0},{5,1},{8,4},{9,5},{12,8},{13,9},{14,12},{15,13},... | collective-permute-start | bytes 442376 | tf_op jit(solution)/shard_map/ppermute | solution.py:289
  74.6 5.2 %collective-permute-start.19 = (bf16[8,9216]{1,0:T(8,128)(2,1)S(1)}, bf16[8,9216]{1,0:T(8,128)(2,1)S(1)}, u32[]{:S(2)}, u32[]{:S(2)}) collective-permute-start(bf16[8,9216]{1,0:T(8,128)(2,1)S(1)} %get-tuple-element.56), channel_id=1, source_target_pairs={{0,4},{1,5},{4,8},{5,9},{8,12},{9,13},{12,14},{13,15},{14,10},{15,... | collective-permute-start | bytes 442376 | tf_op jit(solution)/shard_map/ppermute | solution.py:289
  74.8 5.1 %collective-permute-start.20 = (bf16[8,9216]{1,0:T(8,128)(2,1)S(1)}, bf16[8,9216]{1,0:T(8,128)(2,1)S(1)}, u32[]{:S(2)}, u32[]{:S(2)}) collective-permute-start(bf16[8,9216]{1,0:T(8,128)(2,1)S(1)} %get-tuple-element.57), channel_id=1, source_target_pairs={{0,2},{1,3},{4,0},{5,1},{8,4},{9,5},{12,8},{13,9},{14,12},{15,13},... | collective-permute-start | bytes 442376 | tf_op jit(solution)/shard_map/ppermute | solution.py:289
  77.3 4.6 %collective-permute-start.14 = (bf16[128,64]{1,0:T(8,128)(2,1)S(1)}, bf16[128,64]{1,0:T(8,128)(2,1)S(1)}, u32[]{:S(2)}, u32[]{:S(2)}) collective-permute-start(bf16[128,64]{1,0:T(8,128)(2,1)S(1)} %get-tuple-element.80), channel_id=1, source_target_pairs={{0,1},{1,0},{2,3},{3,2},{4,5},{5,4},{6,7},{7,6},{8,9},{9,8},{10,11... | collective-permute-start | bytes 49160 | tf_op jit(solution)/shard_map/ppermute | solution.py:289
  77.8 7.4 %collective-permute-start.28 = (bf16[8,9216]{1,0:T(8,128)(2,1)S(1)}, bf16[8,9216]{1,0:T(8,128)(2,1)S(1)}, u32[]{:S(2)}, u32[]{:S(2)}) collective-permute-start(bf16[8,9216]{1,0:T(8,128)(2,1)S(1)} %get-tuple-element.66), channel_id=1, source_target_pairs={{0,4},{1,5},{4,8},{5,9},{8,12},{9,13},{12,14},{13,15},{14,10},{15,... | collective-permute-start | bytes 442376 | tf_op jit(solution)/shard_map/ppermute | solution.py:289
  79.8 5.9 %collective-permute-start.29 = (bf16[8,9216]{1,0:T(8,128)(2,1)S(1)}, bf16[8,9216]{1,0:T(8,128)(2,1)S(1)}, u32[]{:S(2)}, u32[]{:S(2)}) collective-permute-start(bf16[8,9216]{1,0:T(8,128)(2,1)S(1)} %get-tuple-element.67), channel_id=1, source_target_pairs={{0,2},{1,3},{4,0},{5,1},{8,4},{9,5},{12,8},{13,9},{14,12},{15,13},... | collective-permute-start | bytes 442376 | tf_op jit(solution)/shard_map/ppermute | solution.py:289
  80.0 6.9 %collective-permute-start.21 = (bf16[8,9216]{1,0:T(8,128)(2,1)S(1)}, bf16[8,9216]{1,0:T(8,128)(2,1)S(1)}, u32[]{:S(2)}, u32[]{:S(2)}) collective-permute-start(bf16[8,9216]{1,0:T(8,128)(2,1)S(1)} %get-tuple-element.58), channel_id=1, source_target_pairs={{0,4},{1,5},{4,8},{5,9},{8,12},{9,13},{12,14},{13,15},{14,10},{15,... | collective-permute-start | bytes 442376 | tf_op jit(solution)/shard_map/ppermute | solution.py:289
  81.9 5.4 %collective-permute-start.22 = (bf16[8,9216]{1,0:T(8,128)(2,1)S(1)}, bf16[8,9216]{1,0:T(8,128)(2,1)S(1)}, u32[]{:S(2)}, u32[]{:S(2)}) collective-permute-start(bf16[8,9216]{1,0:T(8,128)(2,1)S(1)} %get-tuple-element.59), channel_id=1, source_target_pairs={{0,2},{1,3},{4,0},{5,1},{8,4},{9,5},{12,8},{13,9},{14,12},{15,13},... | collective-permute-start | bytes 442376 | tf_op jit(solution)/shard_map/ppermute | solution.py:289
  (2 other events, 6.0 us)
